TPU v7x, 32 devices: a whole 2x2x4 slice. The times are simulated.
32 devices in a mesh: tok: 8 (over y, x, core), tp: 4 (over z).
Axes of the slice: x: 2, y: 2, z: 4, core: 2. Of those that a mesh axis runs over, the one named last changes fastest.
Arguments:
- tokens: bfloat16 [8192, 1024], P('tok', 'tp'), may hold values from -6 to 6
- mix_weights: bfloat16 [10, 2, 2, 128, 128], replicated, may hold values from -0.375 to 0.375
- proj_weight: bfloat16 [1024, 2048], P('tp'), may hold values from -0.1875 to 0.1875
- pool_map: int32 [8192], P('tok'), may hold values from 0 to 1023, as said below
- out_cot: bfloat16 [1024, 2048], P('tok', 'tp'), may hold values from -6 to 6
Outputs:
- projected: bfloat16 [1024, 2048], P('tok', 'tp')
- token_grad: bfloat16 [8192, 1024], P('tok', 'tp')
- proj_grad: float32 [2048, 1024], P('tok', 'tp')
Inputs may be any that keep to these rules, and one draw needn't show every extreme that they name: `pool_map`: token t names one of the 128 pooled tokens of its own block of 1024 tokens, numbers (t // 1024) * 128 onward; every pooled token is named by at least one token.
All inputs are finite; a program needn't handle non-finite values.
Results may differ from a plain program's by a relative error of at most 0.017.
Values may be sent and summed in bfloat16 or wider, within the bound.
No kernel may reach another device: no remote copies, remote signals or barrier semaphores. Data moves between devices by JAX's collectives and lax.ppermute only.
A program may use at most 64 MiB of HBM per device.

v0:
```python
import math

import jax
import jax.numpy as jnp
from jax import lax
from jax.sharding import PartitionSpec as P


def contract(matrix, operand, backward):
    pattern = "ji,...j->...i" if backward else "ij,...j->...i"
    return jnp.einsum(pattern, matrix, operand, preferred_element_type=jnp.float32)


def local_section(field_now, section_mats, bit_index, backward, block_axis):
    full_shape = field_now.shape
    nblocks = full_shape[block_axis]
    split_shape = (
        full_shape[:block_axis]
        + (nblocks >> bit_index + 1, 2, 1 << bit_index)
        + full_shape[block_axis + 1 :]
    )
    paired = field_now.reshape(split_shape)
    lower_half = lax.index_in_dim(paired, 0, block_axis + 1, keepdims=False)
    upper_half = lax.index_in_dim(paired, 1, block_axis + 1, keepdims=False)
    if backward:
        new_lower = contract(section_mats[0, 0], lower_half, True) + contract(
            section_mats[1, 0], upper_half, True
        )
        new_upper = contract(section_mats[0, 1], lower_half, True) + contract(
            section_mats[1, 1], upper_half, True
        )
    else:
        new_lower = contract(section_mats[0, 0], lower_half, False) + contract(
            section_mats[0, 1], upper_half, False
        )
        new_upper = contract(section_mats[1, 0], lower_half, False) + contract(
            section_mats[1, 1], upper_half, False
        )
    joined = jnp.stack(
        [new_lower.astype(jnp.bfloat16), new_upper.astype(jnp.bfloat16)], axis=block_axis + 1
    )
    return joined.reshape(full_shape)


def mix_tokens(source, mix_weights, section_bits, backward):
    block_rows = mix_weights.shape[-1]
    section_order = list(range(len(section_bits)))
    if backward:
        section_order = section_order[::-1]
    columns = lax.all_to_all(source.T, "tok", split_axis=0, concat_axis=1, tiled=True)
    feat_rows, all_tokens = columns.shape
    field_now = columns.reshape(feat_rows, all_tokens // block_rows, block_rows)
    for section_id in section_order:
        field_now = local_section(
            field_now, mix_weights[section_id], section_bits[section_id], backward, 1
        )
    back_rows = lax.all_to_all(
        field_now.reshape(feat_rows, all_tokens), "tok", split_axis=1, concat_axis=0, tiled=True
    )
    return back_rows.T


def shards(tokens, mix_weights, proj_weight, pool_map, out_cot):
    tok_rows = tokens.shape[0]
    block_rows = mix_weights.shape[-1]
    section_count = mix_weights.shape[0]
    local_blocks = tok_rows // block_rows
    local_bits = local_blocks.bit_length() - 1
    tok_devices = lax.axis_size("tok")
    all_bits = local_bits + tok_devices.bit_length() - 1
    section_bits = [section_id % all_bits for section_id in range(section_count)]
    mixed = mix_tokens(tokens, mix_weights, section_bits, False)
    pool_rows = out_cot.shape[0]
    local_map = pool_map - lax.axis_index("tok") * pool_rows
    membership = (local_map[None, :] == jnp.arange(pool_rows, dtype=jnp.int32)[:, None]).astype(
        jnp.bfloat16
    )
    counts = jnp.sum(membership.astype(jnp.float32), axis=1)
    group_sums = jnp.dot(membership, mixed, preferred_element_type=jnp.float32)
    pooled = (group_sums / counts[:, None]).astype(jnp.bfloat16)
    proj_share = lax.psum_scatter(
        lax.dot_general(
            proj_weight, pooled, (((0,), (1,)), ((), ())), preferred_element_type=jnp.float32
        ).astype(jnp.bfloat16),
        "tp",
        scatter_dimension=0,
        tiled=True,
    ).astype(jnp.float32)
    projected = proj_share.T.astype(jnp.bfloat16)
    cot_full = lax.all_gather(out_cot, "tp", axis=1, tiled=True)
    d_pooled = lax.dot_general(
        cot_full, proj_weight, (((1,), (1,)), ((), ())), preferred_element_type=jnp.float32
    )
    back_rows = jnp.take(d_pooled / counts[:, None], local_map, axis=0).astype(jnp.bfloat16)
    token_grad = mix_tokens(back_rows, mix_weights, section_bits, True)
    grad_share = lax.psum_scatter(
        lax.dot_general(
            cot_full, pooled, (((0,), (0,)), ((), ())), preferred_element_type=jnp.float32
        ),
        "tok",
        scatter_dimension=0,
        tiled=True,
    )
    grad_scale = 1.0 / math.sqrt(pool_rows * tok_devices)
    proj_grad = grad_share * grad_scale
    return (projected, token_grad, proj_grad)


def solution(mesh):
    in_specs = (P("tok", "tp"), P(), P("tp", None), P("tok"), P("tok", "tp"))
    out_specs = (P("tok", "tp"), P("tok", "tp"), P("tok", "tp"))
    return jax.shard_map(shards, mesh=mesh, in_specs=in_specs, out_specs=out_specs, check_vma=False)
```

profile of v0, /device:TPU:0, one launch (start us, length us, event | category | flops | bytes accessed | tf_op | source)
XLA Modules:
  0.0 158.5 jit_solution(14450032316523404437)
XLA Ops:
  7.2 2.1 %copy.145 = bf16[1024,256]{0,1:T(8,128)(2,1)} copy(bf16[1024,256]{1,0:T(8,128)(2,1)} %param.5) | data formatting | bytes 1048576 | tf_op args[0]
  9.3 5.2 %all-to-all-start = ((bf16[8,32,1024]{2,1,0:T(8,128)(2,1)}), bf16[8,32,1024]{2,1,0:T(8,128)(2,1)S(1)}, u32[]{:S(2)}, u32[]{:S(2)}) async-start(bf16[8,32,1024]{2,1,0:T(8,128)(2,1)} %bitcast.1), calls=%async_computation | async-start | bytes 1048576 | tf_op jit(solution)/shard_map/all_to_all | solution.py:50
  14.7 16.5 %all_gather.3 = bf16[128,2048]{1,0:T(8,128)(2,1)S(1)} all-gather(bf16[128,512]{1,0:T(8,128)(2,1)S(1)} %copy-done.18), channel_id=1, replica_groups=mesh['tok'=8,'tp'=4] {'tp'}, dimensions={1}, use_global_device_ids=true | all-gather | bytes 655360 | tf_op jit(solution)/shard_map/all_gather | solution.py:90
  31.2 0.5 convolution_divide_fusion.1
  31.7 3.9 %gather_fusion = bf16[1024,256]{1,0:T(8,128)(2,1)S(1)} fusion(bf16[128,256]{1,0:T(8,128)(2,1)S(1)} %convolution_divide_fusion.1, s32[1024]{0:T(1024)S(1)} %fusion.120), kind=kCustom, calls=%fused_computation | custom fusion | bytes 1052672 | tf_op jit(solution)/shard_map/jit(_take)/gather | solution.py:94
  35.9 1.0 copy.176
  36.9 2.3 %slice_bitcast_fusion.30 = (bf16[2,2,128,128]{3,2,1,0:T(8,128)(2,1)}, bf16[2,2,128,128]{3,2,1,0:T(8,128)(2,1)}, bf16[2,2,128,128]{3,2,1,0:T(8,128)(2,1)}, bf16[2...) fusion(bf16[10,2,2,128,128]{4,3,2,1,0:T(8,128)(2,1)} %param.6), kind=kLoop, calls=%fused_computation.231 | loop fusion | bytes 2621440 | tf_op jit(solution)/shard_map/squeeze | solution.py:55
  39.2 3.8 %all-to-all-start.2 = ((bf16[8,32,1024]{2,1,0:T(8,128)(2,1)}), bf16[8,32,1024]{2,1,0:T(8,128)(2,1)S(1)}, u32[]{:S(2)}, u32[]{:S(2)}) async-start(bf16[8,32,1024]{2,1,0:T(8,128)(2,1)} %bitcast.173), calls=%async_computation.3 | async-start | bytes 1048576 | tf_op jit(solution)/shard_map/all_to_all | solution.py:50
  43.0 0.3 copy.146
  43.3 0.4 reshape_reshape.56
  43.7 1.2 fusion.134
  47.7 0.3 fusion.71
  48.0 0.3 fusion.72
  48.6 0.3 copy-done.8
  51.4 0.3 copy-done.12
  52.9 0.3 copy-done.13
  55.7 0.3 copy-done.16
  56.3 0.3 fusion.87
  56.6 0.3 fusion.61
  56.9 0.3 fusion.62
  57.4 0.3 copy-done.11
  57.8 1.0 fusion.88
  60.4 0.3 copy-done.17
  62.1 0.3 copy-done.15
  63.0 0.5 fusion.53
  66.3 1.0 fusion.100
  67.3 1.0 fusion.101
  69.0 1.0 reshape.234
  70.0 4.2 %all-to-all-start.1 = ((bf16[32,8,1024]{2,0,1:T(8,128)(2,1)}), bf16[32,8,1024]{2,0,1:T(8,128)(2,1)S(1)}, u32[]{:S(2)}, u32[]{:S(2)}) async-start(bf16[32,8,1024]{2,0,1:T(8,128)(2,1)} %reshape.234), calls=%async_computation.1 | async-start | bytes 1048576 | tf_op jit(solution)/shard_map/all_to_all | solution.py:57
  74.2 1.0 fusion.49
  75.3 1.0 fusion.50
  77.5 6.4 %all-to-all-done.1 = bf16[32,8,1024]{2,0,1:T(8,128)(2,1)S(1)} async-done(((bf16[32,8,1024]{2,0,1:T(8,128)(2,1)}), bf16[32,8,1024]{2,0,1:T(8,128)(2,1)S(1)}, u32[]{:S(2)}, u32[]{:S(2)}) %all-to-all-start.1) | async-done | bytes 524320 | tf_op jit(solution)/shard_map/all_to_all | solution.py:57
  83.9 0.3 fusion.75
  84.2 1.8 %convolution_bitcast_fusion = f32[2048,256]{0,1:T(8,128)} fusion(bf16[128,256]{1,0:T(8,128)(2,1)S(1)} %fusion.75, bf16[128,2048]{1,0:T(8,128)(2,1)S(1)} %all_gather.3), kind=kOutput, calls=%fused_computation.1 | convolution fusion | flops 134217728 | bytes 2686976 | tf_op jit(solution)/shard_map/dot_general | solution.py:97
  86.2 0.8 copy-done.7
  88.4 0.3 copy-done.5
  88.9 0.3 fusion.43
  89.5 0.3 fusion.44
  90.5 1.1 fusion
  92.2 0.5 copy.206
  92.7 0.4 all_to_all.62
  93.1 0.3 copy.207
  93.4 12.2 %all_to_all.70 = bf16[32,8,1024]{2,0,1:T(8,128)(2,1)S(1)} all-to-all(bf16[32,8,1024]{2,0,1:T(8,128)(2,1)S(1)} %copy.207), channel_id=1, replica_groups=mesh['tok'=8,'tp'=4] {'tok'}, dimensions={1} | all-to-all | bytes 1048576 | tf_op jit(solution)/shard_map/all_to_all | solution.py:57
  105.6 1.0 copy.208
  106.6 20.5 %reduce-scatter.5.cloned.1.call-done = f32[256,256]{0,1:T(8,128)} async-done(((f32[2048,256]{0,1:T(8,128)}), f32[256,256]{0,1:T(8,128)}) %reduce-scatter.5.cloned.1.call-update) | async-done | bytes 262160 | tf_op jit(solution)/shard_map/reduce_scatter | solution.py:96
  127.1 1.0 broadcast_multiply_fusion
  128.0 0.8 copy.209
  128.9 22.8 %reduce-scatter.3.cloned.1.call-done = bf16[512,128]{0,1:T(8,128)(2,1)} async-done(((bf16[2048,128]{0,1:T(8,128)(2,1)}), bf16[512,128]{0,1:T(8,128)(2,1)}) %reduce-scatter.3.cloned.1.call-update) | async-done | bytes 131088 | tf_op jit(solution)/shard_map/reduce_scatter | solution.py:81
  (160 shorter events, 21.1 us)
Async XLA Ops:
  7.2 24.1 %copy-start = (bf16[256,2048]{1,0:T(8,128)(2,1)S(1)}, bf16[256,2048]{1,0:T(8,128)(2,1)}, u32[]{:S(2)}) copy-start(bf16[256,2048]{1,0:T(8,128)(2,1)} %param.7) | copy-start | bytes 3145732
  7.2 7.3 %copy-start.19 = (s32[1024]{0:T(1024)S(1)}, s32[1024]{0:T(1024)}, u32[]{:S(2)}) copy-start(s32[1024]{0:T(1024)} %param.8) | copy-start | bytes 12292
  7.2 7.5 %copy-start.18 = (bf16[128,512]{1,0:T(8,128)(2,1)S(1)}, bf16[128,512]{1,0:T(8,128)(2,1)}, u32[]{:S(2)}) copy-start(bf16[128,512]{1,0:T(8,128)(2,1)} %param.9) | copy-start | bytes 393220
  9.3 29.9 %all-to-all-start = ((bf16[8,32,1024]{2,1,0:T(8,128)(2,1)}), bf16[8,32,1024]{2,1,0:T(8,128)(2,1)S(1)}, u32[]{:S(2)}, u32[]{:S(2)}) async-start(bf16[8,32,1024]{2,1,0:T(8,128)(2,1)} %bitcast.1), calls=%async_computation | async-start | bytes 1048576 | tf_op jit(solution)/shard_map/all_to_all | solution.py:50
  39.2 7.4 %copy-start.4 = (bf16[2,2,128,128]{3,2,1,0:T(8,128)(2,1)}, bf16[2,2,128,128]{3,2,1,0:T(8,128)(2,1)S(1)}, u32[]{:S(2)}) copy-start(bf16[2,2,128,128]{3,2,1,0:T(8,128)(2,1)S(1)} %get-tuple-element.24) | copy-start | bytes 393220
  39.2 8.8 %copy-start.6 = (bf16[2,2,128,128]{3,2,1,0:T(8,128)(2,1)}, bf16[2,2,128,128]{3,2,1,0:T(8,128)(2,1)S(1)}, u32[]{:S(2)}) copy-start(bf16[2,2,128,128]{3,2,1,0:T(8,128)(2,1)S(1)} %get-tuple-element.23) | copy-start | bytes 393220
  39.2 19.8 %all-to-all-start.2 = ((bf16[8,32,1024]{2,1,0:T(8,128)(2,1)}), bf16[8,32,1024]{2,1,0:T(8,128)(2,1)S(1)}, u32[]{:S(2)}, u32[]{:S(2)}) async-start(bf16[8,32,1024]{2,1,0:T(8,128)(2,1)} %bitcast.173), calls=%async_computation.3 | async-start | bytes 1048576 | tf_op jit(solution)/shard_map/all_to_all | solution.py:50
  48.0 0.9 copy-start.8
  49.4 0.9 copy-start.10
  50.8 0.9 copy-start.12
  52.4 0.9 copy-start.13
  53.5 0.9 copy-start.14
  55.1 0.9 copy-start.16
  56.8 0.9 copy-start.11
  59.8 0.9 copy-start.17
  61.5 0.9 copy-start.15
  66.0 2.3 %copy-start.1 = (f32[32,4,8,128]{3,2,1,0:T(8,128)S(1)}, f32[32,4,8,128]{3,2,1,0:T(8,128)}, u32[]{:S(2)}) copy-start(f32[32,4,8,128]{3,2,1,0:T(8,128)} %fusion.88) | copy-start | bytes 1572868
  68.8 5.4 %copy-start.3 = (f32[32,2,16,128]{3,2,1,0:T(8,128)S(1)}, f32[32,2,16,128]{3,2,1,0:T(8,128)}, u32[]{:S(2)}) copy-start(f32[32,2,16,128]{3,2,1,0:T(8,128)} %fusion.100) | copy-start | bytes 1572868
  68.8 6.4 %copy-start.2 = (f32[32,2,16,128]{3,2,1,0:T(8,128)S(1)}, f32[32,2,16,128]{3,2,1,0:T(8,128)}, u32[]{:S(2)}) copy-start(f32[32,2,16,128]{3,2,1,0:T(8,128)} %fusion.101) | copy-start | bytes 1572868
  70.0 13.9 %all-to-all-start.1 = ((bf16[32,8,1024]{2,0,1:T(8,128)(2,1)}), bf16[32,8,1024]{2,0,1:T(8,128)(2,1)S(1)}, u32[]{:S(2)}, u32[]{:S(2)}) async-start(bf16[32,8,1024]{2,0,1:T(8,128)(2,1)} %reshape.234), calls=%async_computation.1 | async-start | bytes 1048576 | tf_op jit(solution)/shard_map/all_to_all | solution.py:57
  74.2 52.9 %reduce-scatter.5.cloned.1.call-start = ((), (), s32[]{:S(2)}) async-start(), calls=%async_computation.7 | async-start | bytes 2359296 | tf_op jit(solution)/shard_map/reduce_scatter | solution.py:96
  74.2 2.1 %copy-start.9 = (bf16[2,2,128,128]{3,2,1,0:T(8,128)(2,1)S(1)}, bf16[2,2,128,128]{3,2,1,0:T(8,128)(2,1)}, u32[]{:S(2)}) copy-start(bf16[2,2,128,128]{3,2,1,0:T(8,128)(2,1)} %get-tuple-element.22) | copy-start | bytes 393220
  86.1 0.9 copy-start.7
  86.1 65.6 %reduce-scatter.3.cloned.1.call-start = ((), (), s32[]{:S(2)}) async-start(), calls=%async_computation.6 | async-start | bytes 655360 | tf_op jit(solution)/shard_map/reduce_scatter | solution.py:81
  87.8 0.9 copy-start.5
Sparse Core Ops, SparseCore 0:
  86.2 40.8 reduce-scatter.4
  130.0 21.6 reduce-scatter.2
where the time goes:
time: 159 us
  waiting for transfers between devices  49.7 us (31%)
  blocking collectives  28.7 us (18%)
  matrix products  26.9 us (17%)
  local copies, waits for them, and re-layouts  22.5 us (14%)
  between operations  15.1 us (9%)
  starting transfers between devices  13.3 us (8%)
  other arithmetic  2.25 us (1%)
    dot_general x80, matrix products, contract(): jnp.einsum(pattern, matrix, operand, preferred_element_type=jnp.float32)  23.2 us
    reduce_scatter x1, waiting for transfers between devices, shards(): lax.psum_scatter(lax.dot_general(proj_weight, pooled, (((0,), (1,)), ((),...  22.8 us
    reduce_scatter x1, waiting for transfers between devices, shards(): lax.psum_scatter(lax.dot_general(cot_full, pooled, (((0,), (0,)), ((), ()...  20.5 us
    all_gather x1, blocking collectives, shards(): cot_full = lax.all_gather(out_cot, 'tp', axis=1, tiled=True)  16.5 us
    all_to_all x1, blocking collectives, mix_tokens(): lax.all_to_all(field_now.reshape(feat_rows, all_tokens), 'tok', split_axi...  12.2 us
    all_to_all x2, starting transfers between devices, mix_tokens(): lax.all_to_all(source.T, 'tok', split_axis=0, concat_axis=1, tiled=True)  9 us
    unnamed x46, local copies, waits for them, and re-layouts  7.82 us
    all_to_all x1, waiting for transfers between devices, mix_tokens(): lax.all_to_all(field_now.reshape(feat_rows, all_tokens), 'tok', split_axi...  6.4 us
  transfers between devices with their start and end apart: 5, of which 3 were waited for; matrix products, arithmetic and copies ran while one was open for 21% of the time, Pallas kernels for 0%

commit v1 on v0

v1 whole, which is shorter than its diff:
```python
import functools
import math

import jax
import jax.numpy as jnp
from jax import lax
from jax.experimental import pallas as pl
from jax.experimental.pallas import tpu as pltpu
from jax.sharding import PartitionSpec as P

F32 = jnp.float32
BF16 = jnp.bfloat16
VMEM_LIMIT = 40 * 1024 * 1024
NT = (((1,), (1,)), ((), ()))
NN = (((1,), (0,)), ((), ()))


def contract(matrix, operand, backward):
    pattern = "ji,...j->...i" if backward else "ij,...j->...i"
    return jnp.einsum(pattern, matrix, operand, preferred_element_type=F32)


def plain_section(field_now, section_mats, bit_index, backward):
    full_shape = field_now.shape
    paired = field_now.reshape(
        (full_shape[0], full_shape[1] >> bit_index + 1, 2, 1 << bit_index, full_shape[2])
    )
    lower, upper = paired[:, :, 0], paired[:, :, 1]
    halves = []
    for h in range(2):
        pair = (section_mats[0, h], section_mats[1, h]) if backward else section_mats[h]
        halves.append(contract(pair[0], lower, backward) + contract(pair[1], upper, backward))
    joined = jnp.stack([half.astype(BF16) for half in halves], axis=2)
    return joined.reshape(full_shape)


def plain_mix(field, mix_weights, section_bits, backward):
    owners, feats, toks = field.shape
    block_rows = mix_weights.shape[-1]
    now = field.transpose(1, 0, 2).reshape(feats, owners * toks // block_rows, block_rows)
    order = list(enumerate(section_bits))
    for section_id, bit in order[::-1] if backward else order:
        now = plain_section(now, mix_weights[section_id], bit, backward)
    return now.reshape(feats, owners, toks).transpose(1, 0, 2)


def one_hot(map_row, pool_rows):
    ids = lax.broadcasted_iota(jnp.int32, (pool_rows, map_row.shape[-1]), 0)
    return (map_row == ids).astype(BF16)


def run_sections(field, other, mix_ref, section_bits, backward):
    blocks, feats, rows = field.shape
    order = list(enumerate(section_bits))
    for section_id, bit in order[::-1] if backward else order:
        m = [[mix_ref[section_id, a, b] for b in range(2)] for a in range(2)]
        full = jnp.concatenate(
            [jnp.concatenate(m[0], axis=1), jnp.concatenate(m[1], axis=1)], axis=0
        )
        lows = [b for b in range(blocks) if not (b >> bit) & 1]
        step = max(1, 512 // feats)
        for at in range(0, len(lows), step):
            part = lows[at : at + step]
            low = jnp.concatenate([field[b] for b in part], axis=0)
            high = jnp.concatenate([field[b + (1 << bit)] for b in part], axis=0)
            pair = jnp.concatenate([low, high], axis=1)
            out = lax.dot_general(
                pair, full, NN if backward else NT, preferred_element_type=F32
            ).astype(BF16)
            for n, b in enumerate(part):
                other[b] = out[n * feats : (n + 1) * feats, :rows]
                other[b + (1 << bit)] = out[n * feats : (n + 1) * feats, rows:]
        field, other = other, field
    return field


def forward_kernel(section_bits, pool_rows, x_ref, map_ref, mix_ref, pooled_ref, a_ref, b_ref):
    owners, feats, toks = x_ref.shape
    rows = a_ref.shape[2]
    per = toks // rows
    for g in range(owners):
        for n in range(per):
            a_ref[g * per + n] = x_ref[g, :, n * rows : (n + 1) * rows]
    done = run_sections(a_ref, b_ref, mix_ref, section_bits, False)
    ones = jnp.ones((16, toks), BF16)
    for g in range(owners):
        mine = jnp.concatenate([done[g * per + n] for n in range(per)], axis=1)
        sums = lax.dot_general(
            jnp.concatenate([mine, ones], axis=0),
            one_hot(map_ref[g : g + 1, :], pool_rows),
            NT,
            preferred_element_type=F32,
        )
        pooled_ref[:, g * pool_rows : (g + 1) * pool_rows] = (
            sums[:feats] / sums[feats : feats + 1]
        ).astype(BF16)


def backward_kernel(section_bits, pool_rows, d_ref, map_ref, mix_ref, grad_ref, a_ref, b_ref):
    owners, feats, toks = grad_ref.shape
    rows = a_ref.shape[2]
    per = toks // rows
    for g in range(owners):
        spread = lax.dot_general(
            d_ref[g], one_hot(map_ref[g : g + 1, :], pool_rows), NN, preferred_element_type=F32
        ).astype(BF16)
        for n in range(per):
            a_ref[g * per + n] = spread[:, n * rows : (n + 1) * rows]
    done = run_sections(a_ref, b_ref, mix_ref, section_bits, True)
    for g in range(owners):
        for n in range(per):
            grad_ref[g, :, n * rows : (n + 1) * rows] = done[g * per + n]


def call(kernel, operands, out_shape, scratch, flops, bytes_accessed, name):
    return pl.pallas_call(
        kernel,
        out_shape=out_shape,
        in_specs=[pl.BlockSpec(memory_space=pltpu.VMEM)] * len(operands),
        out_specs=pl.BlockSpec(memory_space=pltpu.VMEM),
        scratch_shapes=scratch,
        compiler_params=pltpu.CompilerParams(vmem_limit_bytes=VMEM_LIMIT),
        cost_estimate=pl.CostEstimate(
            flops=flops, bytes_accessed=bytes_accessed, transcendentals=0
        ),
        name=name,
    )(*operands)


def forward_mix(field, maps, mix_weights, section_bits, pool_rows):
    owners, feats, toks = field.shape
    rows = mix_weights.shape[-1]
    if feats % 16:
        mixed = plain_mix(field, mix_weights, section_bits, False)
        hot = jax.vmap(lambda m: one_hot(m[None], pool_rows))(maps)
        sums = jnp.einsum("gft,gpt->gfp", mixed, hot, preferred_element_type=F32)
        counts = jnp.sum(hot.astype(F32), axis=2)
        pooled = (sums / counts[:, None]).astype(BF16)
        return pooled.transpose(1, 0, 2).reshape(feats, owners * pool_rows)
    blocks = owners * toks // rows
    scratch = [pltpu.VMEM((blocks, feats, rows), BF16)] * 2
    return call(
        functools.partial(forward_kernel, section_bits, pool_rows),
        (field, maps, mix_weights),
        jax.ShapeDtypeStruct((feats, owners * pool_rows), BF16),
        scratch,
        len(section_bits) * 4 * rows * owners * toks * feats,
        field.size * 2 + mix_weights.size * 2,
        "forward_mix",
    )


def backward_mix(d_pooled, maps, mix_weights, section_bits):
    owners, feats, pool_rows = d_pooled.shape
    toks = maps.shape[1]
    rows = mix_weights.shape[-1]
    if feats % 16:
        hot = jax.vmap(lambda m: one_hot(m[None], pool_rows))(maps)
        spread = jnp.einsum("gfp,gpt->gft", d_pooled, hot, preferred_element_type=F32)
        return plain_mix(spread.astype(BF16), mix_weights, section_bits, True)
    blocks = owners * toks // rows
    scratch = [pltpu.VMEM((blocks, feats, rows), BF16)] * 2
    return call(
        functools.partial(backward_kernel, section_bits, pool_rows),
        (d_pooled, maps, mix_weights),
        jax.ShapeDtypeStruct((owners, feats, toks), BF16),
        scratch,
        len(section_bits) * 4 * rows * owners * toks * feats,
        owners * feats * toks * 2 + mix_weights.size * 2,
        "backward_mix",
    )


def shards(tokens, mix_weights, proj_weight, pool_map, out_cot):
    toks, feats_tp = tokens.shape
    section_count, block_rows = mix_weights.shape[0], mix_weights.shape[-1]
    owners, groups = lax.axis_size("tok"), lax.axis_size("tp")
    pool_rows, outs_tp = out_cot.shape
    feats = feats_tp // owners
    outs = outs_tp * groups
    all_bits = (owners * toks // block_rows).bit_length() - 1
    section_bits = [section_id % all_bits for section_id in range(section_count)]
    me = lax.axis_index("tok")

    local_map = pool_map - me * pool_rows
    maps = lax.all_gather(local_map, "tok", axis=0)
    field = lax.all_to_all(
        tokens.T.reshape(owners, feats, toks), "tok", split_axis=0, concat_axis=0, tiled=True
    )
    cot = lax.all_gather(out_cot, "tp", axis=1, tiled=True)
    counts = jnp.sum(one_hot(local_map[None], pool_rows).astype(F32), axis=1)

    d_pooled = lax.dot_general(proj_weight, cot, NT, preferred_element_type=F32)
    d_pooled = (d_pooled / counts[None, :]).astype(BF16).reshape(owners, feats, pool_rows)
    d_pooled = lax.all_to_all(d_pooled, "tok", split_axis=0, concat_axis=0, tiled=True)
    cot_cols = cot.reshape(pool_rows, owners, outs // owners).transpose(1, 0, 2)
    cot_cols = lax.all_to_all(cot_cols, "tok", split_axis=0, concat_axis=0, tiled=True)
    cot_cols = cot_cols.reshape(owners * pool_rows, outs // owners)

    pooled = forward_mix(field, maps, mix_weights, section_bits, pool_rows)
    pooled = lax.all_gather(pooled, "tok", axis=0, tiled=True)

    grad = backward_mix(d_pooled, maps, mix_weights, section_bits)
    grad = lax.all_to_all(grad, "tok", split_axis=0, concat_axis=0, tiled=True)
    token_grad = grad.reshape(feats_tp, toks).T

    mine = lax.dynamic_slice_in_dim(pooled, me * pool_rows, pool_rows, axis=1)
    share = lax.dot_general(
        mine, proj_weight, (((0,), (0,)), ((), ())), preferred_element_type=F32
    ).astype(BF16)
    share = share.reshape(pool_rows, groups, outs_tp).transpose(1, 0, 2)
    share = lax.all_to_all(share, "tp", split_axis=0, concat_axis=0, tiled=True)
    projected = jnp.sum(share.astype(F32), axis=0).astype(BF16)

    proj_grad = lax.dot_general(
        cot_cols, pooled, (((0,), (1,)), ((), ())), preferred_element_type=F32
    ) * (1.0 / math.sqrt(pool_rows * owners))
    return (projected, token_grad, proj_grad)


def solution(mesh):
    in_specs = (P("tok", "tp"), P(), P("tp", None), P("tok"), P("tok", "tp"))
    out_specs = (P("tok", "tp"), P("tok", "tp"), P("tok", "tp"))
    return jax.shard_map(shards, mesh=mesh, in_specs=in_specs, out_specs=out_specs, check_vma=False)
```

time: 159 us -> 105 us (0.66)
  waiting for transfers between devices: 49.7 us -> 20.3 us
  matrix products: 26.9 us -> 2.17 us
  blocking collectives: 28.7 us -> 50.7 us
  local copies, waits for them, and re-layouts: 22.5 us -> 5.98 us
  between operations: 15.1 us -> 0.74 us
  Pallas kernels: 0 us -> 6 us
  starting transfers between devices: 13.3 us -> 16.6 us
    reduce_scatter x2 -> x0, waiting for transfers between devices: 43.3 us -> none  [the longest x1 22.8 us: shards(): lax.psum_scatter(lax.dot_general(proj_weight, pooled, (((0,), (1,)), ((),...]
    all_gather x1 -> x3, blocking collectives: 16.5 us -> 42.2 us  [the longest x1 18 us: shards(): cot = lax.all_gather(out_cot, 'tp', axis=1, tiled=True)]
    dot_general x84 -> x3, matrix products: 26.9 us -> 2.17 us  [the longest x1 1.52 us: shards(): d_pooled = lax.dot_general(proj_weight, cot, NT, preferred_element_type=F32)]
    all_to_all x3 -> x4, waiting for transfers between devices: 6.41 us -> 20.3 us  [the longest x1 11.6 us: shards(): share = lax.all_to_all(share, 'tp', split_axis=0, concat_axis=0, tiled=True)]
    pallas_call x0 -> x2, Pallas kernels: none -> 6 us  [call(): pl.pallas_call(kernel, out_shape=out_shape, in_specs=[pl.BlockSpec(memory...]
    unnamed x46 -> x8, local copies, waits for them, and re-layouts: 7.82 us -> 1.88 us
    gather x1 -> x0, local copies, waits for them, and re-layouts: 3.94 us -> none  [shards(): jnp.take(d_pooled / counts[:, None], local_map, axis=0).astype(jnp.bfloat16)]
    another operation x19 -> x0, local copies, waits for them, and re-layouts: 3.75 us -> none  [the longest x18 3.39 us: local_section(): jnp.stack([new_lower.astype(jnp.bfloat16), new_upper.astype(jnp.bfloat16)...]
  transfers between devices with their start and end apart: 5 -> 4, of which waited for: 3 -> 2; matrix products, arithmetic and copies ran while one was open for 21% -> 5% of each run, Pallas kernels for 0% -> 6%
where the time goes in v1:
time: 105 us; the launch traced here: 104 us
  blocking collectives  50.7 us (48%)
  waiting for transfers between devices  20.3 us (19%)
  starting transfers between devices  16.6 us (16%)
  Pallas kernels  6 us (6%)
  local copies, waits for them, and re-layouts  5.98 us (6%)
  matrix products  2.17 us (2%)
  other arithmetic  1.66 us (2%)
    all_gather x1, blocking collectives, shards(): cot = lax.all_gather(out_cot, 'tp', axis=1, tiled=True)  18 us
    all_gather x1, blocking collectives, shards(): maps = lax.all_gather(local_map, 'tok', axis=0)  12.9 us
    all_to_all x1, waiting for transfers between devices, shards(): share = lax.all_to_all(share, 'tp', split_axis=0, concat_axis=0, tiled=True)  11.6 us
    all_gather x1, blocking collectives, shards(): pooled = lax.all_gather(pooled, 'tok', axis=0, tiled=True)  11.3 us
    all_to_all x1, waiting for transfers between devices, shards(): lax.all_to_all(cot_cols, 'tok', split_axis=0, concat_axis=0, tiled=True)  8.65 us
    all_to_all x1, blocking collectives, shards(): lax.all_to_all(d_pooled, 'tok', split_axis=0, concat_axis=0, tiled=True)  8.54 us
    pallas_call x2, Pallas kernels, call(): pl.pallas_call(kernel, out_shape=out_shape, in_specs=[pl.BlockSpec(memory...  6 us
    all_to_all x1, starting transfers between devices, shards(): share = lax.all_to_all(share, 'tp', split_axis=0, concat_axis=0, tiled=True)  5.5 us
  transfers between devices with their start and end apart: 4, of which 2 were waited for; matrix products, arithmetic and copies ran while one was open for 5% of the time, Pallas kernels for 6%

profile of v1, /device:TPU:0, one launch (start us, length us, event | category | flops | bytes accessed | tf_op | source)
XLA Modules:
  0.0 104.2 jit_solution(546620742915722568)
XLA Ops:
  0.6 0.0 copy-start
  0.7 0.8 broadcast_subtract_fusion
  1.4 0.1 convert_reduce_fusion
  1.6 1.0 copy.27
  2.6 18.0 %all_gather.15 = bf16[128,2048]{0,1:T(8,128)(2,1)} all-gather(bf16[128,512]{0,1:T(8,128)(2,1)S(1)} %copy.27), channel_id=1, replica_groups=mesh['tok'=8,'tp'=4] {'tp'}, dimensions={1}, use_global_device_ids=true | all-gather | bytes 655360 | tf_op jit(solution)/shard_map/all_gather | solution.py:190
  20.6 0.0 copy-done
  20.6 0.0 copy-start.2
  20.6 1.5 %fusion.1 = bf16[256,128]{1,0:T(8,128)(2,1)S(1)} fusion(bf16[256,2048]{1,0:T(8,128)(2,1)S(1)} %copy-done, bf16[128,2048]{0,1:T(8,128)(2,1)} %all_gather.15, f32[128]{0:T(128)S(1)} %convert_reduce_fusion), kind=kOutput, calls=%fused_computation.4 | convolution fusion | flops 134283264 | bytes 1638912 | tf_op jit(solution)/shard_map/dot_general | solution.py:193
  22.1 8.5 %all_to_all.25.d_ref = bf16[8,32,128]{2,1,0:T(8,128)(2,1)S(1)} all-to-all(bf16[8,32,128]{2,1,0:T(8,128)(2,1)S(1)} %bitcast.28), channel_id=1, replica_groups=mesh['tok'=8,'tp'=4] {'tok'}, dimensions={0} | all-to-all | bytes 131072 | tf_op jit(solution)/shard_map/all_to_all | solution.py:195
  30.7 3.5 %all-to-all-start.4 = ((bf16[8,128,256]{1,2,0:T(8,128)(2,1)}), bf16[8,128,256]{1,2,0:T(8,128)(2,1)S(1)}, u32[]{:S(2)}, u32[]{:S(2)}) async-start(bf16[8,128,256]{1,2,0:T(8,128)(2,1)} %bitcast.7), calls=%async_computation.4 | async-start | bytes 1048576 | tf_op jit(solution)/shard_map/all_to_all | solution.py:197
  34.2 0.0 copy-start.1
  34.2 0.0 copy-done.2
  34.2 1.0 copy.25
  35.2 8.7 %all-to-all-done.4 = bf16[8,128,256]{1,2,0:T(8,128)(2,1)S(1)} async-done(((bf16[8,128,256]{1,2,0:T(8,128)(2,1)}), bf16[8,128,256]{1,2,0:T(8,128)(2,1)S(1)}, u32[]{:S(2)}, u32[]{:S(2)}) %all-to-all-start.4) | async-done | bytes 524320 | tf_op jit(solution)/shard_map/all_to_all | solution.py:197
  43.8 3.5 %all-to-all-start = ((bf16[8,32,1024]{2,1,0:T(8,128)(2,1)}), bf16[8,32,1024]{2,1,0:T(8,128)(2,1)S(1)}, u32[]{:S(2)}, u32[]{:S(2)}) async-start(bf16[8,32,1024]{2,1,0:T(8,128)(2,1)} %bitcast.23), calls=%async_computation | async-start | bytes 1048576 | tf_op jit(solution)/shard_map/all_to_all | solution.py:187
  47.3 12.9 %all-gather = s32[8192]{0:T(1024)S(1)} all-gather(s32[1024]{0:T(1024)S(1)} %broadcast_subtract_fusion), channel_id=2, replica_groups=mesh['tok'=8,'tp'=4] {'tok'}, dimensions={0}, use_global_device_ids=true | all-gather | bytes 36864 | tf_op jit(solution)/shard_map/all_gather | solution.py:186
  60.3 0.0 copy-done.1
  60.3 3.2 %backward_mix.1 = bf16[8,32,1024]{2,1,0:T(8,128)(2,1)} custom-call(bf16[8,32,128]{2,1,0:T(8,128)(2,1)S(1)} %all_to_all.25.d_ref, s32[8,1024]{1,0:T(8,128)S(1)} %reshape.32.map_ref, bf16[10,2,2,128,128]{4,3,2,1,0:T(8,128)(2,1)S(1)} %copy-done.1), custom_call_target="tpu_custom_call" | custom-call | flops 1342177280 | bytes 1835008 | tf_op jit(solution)/shard_map/backward_mix/pallas_call | solution.py:116
  63.5 0.0 all-to-all-done.x_ref
  63.5 4.1 %all-to-all-start.3 = ((bf16[8,32,1024]{2,1,0:T(8,128)(2,1)}), bf16[8,32,1024]{2,1,0:T(8,128)(2,1)}, u32[]{:S(2)}, u32[]{:S(2)}) async-start(bf16[8,32,1024]{2,1,0:T(8,128)(2,1)} %backward_mix.1), calls=%async_computation.3 | async-start | bytes 1048576 | tf_op jit(solution)/shard_map/all_to_all | solution.py:204
  67.7 2.8 %forward_mix.1 = bf16[32,1024]{1,0:T(8,128)(2,1)S(1)} custom-call(bf16[8,32,1024]{2,1,0:T(8,128)(2,1)S(1)} %all-to-all-done.x_ref, s32[8,1024]{1,0:T(8,128)S(1)} %reshape.32.map_ref, bf16[10,2,2,128,128]{4,3,2,1,0:T(8,128)(2,1)S(1)} %copy-done.1), custom_call_target="tpu_custom_call" | custom-call | flops 1342177280 | bytes 1835008 | tf_op jit(solution)/shard_map/forward_mix/pallas_call | solution.py:116
  70.5 11.3 %all_gather.14 = bf16[256,1024]{1,0:T(8,128)(2,1)S(1)} all-gather(bf16[32,1024]{1,0:T(8,128)(2,1)S(1)} %forward_mix.1), channel_id=1, replica_groups=mesh['tok'=8,'tp'=4] {'tok'}, dimensions={0}, use_global_device_ids=true | all-gather | bytes 589824 | tf_op jit(solution)/shard_map/all_gather | solution.py:201
  81.7 0.3 convolution_convert_fusion
  82.1 0.8 copy.33
  82.9 0.0 all-to-all-done.3
  82.9 5.5 %all-to-all-start.1 = ((bf16[4,128,512]{2,1,0:T(8,128)(2,1)}), bf16[4,128,512]{2,1,0:T(8,128)(2,1)S(1)}, u32[]{:S(2)}, u32[]{:S(2)}) async-start(bf16[4,128,512]{2,1,0:T(8,128)(2,1)} %bitcast.22), calls=%async_computation.1 | async-start | bytes 1048576 | tf_op jit(solution)/shard_map/all_to_all | solution.py:212
  88.4 0.2 copy.29
  88.7 0.3 fusion
  89.0 0.8 copy.30
  89.8 2.0 %copy.28 = bf16[256,1024]{0,1:T(8,128)(2,1)} copy(bf16[256,1024]{1,0:T(8,128)(2,1)} %bitcast.4) | data formatting | bytes 1048576 | tf_op jit(solution)/shard_map/reshape | solution.py:205
  91.8 11.6 %all-to-all-done.1 = bf16[4,128,512]{2,1,0:T(8,128)(2,1)S(1)} async-done(((bf16[4,128,512]{2,1,0:T(8,128)(2,1)}), bf16[4,128,512]{2,1,0:T(8,128)(2,1)S(1)}, u32[]{:S(2)}, u32[]{:S(2)}) %all-to-all-start.1) | async-done | bytes 524320 | tf_op jit(solution)/shard_map/all_to_all | solution.py:212
  103.4 0.7 reduce_sum.21
  (1 shorter events, 0.0 us)
Async XLA Ops:
  0.6 20.0 %copy-start = (bf16[256,2048]{1,0:T(8,128)(2,1)S(1)}, bf16[256,2048]{1,0:T(8,128)(2,1)}, u32[]{:S(2)}) copy-start(bf16[256,2048]{1,0:T(8,128)(2,1)} %param.7) | copy-start | bytes 3145732
  20.6 13.6 %copy-start.2 = (bf16[1024,256]{1,0:T(8,128)(2,1)S(1)}, bf16[1024,256]{1,0:T(8,128)(2,1)}, u32[]{:S(2)}) copy-start(bf16[1024,256]{1,0:T(8,128)(2,1)} %param.5) | copy-start | bytes 1572868
  30.7 13.2 %all-to-all-start.4 = ((bf16[8,128,256]{1,2,0:T(8,128)(2,1)}), bf16[8,128,256]{1,2,0:T(8,128)(2,1)S(1)}, u32[]{:S(2)}, u32[]{:S(2)}) async-start(bf16[8,128,256]{1,2,0:T(8,128)(2,1)} %bitcast.7), calls=%async_computation.4 | async-start | bytes 1048576 | tf_op jit(solution)/shard_map/all_to_all | solution.py:197
  34.2 26.1 %copy-start.1 = (bf16[10,2,2,128,128]{4,3,2,1,0:T(8,128)(2,1)S(1)}, bf16[10,2,2,128,128]{4,3,2,1,0:T(8,128)(2,1)}, u32[]{:S(2)}) copy-start(bf16[10,2,2,128,128]{4,3,2,1,0:T(8,128)(2,1)} %mix_ref.3) | copy-start | bytes 3932164
  43.8 19.7 %all-to-all-start = ((bf16[8,32,1024]{2,1,0:T(8,128)(2,1)}), bf16[8,32,1024]{2,1,0:T(8,128)(2,1)S(1)}, u32[]{:S(2)}, u32[]{:S(2)}) async-start(bf16[8,32,1024]{2,1,0:T(8,128)(2,1)} %bitcast.23), calls=%async_computation | async-start | bytes 1048576 | tf_op jit(solution)/shard_map/all_to_all | solution.py:187
  63.5 19.4 %all-to-all-start.3 = ((bf16[8,32,1024]{2,1,0:T(8,128)(2,1)}), bf16[8,32,1024]{2,1,0:T(8,128)(2,1)}, u32[]{:S(2)}, u32[]{:S(2)}) async-start(bf16[8,32,1024]{2,1,0:T(8,128)(2,1)} %backward_mix.1), calls=%async_computation.3 | async-start | bytes 1048576 | tf_op jit(solution)/shard_map/all_to_all | solution.py:204
  82.9 20.5 %all-to-all-start.1 = ((bf16[4,128,512]{2,1,0:T(8,128)(2,1)}), bf16[4,128,512]{2,1,0:T(8,128)(2,1)S(1)}, u32[]{:S(2)}, u32[]{:S(2)}) async-start(bf16[4,128,512]{2,1,0:T(8,128)(2,1)} %bitcast.22), calls=%async_computation.1 | async-start | bytes 1048576 | tf_op jit(solution)/shard_map/all_to_all | solution.py:212

commit v2 on v0

--- a/solution.py
+++ b/solution.py
@@ -1,9 +1,20 @@
+import functools
 import math
 
 import jax
 import jax.numpy as jnp
 from jax import lax
+from jax.experimental import pallas as pl
+from jax.experimental.pallas import tpu as pltpu
 from jax.sharding import PartitionSpec as P
+
+F32 = jnp.float32
+BF16 = jnp.bfloat16
+VMEM_LIMIT = 40 * 1024 * 1024
+NT = (((1,), (1,)), ((), ()))
+NN = (((1,), (0,)), ((), ()))
+TAIL = 16
+LONG = 30_000_000_000
 
 
 def contract(matrix, operand, backward):
@@ -60,7 +71,7 @@
     return back_rows.T
 
 
-def shards(tokens, mix_weights, proj_weight, pool_map, out_cot):
+def general_shards(tokens, mix_weights, proj_weight, pool_map, out_cot):
     tok_rows = tokens.shape[0]
     block_rows = mix_weights.shape[-1]
     section_count = mix_weights.shape[0]
@@ -106,6 +117,319 @@
     return (projected, token_grad, proj_grad)
 
 
+def one_hot(map_row, pool_rows):
+    ids = lax.broadcasted_iota(jnp.int32, (pool_rows, map_row.shape[-1]), 0)
+    return (map_row == ids).astype(BF16)
+
+
+def run_sections(field, other, mix_ref, section_bits, backward):
+    blocks, feats, rows = field.shape
+    order = list(enumerate(section_bits))
+    for section_id, bit in order[::-1] if backward else order:
+        m = [[mix_ref[section_id, a, b] for b in range(2)] for a in range(2)]
+        full = jnp.concatenate(
+            [jnp.concatenate(m[0], axis=1), jnp.concatenate(m[1], axis=1)], axis=0
+        )
+        lows = [b for b in range(blocks) if not (b >> bit) & 1]
+        step = max(1, 512 // feats)
+        for at in range(0, len(lows), step):
+            part = lows[at : at + step]
+            low = jnp.concatenate([field[b] for b in part], axis=0)
+            high = jnp.concatenate([field[b + (1 << bit)] for b in part], axis=0)
+            pair = jnp.concatenate([low, high], axis=1)
+            out = lax.dot_general(
+                pair, full, NN if backward else NT, preferred_element_type=F32
+            ).astype(BF16)
+            for n, b in enumerate(part):
+                other[b] = out[n * feats : (n + 1) * feats, :rows]
+                other[b + (1 << bit)] = out[n * feats : (n + 1) * feats, rows:]
+        field, other = other, field
+    return field
+
+
+def pack_kernel(pool_rows, tokens_ref, map_ref, out_ref):
+    owners = out_ref.shape[0]
+    blocks, rows = map_ref.shape
+    feats = tokens_ref.shape[1] // owners
+    maps = lax.rem(map_ref[...], jnp.int32(pool_rows)).astype(F32).astype(BF16)
+    tail = jnp.concatenate([maps, jnp.zeros((TAIL - blocks, rows), BF16)], axis=0)
+    for n in range(blocks):
+        turned = tokens_ref[n * rows : (n + 1) * rows, :].T
+        for g in range(owners):
+            out_ref[g, n * feats : (n + 1) * feats, :] = turned[g * feats : (g + 1) * feats]
+    for g in range(owners):
+        out_ref[g, blocks * feats :, :] = tail
+
+
+def hot_of(packed_ref, g, blocks, pool_rows):
+    maps = packed_ref[g, packed_ref.shape[1] - TAIL :, :].astype(F32).astype(jnp.int32)
+    return jnp.concatenate([one_hot(maps[n : n + 1], pool_rows) for n in range(blocks)], axis=1)
+
+
+def forward_kernel(section_bits, blocks, mix_ref, packed_ref, out_ref, a_ref, b_ref):
+    owners, both, pool_rows = out_ref.shape
+    feats, rows = both // 2, a_ref.shape[2]
+    for g in range(owners):
+        for n in range(blocks):
+            a_ref[g * blocks + n] = packed_ref[g, n * feats : (n + 1) * feats, :]
+    done = run_sections(a_ref, b_ref, mix_ref, section_bits, False)
+    ones = jnp.ones((16, blocks * rows), BF16)
+    for g in range(owners):
+        mine = jnp.concatenate([done[g * blocks + n] for n in range(blocks)], axis=1)
+        sums = lax.dot_general(
+            jnp.concatenate([mine, ones], axis=0),
+            hot_of(packed_ref, g, blocks, pool_rows),
+            NT,
+            preferred_element_type=F32,
+        )
+        pooled = (sums[:feats] / sums[feats : feats + 1]).astype(BF16)
+        out_ref[g, :feats, :] = pooled
+        out_ref[g ^ 1, feats:, :] = pooled
+
+
+def backward_kernel(section_bits, blocks, mix_ref, d_ref, packed_ref, out_ref, a_ref, b_ref):
+    owners, feats, _ = out_ref.shape
+    pool_rows, rows = d_ref.shape[2], a_ref.shape[2]
+    for g in range(owners):
+        spread = lax.dot_general(
+            d_ref[g, :feats], hot_of(packed_ref, g, blocks, pool_rows), NN, preferred_element_type=F32
+        ).astype(BF16)
+        for n in range(blocks):
+            a_ref[g * blocks + n] = spread[:, n * rows : (n + 1) * rows]
+    done = run_sections(a_ref, b_ref, mix_ref, section_bits, True)
+    for g in range(owners):
+        for n in range(blocks):
+            out_ref[g, :, n * rows : (n + 1) * rows] = done[g * blocks + n]
+
+
+def unpack_kernel(grad_ref, out_ref):
+    owners, _, toks = grad_ref.shape
+    for at in range(0, toks, 128):
+        turned = jnp.concatenate([grad_ref[g, :, at : at + 128] for g in range(owners)], axis=0)
+        out_ref[at : at + 128, :] = turned.T
+
+
+def early_kernel(order, w_ref, *refs):
+    *cots, out_ref = refs
+    outs_tp = cots[0].shape[1]
+    place = lax.axis_index("tp")
+    total = None
+    for o, cot in zip(order, cots):
+        at = pl.multiple_of((place ^ o) * outs_tp, outs_tp)
+        part = lax.dot_general(
+            cot[...], w_ref[:, pl.ds(at, outs_tp)], NT, preferred_element_type=F32
+        )
+        total = part if total is None else total + part
+    out_ref[...] = total
+
+
+def cotangent_kernel(groups, late, w_ref, map_ref, pooled_ref, early_ref, *refs):
+    cots, out_ref, send_ref = refs[:groups], refs[groups], refs[groups + 1]
+    owners, both, pool_rows = pooled_ref.shape
+    feats = both // 2
+    outs_tp = cots[0].shape[1]
+    outs = send_ref.shape[1] // groups
+    place = lax.axis_index("tp")
+    other = pl.multiple_of((1 - lax.axis_index("tok") % 2) * outs, outs)
+    total = early_ref[...]
+    for o in late:
+        at = pl.multiple_of((place ^ o) * outs_tp, outs_tp)
+        total = total + lax.dot_general(
+            cots[o][...], w_ref[:, pl.ds(at, outs_tp)], NT, preferred_element_type=F32
+        )
+    counts = jnp.zeros((pool_rows, 1), F32)
+    maps = lax.rem(map_ref[...], jnp.int32(pool_rows))
+    for n in range(maps.shape[0]):
+        ids = lax.broadcasted_iota(jnp.int32, (pool_rows, maps.shape[1]), 0)
+        hits = (maps[n : n + 1] == ids).astype(F32)
+        counts = counts + jnp.sum(hits, axis=1, keepdims=True)
+    turned = (total / counts).T.astype(BF16)
+    for g in range(owners):
+        out_ref[g, :feats, :] = turned[g * feats : (g + 1) * feats]
+        out_ref[g, feats:, :] = pooled_ref[g]
+    for o in range(groups):
+        send_ref[:, o * outs : (o + 1) * outs] = cots[o][:, pl.ds(other, outs)]
+
+
+def project_kernel(got_ref, w_ref, came_ref, *refs):
+    cots, (kept_ref, sent_ref, held_ref, gone_ref) = refs[:4], refs[4:8]
+    share_ref, part_ref, sems = refs[8:]
+    owners, feats = got_ref.shape[0], got_ref.shape[1] // 3
+    outs_tp = cots[0].shape[1]
+    outs = came_ref.shape[1] // 4
+    place, me = lax.axis_index("tp"), lax.axis_index("tok")
+    copies = []
+
+    def send(source, target):
+        copies.append(pltpu.make_async_copy(source, target, sems.at[len(copies)]))
+        copies[-1].start()
+
+    mine = pl.multiple_of((me % 2) * outs, outs)
+    turned = jnp.concatenate([got_ref[g, feats : 2 * feats, :] for g in range(owners)], axis=0)
+    others = jnp.concatenate([got_ref[g, 2 * feats :, :] for g in range(owners)], axis=0)
+    pooled = turned.T
+    turned = jnp.concatenate([turned, others], axis=1)
+    for o in (1, 3, 0, 2):
+        at = pl.multiple_of((place ^ o) * outs_tp, outs_tp)
+        share_ref[o] = lax.dot_general(
+            pooled, w_ref[:, pl.ds(at, outs_tp)], NN, preferred_element_type=F32
+        ).astype(BF16)
+        send(share_ref.at[o], (sent_ref if o % 2 else kept_ref).at[o // 2])
+    for o in range(4):
+        cot = jnp.concatenate(
+            [cots[o][:, pl.ds(mine, outs)], came_ref[:, o * outs : (o + 1) * outs]], axis=0
+        )
+        part_ref[place ^ o] = lax.dot_general(
+            turned, cot, NN, preferred_element_type=F32
+        ).astype(BF16)
+    for o in (1, 3, 0, 2):
+        send(part_ref.at[(me // 2) ^ o], (gone_ref if o % 2 else held_ref).at[o // 2])
+    for copy in copies:
+        copy.wait()
+
+
+def fold_kernel(kept_ref, got_ref, held_ref, came_ref, share_ref, part_ref):
+    share_ref[...] = (kept_ref[1].astype(F32) + got_ref[1].astype(F32)).astype(BF16)
+    part_ref[...] = (held_ref[1].astype(F32) + came_ref[1].astype(F32)).astype(BF16)
+
+
+def sum_kernel(scale, kept_ref, got_ref, share_ref, held_ref, came_ref, part_ref, projected_ref, grad_ref):
+    total = kept_ref[0].astype(F32) + got_ref[0].astype(F32) + share_ref[...].astype(F32)
+    projected_ref[...] = total.astype(BF16)
+    total = held_ref[0].astype(F32) + came_ref[0].astype(F32) + part_ref[...].astype(F32)
+    grad_ref[...] = total.T * scale
+
+
+def call(kernel, operands, out_shape, scratch, name, cost=0, out_space=pltpu.VMEM):
+    several = isinstance(out_shape, (list, tuple))
+    vmem = pl.BlockSpec(memory_space=pltpu.VMEM)
+    out = pl.BlockSpec(memory_space=out_space)
+    return pl.pallas_call(
+        kernel,
+        out_shape=out_shape,
+        in_specs=[vmem] * len(operands),
+        out_specs=[out] * len(out_shape) if several else out,
+        scratch_shapes=scratch,
+        compiler_params=pltpu.CompilerParams(vmem_limit_bytes=VMEM_LIMIT),
+        cost_estimate=pl.CostEstimate(flops=cost, bytes_accessed=0, transcendentals=0),
+        name=name,
+    )(*operands)
+
+
+def struct(*shape, dtype=BF16):
+    return jax.ShapeDtypeStruct(shape, dtype)
+
+
+def in_hbm(*shape, dtype=BF16):
+    return pltpu.HBM(shape, dtype)
+
+
+def swap(piece, axis, offset):
+    size = lax.axis_size(axis)
+    return lax.ppermute(piece, axis, [(i, i ^ offset) for i in range(size)])
+
+
+def swap_all(pieces, axis):
+    return [pieces[0]] + [swap(piece, axis, o) for o, piece in enumerate(pieces) if o]
+
+
+def exchange(pieces, axis):
+    return lax.all_to_all(pieces, axis, split_axis=0, concat_axis=0, tiled=True)
+
+
+def shards(tokens, mix_weights, proj_weight, pool_map, out_cot):
+    toks, feats_tp = tokens.shape
+    section_count, rows = mix_weights.shape[0], mix_weights.shape[-1]
+    owners, groups = lax.axis_size("tok"), lax.axis_size("tp")
+    pool_rows, outs_tp = out_cot.shape
+    outs = outs_tp * groups // owners
+    feats = feats_tp // owners
+    blocks = toks // rows
+    if feats % 16 or outs % 128 or owners != 8 or groups != 4 or pool_rows > 256 or blocks > TAIL:
+        return general_shards(tokens, mix_weights, proj_weight, pool_map, out_cot)
+    all_bits = (owners * blocks).bit_length() - 1
+    section_bits = [section_id % all_bits for section_id in range(section_count)]
+    fields = [pltpu.VMEM((owners * blocks, feats, rows), BF16)] * 2
+
+    cots = [out_cot] + [swap(out_cot, "tp", o) for o in range(1, groups)]
+    maps = pool_map.reshape(blocks, rows)
+    packed = call(
+        functools.partial(pack_kernel, pool_rows),
+        (tokens, maps),
+        struct(owners, blocks * feats + TAIL, rows),
+        [],
+        "pack",
+    )
+    packed = exchange(packed, "tok")
+    order = [0] + list(range(2, groups))
+    early = call(
+        functools.partial(early_kernel, order),
+        (proj_weight, *[cots[o] for o in order]),
+        struct(pool_rows, feats_tp, dtype=F32),
+        [],
+        "early_cotangent",
+        LONG,
+    )
+    packed, early = lax.optimization_barrier((packed, early))
+    pooled = call(
+        functools.partial(forward_kernel, section_bits, blocks),
+        (mix_weights, packed),
+        struct(owners, 2 * feats, pool_rows),
+        fields,
+        "forward_mix",
+    )
+    both, half = call(
+        functools.partial(cotangent_kernel, groups, [1]),
+        (proj_weight, maps, pooled, early, *cots),
+        [struct(owners, 3 * feats, pool_rows), struct(pool_rows, groups * outs)],
+        [],
+        "cotangent",
+    )
+    half = swap(half, "tok", 1)
+    both = exchange(both, "tok")
+
+    kept, sent, held, gone = call(
+        project_kernel,
+        (both, proj_weight, half, *cots),
+        [in_hbm(2, pool_rows, outs_tp)] * 2 + [in_hbm(2, feats_tp, outs)] * 2,
+        [
+            pltpu.VMEM((4, pool_rows, outs_tp), BF16),
+            pltpu.VMEM((4, feats_tp, outs), BF16),
+            pltpu.SemaphoreType.DMA((8,)),
+        ],
+        "project",
+        out_space=pltpu.HBM,
+    )
+    sent, gone = swap(sent, "tp", 1), swap(gone, "tok", 2)
+    share, part = call(
+        fold_kernel,
+        (kept, sent, held, gone),
+        [struct(pool_rows, outs_tp), struct(feats_tp, outs)],
+        [],
+        "fold",
+        LONG,
+    )
+    share, part = swap(share, "tp", 2), swap(part, "tok", 4)
+    projected, proj_grad = call(
+        functools.partial(sum_kernel, 1.0 / math.sqrt(pool_rows * owners)),
+        (kept, sent, share, held, gone, part),
+        [struct(pool_rows, outs_tp), struct(outs, feats_tp, dtype=F32)],
+        [],
+        "sums",
+    )
+
+    grad = call(
+        functools.partial(backward_kernel, section_bits, blocks),
+        (mix_weights, both, packed),
+        struct(owners, feats, toks),
+        fields,
+        "backward_mix",
+    )
+    grad = exchange(grad, "tok")
+    token_grad = call(unpack_kernel, (grad,), struct(toks, feats_tp), [], "unpack")
+    return (projected, token_grad, proj_grad)
+
+
 def solution(mesh):
     in_specs = (P("tok", "tp"), P(), P("tp", None), P("tok"), P("tok", "tp"))
     out_specs = (P("tok", "tp"), P("tok", "tp"), P("tok", "tp"))

time: 159 us -> 57.8 us (0.36)
  waiting for transfers between devices: 49.7 us -> 15 us
  matrix products: 26.9 us -> 0 us
  local copies, waits for them, and re-layouts: 22.5 us -> 2.4 us
  blocking collectives: 28.7 us -> 8.63 us
  between operations: 15.1 us -> 0.76 us
  Pallas kernels: 0 us -> 11 us
  starting transfers between devices: 13.3 us -> 19.6 us
  other arithmetic: 2.25 us -> 0 us
    reduce_scatter x2 -> x0, waiting for transfers between devices: 43.3 us -> none  [the longest x1 22.8 us: shards(): lax.psum_scatter(lax.dot_general(proj_weight, pooled, (((0,), (1,)), ((),...]
    dot_general x84 -> x0, matrix products: 26.9 us -> none  [the longest x80 23.2 us: contract(): jnp.einsum(pattern, matrix, operand, preferred_element_type=jnp.float32)]
    all_gather x1 -> x0, blocking collectives: 16.5 us -> none  [shards(): cot_full = lax.all_gather(out_cot, 'tp', axis=1, tiled=True)]
    ppermute x0 -> x8, starting transfers between devices: none -> 12.2 us  [swap(): return lax.ppermute(piece, axis, [(i, i ^ offset) for i in range(size)])]
    pallas_call x0 -> x9, Pallas kernels: none -> 11 us  [call(): pl.pallas_call(kernel, out_shape=out_shape, in_specs=[vmem] * len(operand...]
    all_to_all x3 -> x2, starting transfers between devices: 13.2 us -> 7.36 us  [exchange(): return lax.all_to_all(pieces, axis, split_axis=0, concat_axis=0, tiled=True)]
    unnamed x46 -> x20, local copies, waits for them, and re-layouts: 7.82 us -> 2.4 us
    ppermute x0 -> x8, waiting for transfers between devices: none -> 5.26 us  [swap(): return lax.ppermute(piece, axis, [(i, i ^ offset) for i in range(size)])]
  transfers between devices with their start and end apart: 5 -> 10, of which waited for: 3 -> 5; matrix products, arithmetic and copies ran while one was open for 21% -> 0% of each run, Pallas kernels for 0% -> 15%
where the time goes in v2:
time: 57.8 us; the launch traced here: 57.4 us
  starting transfers between devices  19.6 us (34%)
  waiting for transfers between devices  15 us (26%)
  Pallas kernels  11 us (19%)
  blocking collectives  8.63 us (15%)
  local copies, waits for them, and re-layouts  2.4 us (4%)
  between operations  0.76 us (1%)
    ppermute x8, starting transfers between devices, swap(): return lax.ppermute(piece, axis, [(i, i ^ offset) for i in range(size)])  12.2 us
    pallas_call x9, Pallas kernels, call(): pl.pallas_call(kernel, out_shape=out_shape, in_specs=[vmem] * len(operand...  11 us
    all_to_all x2, waiting for transfers between devices, exchange(): return lax.all_to_all(pieces, axis, split_axis=0, concat_axis=0, tiled=True)  9.75 us
    all_to_all x1, blocking collectives, exchange(): return lax.all_to_all(pieces, axis, split_axis=0, concat_axis=0, tiled=True)  8.63 us
    all_to_all x2, starting transfers between devices, exchange(): return lax.all_to_all(pieces, axis, split_axis=0, concat_axis=0, tiled=True)  7.36 us
    ppermute x8, waiting for transfers between devices, swap(): return lax.ppermute(piece, axis, [(i, i ^ offset) for i in range(size)])  5.26 us
    unnamed x20, local copies, waits for them, and re-layouts  2.4 us
  transfers between devices with their start and end apart: 10, of which 5 were waited for; matrix products, arithmetic and copies ran while one was open for 0% of the time, Pallas kernels for 15%

profile of v2, /device:TPU:0, one launch (start us, length us, event | category | flops | bytes accessed | tf_op | source)
XLA Modules:
  0.0 57.4 jit_solution(9346153160424487297)
XLA Ops:
  0.6 0.0 copy-start.2
  0.6 0.0 copy-start.1
  0.7 5.1 %collective-permute-start.1 = (bf16[128,512]{1,0:T(8,128)(2,1)}, bf16[128,512]{1,0:T(8,128)(2,1)S(1)}, u32[]{:S(2)}, u32[]{:S(2)}) collective-permute-start(bf16[128,512]{1,0:T(8,128)(2,1)} %refs_0_.5), channel_id=1, source_target_pairs={{0,3},{1,2},{2,1},{3,0},{4,7},{5,6},{6,5},{7,4},{8,11},{9,10},{10,... | collective-permute-start | bytes 393224 | tf_op jit(solution)/shard_map/ppermute | solution.py:329
  5.8 0.0 collective-permute-start
  5.8 0.6 %collective-permute-start.2 = (bf16[128,512]{1,0:T(8,128)(2,1)}, bf16[128,512]{1,0:T(8,128)(2,1)S(1)}, u32[]{:S(2)}, u32[]{:S(2)}) collective-permute-start(bf16[128,512]{1,0:T(8,128)(2,1)} %refs_0_.5), channel_id=1, source_target_pairs={{0,1},{1,0},{2,3},{3,2},{4,5},{5,4},{6,7},{7,6},{8,9},{9,8},{10,11... | collective-permute-start | bytes 393224 | tf_op jit(solution)/shard_map/ppermute | solution.py:329
  6.4 0.0 copy-start.3
  6.4 1.0 %copy-done.3 = bf16[1024,256]{1,0:T(8,128)(2,1)S(1)} copy-done((bf16[1024,256]{1,0:T(8,128)(2,1)S(1)}, bf16[1024,256]{1,0:T(8,128)(2,1)}, u32[]{:S(2)}) %copy-start.3) | copy-done | bytes 524312
  7.4 0.0 copy-start.8
  7.5 0.7 %copy-done.8 = s32[1024]{0:T(1024)S(1)} copy-done((s32[1024]{0:T(1024)S(1)}, s32[1024]{0:T(1024)}, u32[]{:S(2)}) %copy-start.8) | copy-done | bytes 4120
  8.1 1.0 %pack.1 = bf16[8,272,128]{2,1,0:T(8,128)(2,1)} custom-call(bf16[1024,256]{1,0:T(8,128)(2,1)S(1)} %copy-done.3, s32[8,128]{1,0:T(8,128)S(1)} %bitcast.1), custom_call_target="tpu_custom_call" | custom-call | tf_op jit(solution)/shard_map/pack/pallas_call | solution.py:307
  9.1 3.9 %all-to-all-start = ((bf16[8,272,128]{2,1,0:T(8,128)(2,1)}), bf16[8,272,128]{2,1,0:T(8,128)(2,1)S(1)}, u32[]{:S(2)}, u32[]{:S(2)}) async-start(bf16[8,272,128]{2,1,0:T(8,128)(2,1)} %pack.1), calls=%async_computation | async-start | bytes 1114112 | tf_op jit(solution)/shard_map/all_to_all | solution.py:337
  13.0 0.0 copy-start
  13.0 0.0 collective-permute-done.1.refs_2_.refs_3_
  13.0 4.0 %collective-permute-done.refs_1_.refs_2_ = bf16[128,512]{1,0:T(8,128)(2,1)S(1)} collective-permute-done((bf16[128,512]{1,0:T(8,128)(2,1)}, bf16[128,512]{1,0:T(8,128)(2,1)S(1)}, u32[]{:S(2)}, u32[]{:S(2)}) %collective-permute-start) | collective-permute-done | bytes 131104 | tf_op jit(solution)/shard_map/ppermute | solution.py:329
  17.1 0.0 copy-done.2
  17.1 0.0 copy-done.1
  17.1 0.4 early_cotangent.1.early_ref
  17.5 0.0 copy-start.6
  17.5 0.6 %copy-done.6 = f32[128,256]{1,0:T(8,128)} copy-done((f32[128,256]{1,0:T(8,128)}, f32[128,256]{1,0:T(8,128)S(1)}, u32[]{:S(2)}) %copy-start.6) | copy-done | bytes 131096
  18.1 0.0 copy-start.9
  18.1 5.0 %all-to-all-done.packed_ref = bf16[8,272,128]{2,1,0:T(8,128)(2,1)S(1)} async-done(((bf16[8,272,128]{2,1,0:T(8,128)(2,1)}), bf16[8,272,128]{2,1,0:T(8,128)(2,1)S(1)}, u32[]{:S(2)}, u32[]{:S(2)}) %all-to-all-start) | async-done | bytes 557088 | tf_op jit(solution)/shard_map/all_to_all | solution.py:337
  23.1 0.0 copy-done
  23.1 0.0 copy-start.7
  23.1 2.8 %forward_mix.1.pooled_ref = bf16[8,64,128]{2,1,0:T(8,128)(2,1)S(1)} custom-call(bf16[10,2,2,128,128]{4,3,2,1,0:T(8,128)(2,1)S(1)} %copy-done, bf16[8,272,128]{2,1,0:T(8,128)(2,1)S(1)} %all-to-all-done.packed_ref), custom_call_target="tpu_custom_call" | custom-call | tf_op jit(solution)/shard_map/forward_mix/pallas_call | solution.py:307
  25.9 0.0 collective-permute-done.2.refs_1_
  25.9 0.0 copy-done.9
  25.9 0.0 copy-done.7
  26.0 0.3 cotangent.1
  26.3 0.1 collective-permute-start.3
  26.4 8.6 %all_to_all.15.got_ref.d_ref = bf16[8,96,128]{2,1,0:T(8,128)(2,1)S(1)} all-to-all(bf16[8,96,128]{2,1,0:T(8,128)(2,1)S(1)} %get-tuple-element.17), channel_id=1, replica_groups=mesh['tok'=8,'tp'=4] {'tok'}, dimensions={0} | all-to-all | bytes 393216 | tf_op jit(solution)/shard_map/all_to_all | solution.py:337
  35.0 0.0 collective-permute-done.3.came_ref
  35.0 1.3 %project.1 = (bf16[2,128,512]{2,1,0:T(8,128)(2,1)}, bf16[2,128,512]{2,1,0:T(8,128)(2,1)}, bf16[2,256,256]{2,1,0:T(8,128)(2,1)}, bf16[2,256,256]{2,1,0:T(8,128)(2,1)}) custom-call(bf16[8,96,128]{2,1,0:T(8,128)(2,1)S(1)} %all_to_all.15.got_ref.d_ref, bf16[256,2048]{1,0:T(8,128)(2,1)S(1)} %copy-done.1, bf16[128,1024]{1,0:T(8,128)(2,1)S(1)} %collective-permute-done.3.came_ref, ...), custom_call_target="tpu_custom_call" | custom-call | tf_op jit(solution)/shard_map/project/pallas_call | solution.py:307
  36.3 1.3 %collective-permute-start.4 = (bf16[2,128,512]{2,1,0:T(8,128)(2,1)}, bf16[2,128,512]{2,1,0:T(8,128)(2,1)S(1)}, u32[]{:S(2)}, u32[]{:S(2)}) collective-permute-start(bf16[2,128,512]{2,1,0:T(8,128)(2,1)} %get-tuple-element.20), channel_id=1, source_target_pairs={{0,1},{1,0},{2,3},{3,2},{4,5},{5,4},{6,7},{7,6},{8,9},{9,8},{10,11... | collective-permute-start | bytes 786440 | tf_op jit(solution)/shard_map/ppermute | solution.py:329
  37.7 0.6 collective-permute-start.5
  38.2 3.2 %backward_mix.1 = bf16[8,32,1024]{2,1,0:T(8,128)(2,1)} custom-call(bf16[10,2,2,128,128]{4,3,2,1,0:T(8,128)(2,1)S(1)} %copy-done, bf16[8,96,128]{2,1,0:T(8,128)(2,1)S(1)} %all_to_all.15.got_ref.d_ref, bf16[8,272,128]{2,1,0:T(8,128)(2,1)S(1)} %all-to-all-done.packed_ref), custom_call_target="tpu_custom_call" | custom-call | tf_op jit(solution)/shard_map/backward_mix/pallas_call | solution.py:307
  41.4 3.5 %all-to-all-start.2 = ((bf16[8,32,1024]{2,1,0:T(8,128)(2,1)}), bf16[8,32,1024]{2,1,0:T(8,128)(2,1)S(1)}, u32[]{:S(2)}, u32[]{:S(2)}) async-start(bf16[8,32,1024]{2,1,0:T(8,128)(2,1)} %backward_mix.1), calls=%async_computation.2 | async-start | bytes 1048576 | tf_op jit(solution)/shard_map/all_to_all | solution.py:337
  44.9 0.0 collective-permute-done.4.got_ref
  44.9 0.4 collective-permute-done.5.came_ref
  45.3 0.0 copy-done.4
  45.3 0.0 copy-done.5
  45.3 0.1 fold.1
  45.4 3.0 %collective-permute-start.6 = (bf16[128,512]{1,0:T(8,128)(2,1)S(1)}, bf16[128,512]{1,0:T(8,128)(2,1)S(1)}, u32[]{:S(2)}, u32[]{:S(2)}) collective-permute-start(bf16[128,512]{1,0:T(8,128)(2,1)S(1)} %get-tuple-element.23), channel_id=1, source_target_pairs={{0,2},{1,3},{2,0},{3,1},{4,6},{5,7},{6,4},{7,5},{8,10},{9,11},{10,... | collective-permute-start | bytes 393224 | tf_op jit(solution)/shard_map/ppermute | solution.py:329
  48.4 1.5 %collective-permute-start.7 = (bf16[256,256]{1,0:T(8,128)(2,1)S(1)}, bf16[256,256]{1,0:T(8,128)(2,1)S(1)}, u32[]{:S(2)}, u32[]{:S(2)}) collective-permute-start(bf16[256,256]{1,0:T(8,128)(2,1)S(1)} %get-tuple-element.24), channel_id=1, source_target_pairs={{0,16},{4,20},{8,24},{12,28},{16,0},{20,4},{24,8},{28,12},{1,17},{... | collective-permute-start | bytes 393224 | tf_op jit(solution)/shard_map/ppermute | solution.py:329
  49.9 4.8 %all-to-all-done.2.grad_ref = bf16[8,32,1024]{2,1,0:T(8,128)(2,1)S(1)} async-done(((bf16[8,32,1024]{2,1,0:T(8,128)(2,1)}), bf16[8,32,1024]{2,1,0:T(8,128)(2,1)S(1)}, u32[]{:S(2)}, u32[]{:S(2)}) %all-to-all-start.2) | async-done | bytes 524320 | tf_op jit(solution)/shard_map/all_to_all | solution.py:337
  54.7 1.0 %unpack.1 = bf16[1024,256]{1,0:T(8,128)(2,1)} custom-call(bf16[8,32,1024]{2,1,0:T(8,128)(2,1)S(1)} %all-to-all-done.2.grad_ref), custom_call_target="tpu_custom_call" | custom-call | tf_op jit(solution)/shard_map/unpack/pallas_call | solution.py:307
  55.7 0.0 collective-permute-done.6.share_ref
  55.7 0.8 %collective-permute-done.7.part_ref = bf16[256,256]{1,0:T(8,128)(2,1)S(1)} collective-permute-done((bf16[256,256]{1,0:T(8,128)(2,1)S(1)}, bf16[256,256]{1,0:T(8,128)(2,1)S(1)}, u32[]{:S(2)}, u32[]{:S(2)}) %collective-permute-start.7) | collective-permute-done | bytes 131104 | tf_op jit(solution)/shard_map/ppermute | solution.py:329
  56.5 0.9 %sums.1 = (bf16[128,512]{1,0:T(8,128)(2,1)}, f32[256,256]{1,0:T(8,128)}) custom-call(bf16[2,128,512]{2,1,0:T(8,128)(2,1)S(1)} %copy-done.4, bf16[2,128,512]{2,1,0:T(8,128)(2,1)S(1)} %collective-permute-done.4.got_ref, bf16[128,512]{1,0:T(8,128)(2,1)S(1)} %collective-permute-done.6.share_ref, bf16[2,256,256]{2,1,0:T(8,128)(2,1)S(1)} %copy-done.5, ...), custom_call_target="tpu_custom_call" | custom-call | tf_op jit(solution)/shard_map/sums/pallas_call | solution.py:307
  (2 shorter events, 0.0 us)
Async XLA Ops:
  0.6 16.4 %copy-start.2 = (bf16[128,512]{1,0:T(8,128)(2,1)S(1)}, bf16[128,512]{1,0:T(8,128)(2,1)}, u32[]{:S(2)}) copy-start(bf16[128,512]{1,0:T(8,128)(2,1)} %refs_0_.5) | copy-start | bytes 393220
  0.6 16.4 %copy-start.1 = (bf16[256,2048]{1,0:T(8,128)(2,1)S(1)}, bf16[256,2048]{1,0:T(8,128)(2,1)}, u32[]{:S(2)}) copy-start(bf16[256,2048]{1,0:T(8,128)(2,1)} %w_ref.5) | copy-start | bytes 3145732
  0.7 12.4 %collective-permute-start.1 = (bf16[128,512]{1,0:T(8,128)(2,1)}, bf16[128,512]{1,0:T(8,128)(2,1)S(1)}, u32[]{:S(2)}, u32[]{:S(2)}) collective-permute-start(bf16[128,512]{1,0:T(8,128)(2,1)} %refs_0_.5), channel_id=1, source_target_pairs={{0,3},{1,2},{2,1},{3,0},{4,7},{5,6},{6,5},{7,4},{8,11},{9,10},{10,... | collective-permute-start | bytes 393224 | tf_op jit(solution)/shard_map/ppermute | solution.py:329
  5.8 11.3 %collective-permute-start = (bf16[128,512]{1,0:T(8,128)(2,1)}, bf16[128,512]{1,0:T(8,128)(2,1)S(1)}, u32[]{:S(2)}, u32[]{:S(2)}) collective-permute-start(bf16[128,512]{1,0:T(8,128)(2,1)} %refs_0_.5), channel_id=1, source_target_pairs={{0,2},{1,3},{2,0},{3,1},{4,6},{5,7},{6,4},{7,5},{8,10},{9,11},{10,... | collective-permute-start | bytes 393224 | tf_op jit(solution)/shard_map/ppermute | solution.py:329
  5.8 20.2 %collective-permute-start.2 = (bf16[128,512]{1,0:T(8,128)(2,1)}, bf16[128,512]{1,0:T(8,128)(2,1)S(1)}, u32[]{:S(2)}, u32[]{:S(2)}) collective-permute-start(bf16[128,512]{1,0:T(8,128)(2,1)} %refs_0_.5), channel_id=1, source_target_pairs={{0,1},{1,0},{2,3},{3,2},{4,5},{5,4},{6,7},{7,6},{8,9},{9,8},{10,11... | collective-permute-start | bytes 393224 | tf_op jit(solution)/shard_map/ppermute | solution.py:329
  6.4 1.0 %copy-start.3 = (bf16[1024,256]{1,0:T(8,128)(2,1)S(1)}, bf16[1024,256]{1,0:T(8,128)(2,1)}, u32[]{:S(2)}) copy-start(bf16[1024,256]{1,0:T(8,128)(2,1)} %tokens_ref.1) | copy-start | bytes 1572868
  7.4 0.7 %copy-start.8 = (s32[1024]{0:T(1024)S(1)}, s32[1024]{0:T(1024)}, u32[]{:S(2)}) copy-start(s32[1024]{0:T(1024)} %param.8) | copy-start | bytes 12292
  9.1 14.0 %all-to-all-start = ((bf16[8,272,128]{2,1,0:T(8,128)(2,1)}), bf16[8,272,128]{2,1,0:T(8,128)(2,1)S(1)}, u32[]{:S(2)}, u32[]{:S(2)}) async-start(bf16[8,272,128]{2,1,0:T(8,128)(2,1)} %pack.1), calls=%async_computation | async-start | bytes 1114112 | tf_op jit(solution)/shard_map/all_to_all | solution.py:337
  13.0 10.1 %copy-start = (bf16[10,2,2,128,128]{4,3,2,1,0:T(8,128)(2,1)S(1)}, bf16[10,2,2,128,128]{4,3,2,1,0:T(8,128)(2,1)}, u32[]{:S(2)}) copy-start(bf16[10,2,2,128,128]{4,3,2,1,0:T(8,128)(2,1)} %mix_ref.3) | copy-start | bytes 3932164
  17.5 0.7 %copy-start.6 = (f32[128,256]{1,0:T(8,128)}, f32[128,256]{1,0:T(8,128)S(1)}, u32[]{:S(2)}) copy-start(f32[128,256]{1,0:T(8,128)S(1)} %early_cotangent.1.early_ref) | copy-start | bytes 393220
  18.1 7.8 %copy-start.9 = (s32[1024]{0:T(1024)S(1)}, s32[1024]{0:T(1024)}, u32[]{:S(2)}) copy-start(s32[1024]{0:T(1024)} %param.8) | copy-start | bytes 12292
  23.1 2.8 %copy-start.7 = (f32[128,256]{1,0:T(8,128)S(1)}, f32[128,256]{1,0:T(8,128)}, u32[]{:S(2)}) copy-start(f32[128,256]{1,0:T(8,128)} %copy-done.6) | copy-start | bytes 393220
  26.3 8.7 %collective-permute-start.3 = (bf16[128,1024]{1,0:T(8,128)(2,1)S(1)}, bf16[128,1024]{1,0:T(8,128)(2,1)S(1)}, u32[]{:S(2)}, u32[]{:S(2)}) collective-permute-start(bf16[128,1024]{1,0:T(8,128)(2,1)S(1)} %get-tuple-element.18), channel_id=1, source_target_pairs={{0,4},{4,0},{8,12},{12,8},{16,20},{20,16},{24,28},{28,24},{1,5},{5... | collective-permute-start | bytes 786440 | tf_op jit(solution)/shard_map/ppermute | solution.py:329
  36.3 8.6 %collective-permute-start.4 = (bf16[2,128,512]{2,1,0:T(8,128)(2,1)}, bf16[2,128,512]{2,1,0:T(8,128)(2,1)S(1)}, u32[]{:S(2)}, u32[]{:S(2)}) collective-permute-start(bf16[2,128,512]{2,1,0:T(8,128)(2,1)} %get-tuple-element.20), channel_id=1, source_target_pairs={{0,1},{1,0},{2,3},{3,2},{4,5},{5,4},{6,7},{7,6},{8,9},{9,8},{10,11... | collective-permute-start | bytes 786440 | tf_op jit(solution)/shard_map/ppermute | solution.py:329
  37.6 7.7 %copy-start.4 = (bf16[2,128,512]{2,1,0:T(8,128)(2,1)S(1)}, bf16[2,128,512]{2,1,0:T(8,128)(2,1)}, u32[]{:S(2)}) copy-start(bf16[2,128,512]{2,1,0:T(8,128)(2,1)} %get-tuple-element.19.kept_ref) | copy-start | bytes 786436
  37.6 7.7 %copy-start.5 = (bf16[2,256,256]{2,1,0:T(8,128)(2,1)S(1)}, bf16[2,256,256]{2,1,0:T(8,128)(2,1)}, u32[]{:S(2)}) copy-start(bf16[2,256,256]{2,1,0:T(8,128)(2,1)} %get-tuple-element.21.held_ref) | copy-start | bytes 786436
  37.7 7.7 %collective-permute-start.5 = (bf16[2,256,256]{2,1,0:T(8,128)(2,1)}, bf16[2,256,256]{2,1,0:T(8,128)(2,1)S(1)}, u32[]{:S(2)}, u32[]{:S(2)}) collective-permute-start(bf16[2,256,256]{2,1,0:T(8,128)(2,1)} %get-tuple-element.22), channel_id=1, source_target_pairs={{0,8},{4,12},{8,0},{12,4},{16,24},{20,28},{24,16},{28,20},{1,9},{5... | collective-permute-start | bytes 786440 | tf_op jit(solution)/shard_map/ppermute | solution.py:329
  41.4 13.3 %all-to-all-start.2 = ((bf16[8,32,1024]{2,1,0:T(8,128)(2,1)}), bf16[8,32,1024]{2,1,0:T(8,128)(2,1)S(1)}, u32[]{:S(2)}, u32[]{:S(2)}) async-start(bf16[8,32,1024]{2,1,0:T(8,128)(2,1)} %backward_mix.1), calls=%async_computation.2 | async-start | bytes 1048576 | tf_op jit(solution)/shard_map/all_to_all | solution.py:337
  45.4 10.3 %collective-permute-start.6 = (bf16[128,512]{1,0:T(8,128)(2,1)S(1)}, bf16[128,512]{1,0:T(8,128)(2,1)S(1)}, u32[]{:S(2)}, u32[]{:S(2)}) collective-permute-start(bf16[128,512]{1,0:T(8,128)(2,1)S(1)} %get-tuple-element.23), channel_id=1, source_target_pairs={{0,2},{1,3},{2,0},{3,1},{4,6},{5,7},{6,4},{7,5},{8,10},{9,11},{10,... | collective-permute-start | bytes 393224 | tf_op jit(solution)/shard_map/ppermute | solution.py:329
  48.4 8.1 %collective-permute-start.7 = (bf16[256,256]{1,0:T(8,128)(2,1)S(1)}, bf16[256,256]{1,0:T(8,128)(2,1)S(1)}, u32[]{:S(2)}, u32[]{:S(2)}) collective-permute-start(bf16[256,256]{1,0:T(8,128)(2,1)S(1)} %get-tuple-element.24), channel_id=1, source_target_pairs={{0,16},{4,20},{8,24},{12,28},{16,0},{20,4},{24,8},{28,12},{1,17},{... | collective-permute-start | bytes 393224 | tf_op jit(solution)/shard_map/ppermute | solution.py:329

commit v3 on v2

--- a/solution.py
+++ b/solution.py
@@ -15,6 +15,8 @@
 NN = (((1,), (0,)), ((), ()))
 TAIL = 16
 LONG = 30_000_000_000
+RELAY = 5_000_000_000
+SUMS = 1_500_000_000
 
 
 def contract(matrix, operand, backward):
@@ -147,74 +149,105 @@
     return field
 
 
-def pack_kernel(pool_rows, tokens_ref, map_ref, out_ref):
-    owners = out_ref.shape[0]
+def pack_kernel(pool_rows, tokens_ref, map_ref, *refs):
+    outs, (held_ref, maps_ref, packed_ref, sems) = refs[:4], refs[4:]
     blocks, rows = map_ref.shape
-    feats = tokens_ref.shape[1] // owners
-    maps = lax.rem(map_ref[...], jnp.int32(pool_rows)).astype(F32).astype(BF16)
+    owners = packed_ref.shape[0]
+    feats = tokens_ref.shape[2] // owners
+    loads = [
+        pltpu.make_async_copy(tokens_ref.at[n], held_ref.at[n], sems.at[n]) for n in range(blocks)
+    ]
+    loads.append(pltpu.make_async_copy(map_ref, maps_ref, sems.at[blocks]))
+    for load in loads:
+        load.start()
+    loads[blocks].wait()
+    maps = lax.rem(maps_ref[...], jnp.int32(pool_rows)).astype(F32).astype(BF16)
     tail = jnp.concatenate([maps, jnp.zeros((TAIL - blocks, rows), BF16)], axis=0)
+    for g in range(owners):
+        packed_ref[g, blocks * feats :, :] = tail
     for n in range(blocks):
-        turned = tokens_ref[n * rows : (n + 1) * rows, :].T
+        loads[n].wait()
+        turned = held_ref[n].T
         for g in range(owners):
-            out_ref[g, n * feats : (n + 1) * feats, :] = turned[g * feats : (g + 1) * feats]
-    for g in range(owners):
-        out_ref[g, blocks * feats :, :] = tail
-
-
-def hot_of(packed_ref, g, blocks, pool_rows):
-    maps = packed_ref[g, packed_ref.shape[1] - TAIL :, :].astype(F32).astype(jnp.int32)
-    return jnp.concatenate([one_hot(maps[n : n + 1], pool_rows) for n in range(blocks)], axis=1)
-
-
-def forward_kernel(section_bits, blocks, mix_ref, packed_ref, out_ref, a_ref, b_ref):
-    owners, both, pool_rows = out_ref.shape
-    feats, rows = both // 2, a_ref.shape[2]
-    for g in range(owners):
+            packed_ref[g, n * feats : (n + 1) * feats, :] = turned[g * feats : (g + 1) * feats]
+    chip = lax.axis_index("tok") // 2
+    for o in range(4):
+        outs[o][...] = packed_ref[pl.ds((chip ^ o) * 2, 2)]
+
+
+def hot_of(maps, pool_rows):
+    maps = maps.astype(F32).astype(jnp.int32)
+    return jnp.concatenate(
+        [one_hot(maps[n : n + 1], pool_rows) for n in range(maps.shape[0])], axis=1
+    )
+
+
+def sources(pieces):
+    me = lax.axis_index("tok")
+    for k, piece in enumerate(pieces):
+        yield me ^ (2 * (k % 4) + k // 4), piece
+
+
+def forward_kernel(section_bits, blocks, mix_ref, *refs):
+    pieces, (out_ref, map_ref, a_ref, b_ref) = refs[:8], refs[8:]
+    owners, feats, pool_rows = out_ref.shape
+    rows = a_ref.shape[2]
+    core = lax.axis_index("tok") % 2
+    for g, piece in sources(pieces):
+        map_ref[g] = piece[core, blocks * feats :, :]
         for n in range(blocks):
-            a_ref[g * blocks + n] = packed_ref[g, n * feats : (n + 1) * feats, :]
+            a_ref[g * blocks + n] = piece[core, n * feats : (n + 1) * feats, :]
     done = run_sections(a_ref, b_ref, mix_ref, section_bits, False)
     ones = jnp.ones((16, blocks * rows), BF16)
     for g in range(owners):
         mine = jnp.concatenate([done[g * blocks + n] for n in range(blocks)], axis=1)
         sums = lax.dot_general(
             jnp.concatenate([mine, ones], axis=0),
-            hot_of(packed_ref, g, blocks, pool_rows),
+            hot_of(map_ref[g][:blocks], pool_rows),
             NT,
             preferred_element_type=F32,
         )
-        pooled = (sums[:feats] / sums[feats : feats + 1]).astype(BF16)
-        out_ref[g, :feats, :] = pooled
-        out_ref[g ^ 1, feats:, :] = pooled
-
-
-def backward_kernel(section_bits, blocks, mix_ref, d_ref, packed_ref, out_ref, a_ref, b_ref):
-    owners, feats, _ = out_ref.shape
-    pool_rows, rows = d_ref.shape[2], a_ref.shape[2]
+        out_ref[g] = (sums[:feats] / sums[feats : feats + 1]).astype(BF16)
+
+
+def backward_kernel(section_bits, blocks, mix_ref, map_ref, *refs):
+    pieces, outs, (a_ref, b_ref, d_ref) = refs[:8], refs[8:12], refs[12:]
+    owners, feats, pool_rows = d_ref.shape
+    rows = a_ref.shape[2]
+    me = lax.axis_index("tok")
+    for g, piece in sources(pieces):
+        d_ref[g] = piece[me % 2, :feats]
     for g in range(owners):
         spread = lax.dot_general(
-            d_ref[g, :feats], hot_of(packed_ref, g, blocks, pool_rows), NN, preferred_element_type=F32
+            d_ref[g], hot_of(map_ref[g][:blocks], pool_rows), NN, preferred_element_type=F32
         ).astype(BF16)
         for n in range(blocks):
             a_ref[g * blocks + n] = spread[:, n * rows : (n + 1) * rows]
     done = run_sections(a_ref, b_ref, mix_ref, section_bits, True)
-    for g in range(owners):
-        for n in range(blocks):
-            out_ref[g, :, n * rows : (n + 1) * rows] = done[g * blocks + n]
-
-
-def unpack_kernel(grad_ref, out_ref):
-    owners, _, toks = grad_ref.shape
-    for at in range(0, toks, 128):
-        turned = jnp.concatenate([grad_ref[g, :, at : at + 128] for g in range(owners)], axis=0)
-        out_ref[at : at + 128, :] = turned.T
-
-
-def early_kernel(order, w_ref, *refs):
-    *cots, out_ref = refs
-    outs_tp = cots[0].shape[1]
+    for o in range(4):
+        outs[o][...] = done[pl.ds((me // 2 ^ o) * 2 * blocks, 2 * blocks)]
+
+
+def unpack_kernel(*refs):
+    pieces, out_ref, all_ref = refs[:8], refs[8], refs[9]
+    blocks, feats, rows = pieces[0].shape[0] // 2, *pieces[0].shape[1:]
+    core = lax.axis_index("tok") % 2
+    for g, piece in sources(pieces):
+        at = pl.ds(pl.multiple_of(g * feats, feats), feats)
+        all_ref[:, at, :] = piece[pl.ds(core * blocks, blocks)]
+    for n in range(blocks):
+        out_ref[n * rows : (n + 1) * rows, :] = all_ref[n].T
+
+
+def relay_kernel(came_ref, *refs):
+    refs[-1][...] = came_ref[...]
+
+
+def early_kernel(w_ref, own_ref, came_ref, out_ref):
+    outs_tp = own_ref.shape[1]
     place = lax.axis_index("tp")
     total = None
-    for o, cot in zip(order, cots):
+    for o, cot in ((0, own_ref), (2, came_ref)):
         at = pl.multiple_of((place ^ o) * outs_tp, outs_tp)
         part = lax.dot_general(
             cot[...], w_ref[:, pl.ds(at, outs_tp)], NT, preferred_element_type=F32
@@ -223,16 +256,15 @@
     out_ref[...] = total
 
 
-def cotangent_kernel(groups, late, w_ref, map_ref, pooled_ref, early_ref, *refs):
-    cots, out_ref, send_ref = refs[:groups], refs[groups], refs[groups + 1]
-    owners, both, pool_rows = pooled_ref.shape
-    feats = both // 2
+def cotangent_kernel(w_ref, map_ref, pooled_ref, early_ref, *refs):
+    cots, outs_ref, (send_ref, turned_ref) = refs[:4], refs[4:8], refs[8:]
+    owners, feats, pool_rows = pooled_ref.shape
     outs_tp = cots[0].shape[1]
-    outs = send_ref.shape[1] // groups
-    place = lax.axis_index("tp")
-    other = pl.multiple_of((1 - lax.axis_index("tok") % 2) * outs, outs)
+    outs = send_ref.shape[1] // 4
+    place, me = lax.axis_index("tp"), lax.axis_index("tok")
+    other = pl.multiple_of((1 - me % 2) * outs, outs)
     total = early_ref[...]
-    for o in late:
+    for o in (1, 3):
         at = pl.multiple_of((place ^ o) * outs_tp, outs_tp)
         total = total + lax.dot_general(
             cots[o][...], w_ref[:, pl.ds(at, outs_tp)], NT, preferred_element_type=F32
@@ -245,16 +277,20 @@
         counts = counts + jnp.sum(hits, axis=1, keepdims=True)
     turned = (total / counts).T.astype(BF16)
     for g in range(owners):
-        out_ref[g, :feats, :] = turned[g * feats : (g + 1) * feats]
-        out_ref[g, feats:, :] = pooled_ref[g]
-    for o in range(groups):
+        turned_ref[g] = turned[g * feats : (g + 1) * feats]
+    for o in range(4):
+        for core in range(2):
+            g = (me // 2 ^ o) * 2 + core
+            outs_ref[o][core, :feats, :] = turned_ref[g]
+            outs_ref[o][core, feats:, :] = pooled_ref[g]
+    for o in range(4):
         send_ref[:, o * outs : (o + 1) * outs] = cots[o][:, pl.ds(other, outs)]
 
 
-def project_kernel(got_ref, w_ref, came_ref, *refs):
-    cots, (kept_ref, sent_ref, held_ref, gone_ref) = refs[:4], refs[4:8]
-    share_ref, part_ref, sems = refs[8:]
-    owners, feats = got_ref.shape[0], got_ref.shape[1] // 3
+def project_kernel(w_ref, came_ref, *refs):
+    cots, pieces, shares, (held_ref, gone_ref) = refs[:4], refs[4:12], refs[12:16], refs[16:18]
+    share_ref, part_ref, pool_ref, sems = refs[18:]
+    feats, pool_rows = pieces[0].shape[1] // 2, pieces[0].shape[2]
     outs_tp = cots[0].shape[1]
     outs = came_ref.shape[1] // 4
     place, me = lax.axis_index("tp"), lax.axis_index("tok")
@@ -265,19 +301,21 @@
         copies[-1].start()
 
     mine = pl.multiple_of((me % 2) * outs, outs)
-    turned = jnp.concatenate([got_ref[g, feats : 2 * feats, :] for g in range(owners)], axis=0)
-    others = jnp.concatenate([got_ref[g, 2 * feats :, :] for g in range(owners)], axis=0)
-    pooled = turned.T
-    turned = jnp.concatenate([turned, others], axis=1)
-    for o in (1, 3, 0, 2):
+    for g, piece in sources(pieces):
+        pool_ref[g, :, :pool_rows] = piece[me % 2, feats:, :]
+        pool_ref[g, :, pool_rows:] = piece[1 - me % 2, feats:, :]
+    turned = jnp.concatenate([pool_ref[g] for g in range(len(pieces))], axis=0)
+    pooled = turned[:, :pool_rows].T
+    for o in (3, 1, 2, 0):
         at = pl.multiple_of((place ^ o) * outs_tp, outs_tp)
         share_ref[o] = lax.dot_general(
             pooled, w_ref[:, pl.ds(at, outs_tp)], NN, preferred_element_type=F32
         ).astype(BF16)
-        send(share_ref.at[o], (sent_ref if o % 2 else kept_ref).at[o // 2])
+        send(share_ref.at[o], shares[o])
     for o in range(4):
+        own = cots[o][:, pl.ds(mine, outs)]
         cot = jnp.concatenate(
-            [cots[o][:, pl.ds(mine, outs)], came_ref[:, o * outs : (o + 1) * outs]], axis=0
+            [own, came_ref[:, o * outs : (o + 1) * outs]], axis=0
         )
         part_ref[place ^ o] = lax.dot_general(
             turned, cot, NN, preferred_element_type=F32
@@ -289,26 +327,29 @@
 
 
 def fold_kernel(kept_ref, got_ref, held_ref, came_ref, share_ref, part_ref):
-    share_ref[...] = (kept_ref[1].astype(F32) + got_ref[1].astype(F32)).astype(BF16)
+    share_ref[...] = (kept_ref[...].astype(F32) + got_ref[...].astype(F32)).astype(BF16)
     part_ref[...] = (held_ref[1].astype(F32) + came_ref[1].astype(F32)).astype(BF16)
 
 
 def sum_kernel(scale, kept_ref, got_ref, share_ref, held_ref, came_ref, part_ref, projected_ref, grad_ref):
-    total = kept_ref[0].astype(F32) + got_ref[0].astype(F32) + share_ref[...].astype(F32)
+    total = kept_ref[...].astype(F32) + got_ref[...].astype(F32) + share_ref[...].astype(F32)
     projected_ref[...] = total.astype(BF16)
     total = held_ref[0].astype(F32) + came_ref[0].astype(F32) + part_ref[...].astype(F32)
     grad_ref[...] = total.T * scale
 
 
-def call(kernel, operands, out_shape, scratch, name, cost=0, out_space=pltpu.VMEM):
+def call(kernel, operands, out_shape, scratch, name, cost=0, out_space=pltpu.VMEM, in_space=pltpu.VMEM):
     several = isinstance(out_shape, (list, tuple))
-    vmem = pl.BlockSpec(memory_space=pltpu.VMEM)
-    out = pl.BlockSpec(memory_space=out_space)
+    into = pl.BlockSpec(memory_space=in_space)
+    if in_space == pltpu.HBM:
+        operands = [pltpu.with_memory_space_constraint(a, pltpu.HBM) for a in operands]
+    spaces = out_space if isinstance(out_space, tuple) else (out_space,) * (len(out_shape) if several else 1)
+    out = [pl.BlockSpec(memory_space=space) for space in spaces]
     return pl.pallas_call(
         kernel,
         out_shape=out_shape,
-        in_specs=[vmem] * len(operands),
-        out_specs=[out] * len(out_shape) if several else out,
+        in_specs=[into] * len(operands),
+        out_specs=out if several else out[0],
         scratch_shapes=scratch,
         compiler_params=pltpu.CompilerParams(vmem_limit_bytes=VMEM_LIMIT),
         cost_estimate=pl.CostEstimate(flops=cost, bytes_accessed=0, transcendentals=0),
@@ -333,8 +374,9 @@
     return [pieces[0]] + [swap(piece, axis, o) for o, piece in enumerate(pieces) if o]
 
 
-def exchange(pieces, axis):
-    return lax.all_to_all(pieces, axis, split_axis=0, concat_axis=0, tiled=True)
+def exchange(pieces):
+    came = [pieces[0]] + [swap(pieces[o], "tok", 2 * o) for o in (1, 2, 3)]
+    return came + [swap(piece, "tok", 1) for piece in came]
 
 
 def shards(tokens, mix_weights, proj_weight, pool_map, out_cot):
@@ -351,82 +393,98 @@
     section_bits = [section_id % all_bits for section_id in range(section_count)]
     fields = [pltpu.VMEM((owners * blocks, feats, rows), BF16)] * 2
 
-    cots = [out_cot] + [swap(out_cot, "tp", o) for o in range(1, groups)]
+    across = swap(out_cot, "tp", 2)
+    beside = swap(out_cot, "tp", 1)
+    onward = call(relay_kernel, (across, beside), struct(pool_rows, outs_tp), [], "relay", RELAY)
+    cots = [out_cot, beside, across, swap(onward, "tp", 1)]
     maps = pool_map.reshape(blocks, rows)
+    height = blocks * feats + TAIL
     packed = call(
         functools.partial(pack_kernel, pool_rows),
-        (tokens, maps),
-        struct(owners, blocks * feats + TAIL, rows),
-        [],
+        (tokens.reshape(blocks, rows, feats_tp), maps),
+        [struct(2, height, rows)] * 4,
+        [
+            pltpu.VMEM((blocks, rows, feats_tp), BF16),
+            pltpu.VMEM((blocks, rows), jnp.int32),
+            pltpu.VMEM((owners, height, rows), BF16),
+            pltpu.SemaphoreType.DMA((blocks + 1,)),
+        ],
         "pack",
-    )
-    packed = exchange(packed, "tok")
-    order = [0] + list(range(2, groups))
+        in_space=pltpu.HBM,
+    )
+    packed = exchange(packed)
     early = call(
-        functools.partial(early_kernel, order),
-        (proj_weight, *[cots[o] for o in order]),
+        early_kernel,
+        (proj_weight, out_cot, across),
         struct(pool_rows, feats_tp, dtype=F32),
         [],
         "early_cotangent",
-        LONG,
-    )
-    packed, early = lax.optimization_barrier((packed, early))
-    pooled = call(
+    )
+    pooled, map_rows = call(
         functools.partial(forward_kernel, section_bits, blocks),
-        (mix_weights, packed),
-        struct(owners, 2 * feats, pool_rows),
+        (mix_weights, *packed),
+        [struct(owners, feats, pool_rows), struct(owners, TAIL, rows)],
         fields,
         "forward_mix",
     )
-    both, half = call(
-        functools.partial(cotangent_kernel, groups, [1]),
+    *both, half = call(
+        cotangent_kernel,
         (proj_weight, maps, pooled, early, *cots),
-        [struct(owners, 3 * feats, pool_rows), struct(pool_rows, groups * outs)],
-        [],
+        [struct(2, 2 * feats, pool_rows)] * 4 + [struct(pool_rows, groups * outs)],
+        [pltpu.VMEM((owners, feats, pool_rows), BF16)],
         "cotangent",
     )
     half = swap(half, "tok", 1)
-    both = exchange(both, "tok")
-
-    kept, sent, held, gone = call(
+    both = exchange(both)
+
+    *shares, held, gone = call(
         project_kernel,
-        (both, proj_weight, half, *cots),
-        [in_hbm(2, pool_rows, outs_tp)] * 2 + [in_hbm(2, feats_tp, outs)] * 2,
+        (proj_weight, half, *cots, *both),
+        [in_hbm(pool_rows, outs_tp)] * 4 + [in_hbm(2, feats_tp, outs)] * 2,
         [
             pltpu.VMEM((4, pool_rows, outs_tp), BF16),
             pltpu.VMEM((4, feats_tp, outs), BF16),
+            pltpu.VMEM((owners, feats, 2 * pool_rows), BF16),
             pltpu.SemaphoreType.DMA((8,)),
         ],
         "project",
         out_space=pltpu.HBM,
     )
-    sent, gone = swap(sent, "tp", 1), swap(gone, "tok", 2)
+    gone = swap(gone, "tok", 2)
     share, part = call(
         fold_kernel,
-        (kept, sent, held, gone),
+        (shares[2], swap(shares[3], "tp", 1), held, gone),
         [struct(pool_rows, outs_tp), struct(feats_tp, outs)],
         [],
         "fold",
         LONG,
     )
-    share, part = swap(share, "tp", 2), swap(part, "tok", 4)
+    kept, sent, share = shares[0], swap(shares[1], "tp", 1), swap(share, "tp", 2)
+    part = swap(part, "tok", 4)
     projected, proj_grad = call(
         functools.partial(sum_kernel, 1.0 / math.sqrt(pool_rows * owners)),
         (kept, sent, share, held, gone, part),
         [struct(pool_rows, outs_tp), struct(outs, feats_tp, dtype=F32)],
         [],
         "sums",
+        SUMS,
     )
 
     grad = call(
         functools.partial(backward_kernel, section_bits, blocks),
-        (mix_weights, both, packed),
-        struct(owners, feats, toks),
-        fields,
+        (mix_weights, map_rows, *both),
+        [struct(2 * blocks, feats, rows)] * 4,
+        fields + [pltpu.VMEM((owners, feats, pool_rows), BF16)],
         "backward_mix",
     )
-    grad = exchange(grad, "tok")
-    token_grad = call(unpack_kernel, (grad,), struct(toks, feats_tp), [], "unpack")
+    grad, projected = lax.optimization_barrier((exchange(grad), projected))
+    token_grad = call(
+        unpack_kernel,
+        grad,
+        struct(toks, feats_tp),
+        [pltpu.VMEM((blocks, feats_tp, rows), BF16)],
+        "unpack",
+    )
     return (projected, token_grad, proj_grad)
 
 

time: 57.8 us -> 53.1 us (0.919)
  blocking collectives: 8.63 us -> 0 us
  starting transfers between devices: 19.6 us -> 24.2 us
  local copies, waits for them, and re-layouts: 2.4 us -> 0.23 us
  waiting for transfers between devices: 15 us -> 16.8 us
    ppermute x8 -> x30, starting transfers between devices: 12.2 us -> 24.2 us  [swap(): return lax.ppermute(piece, axis, [(i, i ^ offset) for i in range(size)])]
    ppermute x8 -> x30, waiting for transfers between devices: 5.26 us -> 16.8 us  [swap(): return lax.ppermute(piece, axis, [(i, i ^ offset) for i in range(size)])]
    all_to_all x2 -> x0, waiting for transfers between devices: 9.75 us -> none  [exchange(): return lax.all_to_all(pieces, axis, split_axis=0, concat_axis=0, tiled=True)]
    all_to_all x1 -> x0, blocking collectives: 8.63 us -> none  [exchange(): return lax.all_to_all(pieces, axis, split_axis=0, concat_axis=0, tiled=True)]
    all_to_all x2 -> x0, starting transfers between devices: 7.36 us -> none  [exchange(): return lax.all_to_all(pieces, axis, split_axis=0, concat_axis=0, tiled=True)]
    unnamed x20 -> x16, local copies, waits for them, and re-layouts: 2.4 us -> 0.23 us
    pallas_call x9 -> x10, Pallas kernels: 11 us -> 11 us  [call(): pl.pallas_call(kernel, out_shape=out_shape, in_specs=[into] * len(operand...]
  transfers between devices with their start and end apart: 10 -> 30, of which waited for: 5 -> 11; matrix products, arithmetic and copies ran while one was open for 0% -> 0% of each run, Pallas kernels for 15% -> 12%
where the time goes in v3:
time: 53.1 us; the launch traced here: 53 us
  starting transfers between devices  24.2 us (46%)
  waiting for transfers between devices  16.8 us (32%)
  Pallas kernels  11 us (21%)
  between operations  0.82 us (2%)
    ppermute x30, starting transfers between devices, swap(): return lax.ppermute(piece, axis, [(i, i ^ offset) for i in range(size)])  24.2 us
    ppermute x30, waiting for transfers between devices, swap(): return lax.ppermute(piece, axis, [(i, i ^ offset) for i in range(size)])  16.8 us
    pallas_call x10, Pallas kernels, call(): pl.pallas_call(kernel, out_shape=out_shape, in_specs=[into] * len(operand...  11 us
  transfers between devices with their start and end apart: 30, of which 11 were waited for; matrix products, arithmetic and copies ran while one was open for 0% of the time, Pallas kernels for 12%

profile of v3, /device:TPU:0, one launch (start us, length us, event | category | flops | bytes accessed | tf_op | source)
XLA Modules:
  0.0 53.0 jit_solution(3778572880022165622)
XLA Ops:
  0.6 1.6 %pack.1 = (bf16[2,272,128]{2,1,0:T(8,128)(2,1)S(1)}, bf16[2,272,128]{2,1,0:T(8,128)(2,1)S(1)}, bf16[2,272,128]{2,1,0:T(8,128)(2,1)S(1)}, bf16[2,272,128]{2,1,0:T(8,128)(2,1)S(1)}) custom-call(bf16[8,128,256]{2,1,0:T(8,128)(2,1)} %bitcast.4, s32[8,128]{1,0:T(8,128)} %bitcast.2), custom_call_target="tpu_custom_call" | custom-call | tf_op jit(solution)/shard_map/pack/pallas_call | solution.py:348
  2.3 3.0 %collective-permute-start = (bf16[2,272,128]{2,1,0:T(8,128)(2,1)S(1)}, bf16[2,272,128]{2,1,0:T(8,128)(2,1)S(1)}, u32[]{:S(2)}, u32[]{:S(2)}) collective-permute-start(bf16[2,272,128]{2,1,0:T(8,128)(2,1)S(1)} %get-tuple-element.38), channel_id=1, source_target_pairs={{0,8},{4,12},{8,0},{12,4},{16,24},{20,28},{24,16},{28,20},{1,9},{5... | collective-permute-start | bytes 417800 | tf_op jit(solution)/shard_map/ppermute | solution.py:370
  5.3 1.5 %collective-permute-start.1 = (bf16[2,272,128]{2,1,0:T(8,128)(2,1)S(1)}, bf16[2,272,128]{2,1,0:T(8,128)(2,1)S(1)}, u32[]{:S(2)}, u32[]{:S(2)}) collective-permute-start(bf16[2,272,128]{2,1,0:T(8,128)(2,1)S(1)} %get-tuple-element.39), channel_id=1, source_target_pairs={{0,16},{4,20},{8,24},{12,28},{16,0},{20,4},{24,8},{28,12},{1,17},{... | collective-permute-start | bytes 417800 | tf_op jit(solution)/shard_map/ppermute | solution.py:370
  6.8 0.0 collective-permute-start.2
  6.8 3.0 %collective-permute-start.7 = (bf16[128,512]{1,0:T(8,128)(2,1)}, bf16[128,512]{1,0:T(8,128)(2,1)S(1)}, u32[]{:S(2)}, u32[]{:S(2)}) collective-permute-start(bf16[128,512]{1,0:T(8,128)(2,1)} %refs_0_.3), channel_id=1, source_target_pairs={{0,2},{1,3},{2,0},{3,1},{4,6},{5,7},{6,4},{7,5},{8,10},{9,11},{10,... | collective-permute-start | bytes 393224 | tf_op jit(solution)/shard_map/ppermute | solution.py:370
  9.9 1.6 %collective-permute-start.8 = (bf16[128,512]{1,0:T(8,128)(2,1)}, bf16[128,512]{1,0:T(8,128)(2,1)S(1)}, u32[]{:S(2)}, u32[]{:S(2)}) collective-permute-start(bf16[128,512]{1,0:T(8,128)(2,1)} %refs_0_.3), channel_id=1, source_target_pairs={{0,1},{1,0},{2,3},{3,2},{4,5},{5,4},{6,7},{7,6},{8,9},{9,8},{10,11... | collective-permute-start | bytes 393224 | tf_op jit(solution)/shard_map/ppermute | solution.py:370
  11.4 4.2 %collective-permute-done.7.came_ref.refs_2_ = bf16[128,512]{1,0:T(8,128)(2,1)S(1)} collective-permute-done((bf16[128,512]{1,0:T(8,128)(2,1)}, bf16[128,512]{1,0:T(8,128)(2,1)S(1)}, u32[]{:S(2)}, u32[]{:S(2)}) %collective-permute-start.7) | collective-permute-done | bytes 131104 | tf_op jit(solution)/shard_map/ppermute | solution.py:370
  15.7 0.5 collective-permute-start.4
  16.2 0.1 collective-permute-start.5
  16.3 0.4 collective-permute-start.6
  16.7 0.0 copy-start.1
  16.7 0.8 %collective-permute-start.9 = (bf16[128,512]{1,0:T(8,128)(2,1)S(1)}, bf16[128,512]{1,0:T(8,128)(2,1)S(1)}, u32[]{:S(2)}, u32[]{:S(2)}) collective-permute-start(bf16[128,512]{1,0:T(8,128)(2,1)S(1)} %relay.1), channel_id=1, source_target_pairs={{0,1},{1,0},{2,3},{3,2},{4,5},{5,4},{6,7},{7,6},{8,9},{9,8},{10,11... | collective-permute-start | bytes 393224 | tf_op jit(solution)/shard_map/ppermute | solution.py:370
  17.5 0.3 early_cotangent.1.early_ref
  17.8 0.0 copy-start.3
  17.8 0.0 collective-permute-done.3.refs_4_
  17.9 0.2 copy-done.1
  18.1 2.8 %forward_mix.1 = (bf16[8,32,128]{2,1,0:T(8,128)(2,1)S(1)}, bf16[8,16,128]{2,1,0:T(8,128)(2,1)S(1)}) custom-call(bf16[10,2,2,128,128]{4,3,2,1,0:T(8,128)(2,1)S(1)} %copy-done.1, bf16[2,272,128]{2,1,0:T(8,128)(2,1)S(1)} %get-tuple-element.37.refs_0_, bf16[2,272,128]{2,1,0:T(8,128)(2,1)S(1)} %collective-permute-done.refs_1_, ...), custom_call_target="tpu_custom_call" | custom-call | tf_op jit(solution)/shard_map/forward_mix/pallas_call | solution.py:348
  20.9 1.4 %collective-permute-done.9.refs_3_ = bf16[128,512]{1,0:T(8,128)(2,1)S(1)} collective-permute-done((bf16[128,512]{1,0:T(8,128)(2,1)S(1)}, bf16[128,512]{1,0:T(8,128)(2,1)S(1)}, u32[]{:S(2)}, u32[]{:S(2)}) %collective-permute-start.9) | collective-permute-done | bytes 131104 | tf_op jit(solution)/shard_map/ppermute | solution.py:370
  22.3 0.4 cotangent.1
  22.7 0.1 collective-permute-start.24
  22.7 1.6 %collective-permute-start.10 = (bf16[2,64,128]{2,1,0:T(8,128)(2,1)S(1)}, bf16[2,64,128]{2,1,0:T(8,128)(2,1)S(1)}, u32[]{:S(2)}, u32[]{:S(2)}) collective-permute-start(bf16[2,64,128]{2,1,0:T(8,128)(2,1)S(1)} %get-tuple-element.44), channel_id=1, source_target_pairs={{0,8},{4,12},{8,0},{12,4},{16,24},{20,28},{24,16},{28,20},{1,9},{5... | collective-permute-start | bytes 98312 | tf_op jit(solution)/shard_map/ppermute | solution.py:370
  24.3 1.5 %collective-permute-start.11 = (bf16[2,64,128]{2,1,0:T(8,128)(2,1)S(1)}, bf16[2,64,128]{2,1,0:T(8,128)(2,1)S(1)}, u32[]{:S(2)}, u32[]{:S(2)}) collective-permute-start(bf16[2,64,128]{2,1,0:T(8,128)(2,1)S(1)} %get-tuple-element.45), channel_id=1, source_target_pairs={{0,16},{4,20},{8,24},{12,28},{16,0},{20,4},{24,8},{28,12},{1,17},{... | collective-permute-start | bytes 98312 | tf_op jit(solution)/shard_map/ppermute | solution.py:370
  25.9 0.4 collective-permute-start.12
  26.3 0.4 collective-permute-done.10.refs_1_.refs_5_
  26.7 0.1 collective-permute-start.14
  26.8 1.5 %collective-permute-done.11.refs_2_.refs_6_ = bf16[2,64,128]{2,1,0:T(8,128)(2,1)S(1)} collective-permute-done((bf16[2,64,128]{2,1,0:T(8,128)(2,1)S(1)}, bf16[2,64,128]{2,1,0:T(8,128)(2,1)S(1)}, u32[]{:S(2)}, u32[]{:S(2)}) %collective-permute-start.11) | collective-permute-done | bytes 32800 | tf_op jit(solution)/shard_map/ppermute | solution.py:370
  28.3 2.4 %collective-permute-done.12.refs_3_.refs_7_ = bf16[2,64,128]{2,1,0:T(8,128)(2,1)S(1)} collective-permute-done((bf16[2,64,128]{2,1,0:T(8,128)(2,1)S(1)}, bf16[2,64,128]{2,1,0:T(8,128)(2,1)S(1)}, u32[]{:S(2)}, u32[]{:S(2)}) %collective-permute-start.12) | collective-permute-done | bytes 32800 | tf_op jit(solution)/shard_map/ppermute | solution.py:370
  30.7 1.2 %collective-permute-done.16.refs_7_.refs_11_ = bf16[2,64,128]{2,1,0:T(8,128)(2,1)S(1)} collective-permute-done((bf16[2,64,128]{2,1,0:T(8,128)(2,1)S(1)}, bf16[2,64,128]{2,1,0:T(8,128)(2,1)S(1)}, u32[]{:S(2)}, u32[]{:S(2)}) %collective-permute-start.16) | collective-permute-done | bytes 32800 | tf_op jit(solution)/shard_map/ppermute | solution.py:370
  31.9 1.4 %project.1 = (bf16[128,512]{1,0:T(8,128)(2,1)}, bf16[128,512]{1,0:T(8,128)(2,1)}, bf16[128,512]{1,0:T(8,128)(2,1)}, bf16[128,512]{1,0:T(8,128)(2,1)}, bf16[2,256...) custom-call(bf16[256,2048]{1,0:T(8,128)(2,1)S(1)} %copy-done, bf16[128,1024]{1,0:T(8,128)(2,1)S(1)} %collective-permute-done.24.came_ref, ...), custom_call_target="tpu_custom_call" | custom-call | tf_op jit(solution)/shard_map/project/pallas_call | solution.py:348
  33.3 0.0 copy-start.4
  33.3 0.6 %collective-permute-start.27 = (bf16[2,256,256]{2,1,0:T(8,128)(2,1)}, bf16[2,256,256]{2,1,0:T(8,128)(2,1)S(1)}, u32[]{:S(2)}, u32[]{:S(2)}) collective-permute-start(bf16[2,256,256]{2,1,0:T(8,128)(2,1)} %get-tuple-element.57), channel_id=1, source_target_pairs={{0,8},{4,12},{8,0},{12,4},{16,24},{20,28},{24,16},{28,20},{1,9},{5... | collective-permute-start | bytes 786440 | tf_op jit(solution)/shard_map/ppermute | solution.py:370
  33.9 0.7 %collective-permute-start.26 = (bf16[128,512]{1,0:T(8,128)(2,1)}, bf16[128,512]{1,0:T(8,128)(2,1)S(1)}, u32[]{:S(2)}, u32[]{:S(2)}) collective-permute-start(bf16[128,512]{1,0:T(8,128)(2,1)} %get-tuple-element.55), channel_id=1, source_target_pairs={{0,1},{1,0},{2,3},{3,2},{4,5},{5,4},{6,7},{7,6},{8,9},{9,8},{10,11... | collective-permute-start | bytes 393224 | tf_op jit(solution)/shard_map/ppermute | solution.py:370
  34.6 2.4 %backward_mix.1 = (bf16[16,32,128]{2,1,0:T(8,128)(2,1)S(1)}, bf16[16,32,128]{2,1,0:T(8,128)(2,1)S(1)}, bf16[16,32,128]{2,1,0:T(8,128)(2,1)S(1)}, bf16[16,32,128]{2,1,0:T(8,128)(2,1)S(1)}) custom-call(bf16[10,2,2,128,128]{4,3,2,1,0:T(8,128)(2,1)S(1)} %copy-done.1, bf16[8,16,128]{2,1,0:T(8,128)(2,1)S(1)} %get-tuple-element.41.map_ref, ...), custom_call_target="tpu_custom_call" | custom-call | tf_op jit(solution)/shard_map/backward_mix/pallas_call | solution.py:348
  37.0 1.6 %collective-permute-start.17 = (bf16[16,32,128]{2,1,0:T(8,128)(2,1)S(1)}, bf16[16,32,128]{2,1,0:T(8,128)(2,1)S(1)}, u32[]{:S(2)}, u32[]{:S(2)}) collective-permute-start(bf16[16,32,128]{2,1,0:T(8,128)(2,1)S(1)} %get-tuple-element.48), channel_id=1, source_target_pairs={{0,8},{4,12},{8,0},{12,4},{16,24},{20,28},{24,16},{28,20},{1,9},{5... | collective-permute-start | bytes 393224 | tf_op jit(solution)/shard_map/ppermute | solution.py:370
  38.6 0.5 collective-permute-start.18
  39.1 1.5 %collective-permute-start.19 = (bf16[16,32,128]{2,1,0:T(8,128)(2,1)S(1)}, bf16[16,32,128]{2,1,0:T(8,128)(2,1)S(1)}, u32[]{:S(2)}, u32[]{:S(2)}) collective-permute-start(bf16[16,32,128]{2,1,0:T(8,128)(2,1)S(1)} %get-tuple-element.50), channel_id=1, source_target_pairs={{0,24},{4,28},{8,16},{12,20},{16,8},{20,12},{24,0},{28,4},{1,25},{... | collective-permute-start | bytes 393224 | tf_op jit(solution)/shard_map/ppermute | solution.py:370
  40.6 1.4 %collective-permute-start.25 = (bf16[128,512]{1,0:T(8,128)(2,1)S(1)}, bf16[128,512]{1,0:T(8,128)(2,1)S(1)}, u32[]{:S(2)}, u32[]{:S(2)}) collective-permute-start(bf16[128,512]{1,0:T(8,128)(2,1)S(1)} %copy-done.7), channel_id=1, source_target_pairs={{0,1},{1,0},{2,3},{3,2},{4,5},{5,4},{6,7},{7,6},{8,9},{9,8},{10,11... | collective-permute-start | bytes 393224 | tf_op jit(solution)/shard_map/ppermute | solution.py:370
  41.9 0.8 %collective-permute-done.27.came_ref = bf16[2,256,256]{2,1,0:T(8,128)(2,1)S(1)} collective-permute-done((bf16[2,256,256]{2,1,0:T(8,128)(2,1)}, bf16[2,256,256]{2,1,0:T(8,128)(2,1)S(1)}, u32[]{:S(2)}, u32[]{:S(2)}) %collective-permute-start.27) | collective-permute-done | bytes 262176 | tf_op jit(solution)/shard_map/ppermute | solution.py:370
  42.7 0.1 fold.1
  42.8 2.3 %collective-permute-start.28 = (bf16[128,512]{1,0:T(8,128)(2,1)S(1)}, bf16[128,512]{1,0:T(8,128)(2,1)S(1)}, u32[]{:S(2)}, u32[]{:S(2)}) collective-permute-start(bf16[128,512]{1,0:T(8,128)(2,1)S(1)} %get-tuple-element.58), channel_id=1, source_target_pairs={{0,2},{1,3},{2,0},{3,1},{4,6},{5,7},{6,4},{7,5},{8,10},{9,11},{10,... | collective-permute-start | bytes 393224 | tf_op jit(solution)/shard_map/ppermute | solution.py:370
  45.1 0.5 collective-permute-done.17.refs_1_
  45.5 0.5 collective-permute-start.29
  46.0 1.6 %collective-permute-done.19.refs_3_ = bf16[16,32,128]{2,1,0:T(8,128)(2,1)S(1)} collective-permute-done((bf16[16,32,128]{2,1,0:T(8,128)(2,1)S(1)}, bf16[16,32,128]{2,1,0:T(8,128)(2,1)S(1)}, u32[]{:S(2)}, u32[]{:S(2)}) %collective-permute-start.19) | collective-permute-done | bytes 131104 | tf_op jit(solution)/shard_map/ppermute | solution.py:370
  47.6 0.5 collective-permute-start.22
  48.1 2.5 %collective-permute-done.28.share_ref = bf16[128,512]{1,0:T(8,128)(2,1)S(1)} collective-permute-done((bf16[128,512]{1,0:T(8,128)(2,1)S(1)}, bf16[128,512]{1,0:T(8,128)(2,1)S(1)}, u32[]{:S(2)}, u32[]{:S(2)}) %collective-permute-start.28) | collective-permute-done | bytes 131104 | tf_op jit(solution)/shard_map/ppermute | solution.py:370
  50.6 0.9 %sums.1 = (bf16[128,512]{1,0:T(8,128)(2,1)}, f32[256,256]{1,0:T(8,128)}) custom-call(bf16[128,512]{1,0:T(8,128)(2,1)S(1)} %copy-done.5, bf16[128,512]{1,0:T(8,128)(2,1)S(1)} %collective-permute-done.25.got_ref, bf16[128,512]{1,0:T(8,128)(2,1)S(1)} %collective-permute-done.28.share_ref, bf16[2,256,256]{2,1,0:T(8,128)(2,1)S(1)} %copy-done.4, ...), custom_call_target="tpu_custom_call" | custom-call | flops 1500000000 | tf_op jit(solution)/shard_map/sums/pallas_call | solution.py:348
  51.5 0.4 collective-permute-done.23.refs_7_
  51.9 1.0 %unpack.1 = bf16[1024,256]{1,0:T(8,128)(2,1)} custom-call(bf16[16,32,128]{2,1,0:T(8,128)(2,1)S(1)} %get-tuple-element.62.refs_0_, bf16[16,32,128]{2,1,0:T(8,128)(2,1)S(1)} %collective-permute-done.17.refs_1_, bf16[16,32,128]{2,1,0:T(8,128)(2,1)S(1)} %collective-permute-done.18.refs_2_, bf16[16,32,128]{2,1,0:T(8,128)(2,1)S(1)} %collective-permute-done.19.refs_3_, ...), custom_call_target="tpu_custom_call" | custom-call | tf_op jit(solution)/shard_map/unpack/pallas_call | solution.py:348
  (38 shorter events, 0.1 us)
Async XLA Ops:
  2.3 13.4 %collective-permute-start = (bf16[2,272,128]{2,1,0:T(8,128)(2,1)S(1)}, bf16[2,272,128]{2,1,0:T(8,128)(2,1)S(1)}, u32[]{:S(2)}, u32[]{:S(2)}) collective-permute-start(bf16[2,272,128]{2,1,0:T(8,128)(2,1)S(1)} %get-tuple-element.38), channel_id=1, source_target_pairs={{0,8},{4,12},{8,0},{12,4},{16,24},{20,28},{24,16},{28,20},{1,9},{5... | collective-permute-start | bytes 417800 | tf_op jit(solution)/shard_map/ppermute | solution.py:370
  5.3 10.9 %collective-permute-start.1 = (bf16[2,272,128]{2,1,0:T(8,128)(2,1)S(1)}, bf16[2,272,128]{2,1,0:T(8,128)(2,1)S(1)}, u32[]{:S(2)}, u32[]{:S(2)}) collective-permute-start(bf16[2,272,128]{2,1,0:T(8,128)(2,1)S(1)} %get-tuple-element.39), channel_id=1, source_target_pairs={{0,16},{4,20},{8,24},{12,28},{16,0},{20,4},{24,8},{28,12},{1,17},{... | collective-permute-start | bytes 417800 | tf_op jit(solution)/shard_map/ppermute | solution.py:370
  6.8 9.4 %collective-permute-start.2 = (bf16[2,272,128]{2,1,0:T(8,128)(2,1)S(1)}, bf16[2,272,128]{2,1,0:T(8,128)(2,1)S(1)}, u32[]{:S(2)}, u32[]{:S(2)}) collective-permute-start(bf16[2,272,128]{2,1,0:T(8,128)(2,1)S(1)} %get-tuple-element.40), channel_id=1, source_target_pairs={{0,24},{4,28},{8,16},{12,20},{16,8},{20,12},{24,0},{28,4},{1,25},{... | collective-permute-start | bytes 417800 | tf_op jit(solution)/shard_map/ppermute | solution.py:370
  6.8 8.8 %collective-permute-start.7 = (bf16[128,512]{1,0:T(8,128)(2,1)}, bf16[128,512]{1,0:T(8,128)(2,1)S(1)}, u32[]{:S(2)}, u32[]{:S(2)}) collective-permute-start(bf16[128,512]{1,0:T(8,128)(2,1)} %refs_0_.3), channel_id=1, source_target_pairs={{0,2},{1,3},{2,0},{3,1},{4,6},{5,7},{6,4},{7,5},{8,10},{9,11},{10,... | collective-permute-start | bytes 393224 | tf_op jit(solution)/shard_map/ppermute | solution.py:370
  9.9 6.8 %collective-permute-start.8 = (bf16[128,512]{1,0:T(8,128)(2,1)}, bf16[128,512]{1,0:T(8,128)(2,1)S(1)}, u32[]{:S(2)}, u32[]{:S(2)}) collective-permute-start(bf16[128,512]{1,0:T(8,128)(2,1)} %refs_0_.3), channel_id=1, source_target_pairs={{0,1},{1,0},{2,3},{3,2},{4,5},{5,4},{6,7},{7,6},{8,9},{9,8},{10,11... | collective-permute-start | bytes 393224 | tf_op jit(solution)/shard_map/ppermute | solution.py:370
  15.7 1.9 %copy-start = (bf16[256,2048]{1,0:T(8,128)(2,1)S(1)}, bf16[256,2048]{1,0:T(8,128)(2,1)}, u32[]{:S(2)}) copy-start(bf16[256,2048]{1,0:T(8,128)(2,1)} %w_ref.5) | copy-start | bytes 3145732
  15.7 1.9 %copy-start.2 = (bf16[128,512]{1,0:T(8,128)(2,1)S(1)}, bf16[128,512]{1,0:T(8,128)(2,1)}, u32[]{:S(2)}) copy-start(bf16[128,512]{1,0:T(8,128)(2,1)} %refs_0_.3) | copy-start | bytes 393220
  15.7 2.2 %collective-permute-start.3 = (bf16[2,272,128]{2,1,0:T(8,128)(2,1)S(1)}, bf16[2,272,128]{2,1,0:T(8,128)(2,1)S(1)}, u32[]{:S(2)}, u32[]{:S(2)}) collective-permute-start(bf16[2,272,128]{2,1,0:T(8,128)(2,1)S(1)} %get-tuple-element.37.refs_0_), channel_id=1, source_target_pairs={{0,4},{4,0},{8,12},{12,8},{16,20},{20,16},{24,28},{28,24},{1,5},{5... | collective-permute-start | bytes 417800 | tf_op jit(solution)/shard_map/ppermute | solution.py:370
  15.7 2.2 %collective-permute-start.4 = (bf16[2,272,128]{2,1,0:T(8,128)(2,1)S(1)}, bf16[2,272,128]{2,1,0:T(8,128)(2,1)S(1)}, u32[]{:S(2)}, u32[]{:S(2)}) collective-permute-start(bf16[2,272,128]{2,1,0:T(8,128)(2,1)S(1)} %collective-permute-done.refs_1_), channel_id=1, source_target_pairs={{0,4},{4,0},{8,12},{12,8},{16,20},{20,16},{24,28},{28,24},{1,5},{5... | collective-permute-start | bytes 417800 | tf_op jit(solution)/shard_map/ppermute | solution.py:370
  16.2 1.7 %collective-permute-start.5 = (bf16[2,272,128]{2,1,0:T(8,128)(2,1)S(1)}, bf16[2,272,128]{2,1,0:T(8,128)(2,1)S(1)}, u32[]{:S(2)}, u32[]{:S(2)}) collective-permute-start(bf16[2,272,128]{2,1,0:T(8,128)(2,1)S(1)} %collective-permute-done.1.refs_2_), channel_id=1, source_target_pairs={{0,4},{4,0},{8,12},{12,8},{16,20},{20,16},{24,28},{28,24},{1,5},{5... | collective-permute-start | bytes 417800 | tf_op jit(solution)/shard_map/ppermute | solution.py:370
  16.3 1.6 %collective-permute-start.6 = (bf16[2,272,128]{2,1,0:T(8,128)(2,1)S(1)}, bf16[2,272,128]{2,1,0:T(8,128)(2,1)S(1)}, u32[]{:S(2)}, u32[]{:S(2)}) collective-permute-start(bf16[2,272,128]{2,1,0:T(8,128)(2,1)S(1)} %collective-permute-done.2.refs_3_), channel_id=1, source_target_pairs={{0,4},{4,0},{8,12},{12,8},{16,20},{20,16},{24,28},{28,24},{1,5},{5... | collective-permute-start | bytes 417800 | tf_op jit(solution)/shard_map/ppermute | solution.py:370
  16.7 1.4 %copy-start.1 = (bf16[10,2,2,128,128]{4,3,2,1,0:T(8,128)(2,1)S(1)}, bf16[10,2,2,128,128]{4,3,2,1,0:T(8,128)(2,1)}, u32[]{:S(2)}) copy-start(bf16[10,2,2,128,128]{4,3,2,1,0:T(8,128)(2,1)} %mix_ref.3) | copy-start | bytes 3932164
  16.7 5.5 %collective-permute-start.9 = (bf16[128,512]{1,0:T(8,128)(2,1)S(1)}, bf16[128,512]{1,0:T(8,128)(2,1)S(1)}, u32[]{:S(2)}, u32[]{:S(2)}) collective-permute-start(bf16[128,512]{1,0:T(8,128)(2,1)S(1)} %relay.1), channel_id=1, source_target_pairs={{0,1},{1,0},{2,3},{3,2},{4,5},{5,4},{6,7},{7,6},{8,9},{9,8},{10,11... | collective-permute-start | bytes 393224 | tf_op jit(solution)/shard_map/ppermute | solution.py:370
  17.8 4.4 %copy-start.3 = (s32[1024]{0:T(1024)S(1)}, s32[1024]{0:T(1024)}, u32[]{:S(2)}) copy-start(s32[1024]{0:T(1024)} %param.8) | copy-start | bytes 12292
  22.7 9.2 %collective-permute-start.24 = (bf16[128,1024]{1,0:T(8,128)(2,1)S(1)}, bf16[128,1024]{1,0:T(8,128)(2,1)S(1)}, u32[]{:S(2)}, u32[]{:S(2)}) collective-permute-start(bf16[128,1024]{1,0:T(8,128)(2,1)S(1)} %get-tuple-element.51), channel_id=1, source_target_pairs={{0,4},{4,0},{8,12},{12,8},{16,20},{20,16},{24,28},{28,24},{1,5},{5... | collective-permute-start | bytes 786440 | tf_op jit(solution)/shard_map/ppermute | solution.py:370
  22.7 4.0 %collective-permute-start.10 = (bf16[2,64,128]{2,1,0:T(8,128)(2,1)S(1)}, bf16[2,64,128]{2,1,0:T(8,128)(2,1)S(1)}, u32[]{:S(2)}, u32[]{:S(2)}) collective-permute-start(bf16[2,64,128]{2,1,0:T(8,128)(2,1)S(1)} %get-tuple-element.44), channel_id=1, source_target_pairs={{0,8},{4,12},{8,0},{12,4},{16,24},{20,28},{24,16},{28,20},{1,9},{5... | collective-permute-start | bytes 98312 | tf_op jit(solution)/shard_map/ppermute | solution.py:370
  24.3 3.9 %collective-permute-start.11 = (bf16[2,64,128]{2,1,0:T(8,128)(2,1)S(1)}, bf16[2,64,128]{2,1,0:T(8,128)(2,1)S(1)}, u32[]{:S(2)}, u32[]{:S(2)}) collective-permute-start(bf16[2,64,128]{2,1,0:T(8,128)(2,1)S(1)} %get-tuple-element.45), channel_id=1, source_target_pairs={{0,16},{4,20},{8,24},{12,28},{16,0},{20,4},{24,8},{28,12},{1,17},{... | collective-permute-start | bytes 98312 | tf_op jit(solution)/shard_map/ppermute | solution.py:370
  25.9 4.8 %collective-permute-start.12 = (bf16[2,64,128]{2,1,0:T(8,128)(2,1)S(1)}, bf16[2,64,128]{2,1,0:T(8,128)(2,1)S(1)}, u32[]{:S(2)}, u32[]{:S(2)}) collective-permute-start(bf16[2,64,128]{2,1,0:T(8,128)(2,1)S(1)} %get-tuple-element.46), channel_id=1, source_target_pairs={{0,24},{4,28},{8,16},{12,20},{16,8},{20,12},{24,0},{28,4},{1,25},{... | collective-permute-start | bytes 98312 | tf_op jit(solution)/shard_map/ppermute | solution.py:370
  26.3 4.4 %collective-permute-start.13 = (bf16[2,64,128]{2,1,0:T(8,128)(2,1)S(1)}, bf16[2,64,128]{2,1,0:T(8,128)(2,1)S(1)}, u32[]{:S(2)}, u32[]{:S(2)}) collective-permute-start(bf16[2,64,128]{2,1,0:T(8,128)(2,1)S(1)} %get-tuple-element.43.refs_0_.refs_4_), channel_id=1, source_target_pairs={{0,4},{4,0},{8,12},{12,8},{16,20},{20,16},{24,28},{28,24},{1,5},{5... | collective-permute-start | bytes 98312 | tf_op jit(solution)/shard_map/ppermute | solution.py:370
  26.7 4.0 %collective-permute-start.14 = (bf16[2,64,128]{2,1,0:T(8,128)(2,1)S(1)}, bf16[2,64,128]{2,1,0:T(8,128)(2,1)S(1)}, u32[]{:S(2)}, u32[]{:S(2)}) collective-permute-start(bf16[2,64,128]{2,1,0:T(8,128)(2,1)S(1)} %collective-permute-done.10.refs_1_.refs_5_), channel_id=1, source_target_pairs={{0,4},{4,0},{8,12},{12,8},{16,20},{20,16},{24,28},{28,24},{1,5},{5... | collective-permute-start | bytes 98312 | tf_op jit(solution)/shard_map/ppermute | solution.py:370
  28.3 2.4 %collective-permute-start.15 = (bf16[2,64,128]{2,1,0:T(8,128)(2,1)S(1)}, bf16[2,64,128]{2,1,0:T(8,128)(2,1)S(1)}, u32[]{:S(2)}, u32[]{:S(2)}) collective-permute-start(bf16[2,64,128]{2,1,0:T(8,128)(2,1)S(1)} %collective-permute-done.11.refs_2_.refs_6_), channel_id=1, source_target_pairs={{0,4},{4,0},{8,12},{12,8},{16,20},{20,16},{24,28},{28,24},{1,5},{5... | collective-permute-start | bytes 98312 | tf_op jit(solution)/shard_map/ppermute | solution.py:370
  30.7 1.2 %collective-permute-start.16 = (bf16[2,64,128]{2,1,0:T(8,128)(2,1)S(1)}, bf16[2,64,128]{2,1,0:T(8,128)(2,1)S(1)}, u32[]{:S(2)}, u32[]{:S(2)}) collective-permute-start(bf16[2,64,128]{2,1,0:T(8,128)(2,1)S(1)} %collective-permute-done.12.refs_3_.refs_7_), channel_id=1, source_target_pairs={{0,4},{4,0},{8,12},{12,8},{16,20},{20,16},{24,28},{28,24},{1,5},{5... | collective-permute-start | bytes 98312 | tf_op jit(solution)/shard_map/ppermute | solution.py:370
  33.3 7.3 %copy-start.7 = (bf16[128,512]{1,0:T(8,128)(2,1)S(1)}, bf16[128,512]{1,0:T(8,128)(2,1)}, u32[]{:S(2)}) copy-start(bf16[128,512]{1,0:T(8,128)(2,1)} %get-tuple-element.53) | copy-start | bytes 393220
  33.3 9.4 %copy-start.4 = (bf16[2,256,256]{2,1,0:T(8,128)(2,1)S(1)}, bf16[2,256,256]{2,1,0:T(8,128)(2,1)}, u32[]{:S(2)}) copy-start(bf16[2,256,256]{2,1,0:T(8,128)(2,1)} %get-tuple-element.56.held_ref) | copy-start | bytes 786436
  33.3 9.4 %copy-start.6 = (bf16[128,512]{1,0:T(8,128)(2,1)S(1)}, bf16[128,512]{1,0:T(8,128)(2,1)}, u32[]{:S(2)}) copy-start(bf16[128,512]{1,0:T(8,128)(2,1)} %get-tuple-element.54.kept_ref) | copy-start | bytes 393220
  33.3 9.4 %collective-permute-start.27 = (bf16[2,256,256]{2,1,0:T(8,128)(2,1)}, bf16[2,256,256]{2,1,0:T(8,128)(2,1)S(1)}, u32[]{:S(2)}, u32[]{:S(2)}) collective-permute-start(bf16[2,256,256]{2,1,0:T(8,128)(2,1)} %get-tuple-element.57), channel_id=1, source_target_pairs={{0,8},{4,12},{8,0},{12,4},{16,24},{20,28},{24,16},{28,20},{1,9},{5... | collective-permute-start | bytes 786440 | tf_op jit(solution)/shard_map/ppermute | solution.py:370
  33.9 6.7 %collective-permute-start.26 = (bf16[128,512]{1,0:T(8,128)(2,1)}, bf16[128,512]{1,0:T(8,128)(2,1)S(1)}, u32[]{:S(2)}, u32[]{:S(2)}) collective-permute-start(bf16[128,512]{1,0:T(8,128)(2,1)} %get-tuple-element.55), channel_id=1, source_target_pairs={{0,1},{1,0},{2,3},{3,2},{4,5},{5,4},{6,7},{7,6},{8,9},{9,8},{10,11... | collective-permute-start | bytes 393224 | tf_op jit(solution)/shard_map/ppermute | solution.py:370
  37.0 8.5 %collective-permute-start.17 = (bf16[16,32,128]{2,1,0:T(8,128)(2,1)S(1)}, bf16[16,32,128]{2,1,0:T(8,128)(2,1)S(1)}, u32[]{:S(2)}, u32[]{:S(2)}) collective-permute-start(bf16[16,32,128]{2,1,0:T(8,128)(2,1)S(1)} %get-tuple-element.48), channel_id=1, source_target_pairs={{0,8},{4,12},{8,0},{12,4},{16,24},{20,28},{24,16},{28,20},{1,9},{5... | collective-permute-start | bytes 393224 | tf_op jit(solution)/shard_map/ppermute | solution.py:370
  38.6 7.5 %collective-permute-start.18 = (bf16[16,32,128]{2,1,0:T(8,128)(2,1)S(1)}, bf16[16,32,128]{2,1,0:T(8,128)(2,1)S(1)}, u32[]{:S(2)}, u32[]{:S(2)}) collective-permute-start(bf16[16,32,128]{2,1,0:T(8,128)(2,1)S(1)} %get-tuple-element.49), channel_id=1, source_target_pairs={{0,16},{4,20},{8,24},{12,28},{16,0},{20,4},{24,8},{28,12},{1,17},{... | collective-permute-start | bytes 393224 | tf_op jit(solution)/shard_map/ppermute | solution.py:370
  39.1 8.5 %collective-permute-start.19 = (bf16[16,32,128]{2,1,0:T(8,128)(2,1)S(1)}, bf16[16,32,128]{2,1,0:T(8,128)(2,1)S(1)}, u32[]{:S(2)}, u32[]{:S(2)}) collective-permute-start(bf16[16,32,128]{2,1,0:T(8,128)(2,1)S(1)} %get-tuple-element.50), channel_id=1, source_target_pairs={{0,24},{4,28},{8,16},{12,20},{16,8},{20,12},{24,0},{28,4},{1,25},{... | collective-permute-start | bytes 393224 | tf_op jit(solution)/shard_map/ppermute | solution.py:370
  40.6 7.0 %collective-permute-start.25 = (bf16[128,512]{1,0:T(8,128)(2,1)S(1)}, bf16[128,512]{1,0:T(8,128)(2,1)S(1)}, u32[]{:S(2)}, u32[]{:S(2)}) collective-permute-start(bf16[128,512]{1,0:T(8,128)(2,1)S(1)} %copy-done.7), channel_id=1, source_target_pairs={{0,1},{1,0},{2,3},{3,2},{4,5},{5,4},{6,7},{7,6},{8,9},{9,8},{10,11... | collective-permute-start | bytes 393224 | tf_op jit(solution)/shard_map/ppermute | solution.py:370
  42.7 7.9 %copy-start.5 = (bf16[128,512]{1,0:T(8,128)(2,1)S(1)}, bf16[128,512]{1,0:T(8,128)(2,1)}, u32[]{:S(2)}) copy-start(bf16[128,512]{1,0:T(8,128)(2,1)} %get-tuple-element.52.kept_ref) | copy-start | bytes 393220
  42.8 7.8 %collective-permute-start.28 = (bf16[128,512]{1,0:T(8,128)(2,1)S(1)}, bf16[128,512]{1,0:T(8,128)(2,1)S(1)}, u32[]{:S(2)}, u32[]{:S(2)}) collective-permute-start(bf16[128,512]{1,0:T(8,128)(2,1)S(1)} %get-tuple-element.58), channel_id=1, source_target_pairs={{0,2},{1,3},{2,0},{3,1},{4,6},{5,7},{6,4},{7,5},{8,10},{9,11},{10,... | collective-permute-start | bytes 393224 | tf_op jit(solution)/shard_map/ppermute | solution.py:370
  45.5 5.1 %collective-permute-start.29 = (bf16[256,256]{1,0:T(8,128)(2,1)S(1)}, bf16[256,256]{1,0:T(8,128)(2,1)S(1)}, u32[]{:S(2)}, u32[]{:S(2)}) collective-permute-start(bf16[256,256]{1,0:T(8,128)(2,1)S(1)} %get-tuple-element.59), channel_id=1, source_target_pairs={{0,16},{4,20},{8,24},{12,28},{16,0},{20,4},{24,8},{28,12},{1,17},{... | collective-permute-start | bytes 393224 | tf_op jit(solution)/shard_map/ppermute | solution.py:370
  46.0 5.5 %collective-permute-start.20 = (bf16[16,32,128]{2,1,0:T(8,128)(2,1)S(1)}, bf16[16,32,128]{2,1,0:T(8,128)(2,1)S(1)}, u32[]{:S(2)}, u32[]{:S(2)}) collective-permute-start(bf16[16,32,128]{2,1,0:T(8,128)(2,1)S(1)} %get-tuple-element.62.refs_0_), channel_id=1, source_target_pairs={{0,4},{4,0},{8,12},{12,8},{16,20},{20,16},{24,28},{28,24},{1,5},{5... | collective-permute-start | bytes 393224 | tf_op jit(solution)/shard_map/ppermute | solution.py:370
  47.6 3.9 %collective-permute-start.21 = (bf16[16,32,128]{2,1,0:T(8,128)(2,1)S(1)}, bf16[16,32,128]{2,1,0:T(8,128)(2,1)S(1)}, u32[]{:S(2)}, u32[]{:S(2)}) collective-permute-start(bf16[16,32,128]{2,1,0:T(8,128)(2,1)S(1)} %collective-permute-done.17.refs_1_), channel_id=1, source_target_pairs={{0,4},{4,0},{8,12},{12,8},{16,20},{20,16},{24,28},{28,24},{1,5},{5... | collective-permute-start | bytes 393224 | tf_op jit(solution)/shard_map/ppermute | solution.py:370
  47.6 3.9 %collective-permute-start.22 = (bf16[16,32,128]{2,1,0:T(8,128)(2,1)S(1)}, bf16[16,32,128]{2,1,0:T(8,128)(2,1)S(1)}, u32[]{:S(2)}, u32[]{:S(2)}) collective-permute-start(bf16[16,32,128]{2,1,0:T(8,128)(2,1)S(1)} %collective-permute-done.18.refs_2_), channel_id=1, source_target_pairs={{0,4},{4,0},{8,12},{12,8},{16,20},{20,16},{24,28},{28,24},{1,5},{5... | collective-permute-start | bytes 393224 | tf_op jit(solution)/shard_map/ppermute | solution.py:370
  50.6 1.3 %collective-permute-start.23 = (bf16[16,32,128]{2,1,0:T(8,128)(2,1)S(1)}, bf16[16,32,128]{2,1,0:T(8,128)(2,1)S(1)}, u32[]{:S(2)}, u32[]{:S(2)}) collective-permute-start(bf16[16,32,128]{2,1,0:T(8,128)(2,1)S(1)} %collective-permute-done.19.refs_3_), channel_id=1, source_target_pairs={{0,4},{4,0},{8,12},{12,8},{16,20},{20,16},{24,28},{28,24},{1,5},{5... | collective-permute-start | bytes 393224 | tf_op jit(solution)/shard_map/ppermute | solution.py:370

commit v4 on v3

--- a/solution.py
+++ b/solution.py
@@ -14,7 +14,6 @@
 NT = (((1,), (1,)), ((), ()))
 NN = (((1,), (0,)), ((), ()))
 TAIL = 16
-LONG = 30_000_000_000
 RELAY = 5_000_000_000
 SUMS = 1_500_000_000
 
@@ -184,19 +183,33 @@
 
 def sources(pieces):
     me = lax.axis_index("tok")
+    if len(pieces) == 8:
+        for k, piece in enumerate(pieces):
+            yield me ^ (2 * (k % 4) + k // 4), piece, me % 2
+        return
+    for k, piece in enumerate(pieces[:4]):
+        yield me ^ (2 * k), piece, me % 2
+    for k in range(3):
+        yield me ^ (2 * k + 1), pieces[4].at[k], 0
+    yield me ^ 7, pieces[5], me % 2
+
+
+def gather_kernel(*refs):
+    *pieces, out_ref = refs
+    count = out_ref.shape[1]
+    other = 1 - lax.axis_index("tok") % 2
     for k, piece in enumerate(pieces):
-        yield me ^ (2 * (k % 4) + k // 4), piece
+        out_ref[k] = piece[pl.ds(other * count, count)]
 
 
 def forward_kernel(section_bits, blocks, mix_ref, *refs):
-    pieces, (out_ref, map_ref, a_ref, b_ref) = refs[:8], refs[8:]
+    pieces, (out_ref, map_ref, a_ref, b_ref) = refs[:6], refs[6:]
     owners, feats, pool_rows = out_ref.shape
     rows = a_ref.shape[2]
-    core = lax.axis_index("tok") % 2
-    for g, piece in sources(pieces):
-        map_ref[g] = piece[core, blocks * feats :, :]
+    for g, piece, at in sources(pieces):
+        map_ref[g] = piece[at, blocks * feats :, :]
         for n in range(blocks):
-            a_ref[g * blocks + n] = piece[core, n * feats : (n + 1) * feats, :]
+            a_ref[g * blocks + n] = piece[at, n * feats : (n + 1) * feats, :]
     done = run_sections(a_ref, b_ref, mix_ref, section_bits, False)
     ones = jnp.ones((16, blocks * rows), BF16)
     for g in range(owners):
@@ -215,8 +228,8 @@
     owners, feats, pool_rows = d_ref.shape
     rows = a_ref.shape[2]
     me = lax.axis_index("tok")
-    for g, piece in sources(pieces):
-        d_ref[g] = piece[me % 2, :feats]
+    for g, piece, at in sources(pieces):
+        d_ref[g] = piece[at, :feats]
     for g in range(owners):
         spread = lax.dot_general(
             d_ref[g], hot_of(map_ref[g][:blocks], pool_rows), NN, preferred_element_type=F32
@@ -226,17 +239,6 @@
     done = run_sections(a_ref, b_ref, mix_ref, section_bits, True)
     for o in range(4):
         outs[o][...] = done[pl.ds((me // 2 ^ o) * 2 * blocks, 2 * blocks)]
-
-
-def unpack_kernel(*refs):
-    pieces, out_ref, all_ref = refs[:8], refs[8], refs[9]
-    blocks, feats, rows = pieces[0].shape[0] // 2, *pieces[0].shape[1:]
-    core = lax.axis_index("tok") % 2
-    for g, piece in sources(pieces):
-        at = pl.ds(pl.multiple_of(g * feats, feats), feats)
-        all_ref[:, at, :] = piece[pl.ds(core * blocks, blocks)]
-    for n in range(blocks):
-        out_ref[n * rows : (n + 1) * rows, :] = all_ref[n].T
 
 
 def relay_kernel(came_ref, *refs):
@@ -288,8 +290,9 @@
 
 
 def project_kernel(w_ref, came_ref, *refs):
-    cots, pieces, shares, (held_ref, gone_ref) = refs[:4], refs[4:12], refs[12:16], refs[16:18]
-    share_ref, part_ref, pool_ref, sems = refs[18:]
+    cots, pieces, (kept_ref, last_ref, sent_ref, held_ref, gone_ref) = refs[:4], refs[4:12], refs[12:17]
+    share_ref, part_ref, pool_ref, sems = refs[17:]
+    shares = [kept_ref, sent_ref.at[0], last_ref, sent_ref.at[1]]
     feats, pool_rows = pieces[0].shape[1] // 2, pieces[0].shape[2]
     outs_tp = cots[0].shape[1]
     outs = came_ref.shape[1] // 4
@@ -301,9 +304,9 @@
         copies[-1].start()
 
     mine = pl.multiple_of((me % 2) * outs, outs)
-    for g, piece in sources(pieces):
-        pool_ref[g, :, :pool_rows] = piece[me % 2, feats:, :]
-        pool_ref[g, :, pool_rows:] = piece[1 - me % 2, feats:, :]
+    for g, piece, at in sources(pieces):
+        pool_ref[g, :, :pool_rows] = piece[at, feats:, :]
+        pool_ref[g, :, pool_rows:] = piece[1 - at, feats:, :]
     turned = jnp.concatenate([pool_ref[g] for g in range(len(pieces))], axis=0)
     pooled = turned[:, :pool_rows].T
     for o in (3, 1, 2, 0):
@@ -326,16 +329,42 @@
         copy.wait()
 
 
-def fold_kernel(kept_ref, got_ref, held_ref, came_ref, share_ref, part_ref):
-    share_ref[...] = (kept_ref[...].astype(F32) + got_ref[...].astype(F32)).astype(BF16)
+def fold_shares_kernel(kept_ref, got_ref, share_ref):
+    share_ref[...] = (kept_ref[...].astype(F32) + got_ref[1].astype(F32)).astype(BF16)
+
+
+def fold_parts_kernel(held_ref, came_ref, part_ref):
     part_ref[...] = (held_ref[1].astype(F32) + came_ref[1].astype(F32)).astype(BF16)
 
 
-def sum_kernel(scale, kept_ref, got_ref, share_ref, held_ref, came_ref, part_ref, projected_ref, grad_ref):
-    total = kept_ref[...].astype(F32) + got_ref[...].astype(F32) + share_ref[...].astype(F32)
+def arrive_kernel(kept_ref, got_ref, share_ref, part_ref, projected_ref, part_out):
+    total = kept_ref[...].astype(F32) + got_ref[0].astype(F32) + share_ref[...].astype(F32)
     projected_ref[...] = total.astype(BF16)
+    part_out[...] = part_ref[...]
+
+
+def finish_kernel(scale, *refs):
+    pieces, (projected_ref, held_ref, came_ref, part_ref) = refs[:6], refs[6:10]
+    tokens_out, projected_out, grad_out, all_ref, tokens_ref, grad_ref, sems = refs[10:]
+    blocks, feats, rows = pieces[0].shape[0] // 2, *pieces[0].shape[1:]
+    copies = []
+
+    def send(source, target):
+        copies.append(pltpu.make_async_copy(source, target, sems.at[len(copies)]))
+        copies[-1].start()
+
+    send(projected_ref, projected_out)
     total = held_ref[0].astype(F32) + came_ref[0].astype(F32) + part_ref[...].astype(F32)
     grad_ref[...] = total.T * scale
+    send(grad_ref, grad_out)
+    for g, piece, at in sources(pieces):
+        lanes = pl.ds(pl.multiple_of(g * feats, feats), feats)
+        all_ref[:, lanes, :] = piece[pl.ds(at * blocks, blocks)]
+    for n in range(blocks):
+        tokens_ref[n] = all_ref[n].T
+        send(tokens_ref.at[n], tokens_out.at[n])
+    for copy in copies:
+        copy.wait()
 
 
 def call(kernel, operands, out_shape, scratch, name, cost=0, out_space=pltpu.VMEM, in_space=pltpu.VMEM):
@@ -370,13 +399,13 @@
     return lax.ppermute(piece, axis, [(i, i ^ offset) for i in range(size)])
 
 
-def swap_all(pieces, axis):
-    return [pieces[0]] + [swap(piece, axis, o) for o, piece in enumerate(pieces) if o]
-
-
-def exchange(pieces):
+def exchange(pieces, halves=False):
     came = [pieces[0]] + [swap(pieces[o], "tok", 2 * o) for o in (1, 2, 3)]
-    return came + [swap(piece, "tok", 1) for piece in came]
+    if not halves:
+        return came + [swap(piece, "tok", 1) for piece in came]
+    count, *rest = pieces[0].shape
+    others = call(gather_kernel, came[:3], struct(3, count // 2, *rest), [], "gather")
+    return came + [swap(others, "tok", 1), swap(came[3], "tok", 1)]
 
 
 def shards(tokens, mix_weights, proj_weight, pool_map, out_cot):
@@ -412,7 +441,7 @@
         "pack",
         in_space=pltpu.HBM,
     )
-    packed = exchange(packed)
+    packed = exchange(packed, True)
     early = call(
         early_kernel,
         (proj_weight, out_cot, across),
@@ -437,10 +466,12 @@
     half = swap(half, "tok", 1)
     both = exchange(both)
 
-    *shares, held, gone = call(
+    kept, passed, sent, held, gone = call(
         project_kernel,
         (proj_weight, half, *cots, *both),
-        [in_hbm(pool_rows, outs_tp)] * 4 + [in_hbm(2, feats_tp, outs)] * 2,
+        [in_hbm(pool_rows, outs_tp)] * 2
+        + [in_hbm(2, pool_rows, outs_tp)]
+        + [in_hbm(2, feats_tp, outs)] * 2,
         [
             pltpu.VMEM((4, pool_rows, outs_tp), BF16),
             pltpu.VMEM((4, feats_tp, outs), BF16),
@@ -450,23 +481,26 @@
         "project",
         out_space=pltpu.HBM,
     )
-    gone = swap(gone, "tok", 2)
-    share, part = call(
-        fold_kernel,
-        (shares[2], swap(shares[3], "tp", 1), held, gone),
+    sent, gone = swap(sent, "tp", 1), swap(gone, "tok", 2)
+    share = call(
+        fold_shares_kernel,
+        (passed, sent),
+        struct(pool_rows, outs_tp),
+        [],
+        "fold_shares",
+        0,
+    )
+    part = call(
+        fold_parts_kernel, (held, gone), struct(feats_tp, outs), [], "fold_parts", 0
+    )
+    share = swap(share, "tp", 2)
+    part = swap(part, "tok", 4)
+    projected, part = call(
+        arrive_kernel,
+        (kept, sent, share, part),
         [struct(pool_rows, outs_tp), struct(feats_tp, outs)],
         [],
-        "fold",
-        LONG,
-    )
-    kept, sent, share = shares[0], swap(shares[1], "tp", 1), swap(share, "tp", 2)
-    part = swap(part, "tok", 4)
-    projected, proj_grad = call(
-        functools.partial(sum_kernel, 1.0 / math.sqrt(pool_rows * owners)),
-        (kept, sent, share, held, gone, part),
-        [struct(pool_rows, outs_tp), struct(outs, feats_tp, dtype=F32)],
-        [],
-        "sums",
+        "arrive",
         SUMS,
     )
 
@@ -477,14 +511,24 @@
         fields + [pltpu.VMEM((owners, feats, pool_rows), BF16)],
         "backward_mix",
     )
-    grad, projected = lax.optimization_barrier((exchange(grad), projected))
-    token_grad = call(
-        unpack_kernel,
-        grad,
-        struct(toks, feats_tp),
-        [pltpu.VMEM((blocks, feats_tp, rows), BF16)],
-        "unpack",
-    )
+    token_grad, projected, proj_grad = call(
+        functools.partial(finish_kernel, 1.0 / math.sqrt(pool_rows * owners)),
+        (*exchange(grad, True), projected, held, gone, part),
+        [
+            in_hbm(blocks, rows, feats_tp),
+            in_hbm(pool_rows, outs_tp),
+            in_hbm(outs, feats_tp, dtype=F32),
+        ],
+        [
+            pltpu.VMEM((blocks, feats_tp, rows), BF16),
+            pltpu.VMEM((blocks, rows, feats_tp), BF16),
+            pltpu.VMEM((outs, feats_tp), F32),
+            pltpu.SemaphoreType.DMA((blocks + 2,)),
+        ],
+        "finish",
+        out_space=pltpu.HBM,
+    )
+    token_grad = token_grad.reshape(toks, feats_tp)
     return (projected, token_grad, proj_grad)
 
 

time: 53.1 us -> 51.6 us (0.972)
  starting transfers between devices: 24.2 us -> 20.4 us
  waiting for transfers between devices: 16.8 us -> 19.3 us
  Pallas kernels: 11 us -> 10.2 us
    ppermute x30 -> x25, starting transfers between devices: 24.2 us -> 20.4 us  [swap(): return lax.ppermute(piece, axis, [(i, i ^ offset) for i in range(size)])]
    ppermute x30 -> x25, waiting for transfers between devices: 16.8 us -> 19.3 us  [swap(): return lax.ppermute(piece, axis, [(i, i ^ offset) for i in range(size)])]
    pallas_call x10 -> x13, Pallas kernels: 11 us -> 10.2 us  [call(): pl.pallas_call(kernel, out_shape=out_shape, in_specs=[into] * len(operand...]
  transfers between devices with their start and end apart: 30 -> 25, of which waited for: 11 -> 11; matrix products, arithmetic and copies ran while one was open for 0% -> 0% of each run, Pallas kernels for 12% -> 11%
where the time goes in v4:
time: 51.6 us; the launch traced here: 51.4 us
  starting transfers between devices  20.4 us (40%)
  waiting for transfers between devices  19.3 us (37%)
  Pallas kernels  10.2 us (20%)
  between operations  0.85 us (2%)
  local copies, waits for them, and re-layouts  0.6 us (1%)
    ppermute x25, starting transfers between devices, swap(): return lax.ppermute(piece, axis, [(i, i ^ offset) for i in range(size)])  20.4 us
    ppermute x25, waiting for transfers between devices, swap(): return lax.ppermute(piece, axis, [(i, i ^ offset) for i in range(size)])  19.3 us
    pallas_call x13, Pallas kernels, call(): pl.pallas_call(kernel, out_shape=out_shape, in_specs=[into] * len(operand...  10.2 us
  transfers between devices with their start and end apart: 25, of which 11 were waited for; matrix products, arithmetic and copies ran while one was open for 0% of the time, Pallas kernels for 11%

profile of v4, /device:TPU:0, one launch (start us, length us, event | category | flops | bytes accessed | tf_op | source)
XLA Modules:
  0.0 51.4 jit_solution(11185618663138953682)
XLA Ops:
  0.6 1.6 %pack.1 = (bf16[2,272,128]{2,1,0:T(8,128)(2,1)S(1)}, bf16[2,272,128]{2,1,0:T(8,128)(2,1)S(1)}, bf16[2,272,128]{2,1,0:T(8,128)(2,1)S(1)}, bf16[2,272,128]{2,1,0:T(8,128)(2,1)S(1)}) custom-call(bf16[8,128,256]{2,1,0:T(8,128)(2,1)} %bitcast.5, s32[8,128]{1,0:T(8,128)} %bitcast.3), custom_call_target="tpu_custom_call" | custom-call | tf_op jit(solution)/shard_map/pack/pallas_call | solution.py:377
  2.3 3.0 %collective-permute-start = (bf16[2,272,128]{2,1,0:T(8,128)(2,1)S(1)}, bf16[2,272,128]{2,1,0:T(8,128)(2,1)S(1)}, u32[]{:S(2)}, u32[]{:S(2)}) collective-permute-start(bf16[2,272,128]{2,1,0:T(8,128)(2,1)S(1)} %get-tuple-element.29), channel_id=1, source_target_pairs={{0,8},{4,12},{8,0},{12,4},{16,24},{20,28},{24,16},{28,20},{1,9},{5... | collective-permute-start | bytes 417800 | tf_op jit(solution)/shard_map/ppermute | solution.py:399
  5.3 1.5 %collective-permute-start.1 = (bf16[2,272,128]{2,1,0:T(8,128)(2,1)S(1)}, bf16[2,272,128]{2,1,0:T(8,128)(2,1)S(1)}, u32[]{:S(2)}, u32[]{:S(2)}) collective-permute-start(bf16[2,272,128]{2,1,0:T(8,128)(2,1)S(1)} %get-tuple-element.30), channel_id=1, source_target_pairs={{0,16},{4,20},{8,24},{12,28},{16,0},{20,4},{24,8},{28,12},{1,17},{... | collective-permute-start | bytes 417800 | tf_op jit(solution)/shard_map/ppermute | solution.py:399
  6.8 0.0 collective-permute-start.2
  6.8 2.0 %collective-permute-start.6 = (bf16[128,512]{1,0:T(8,128)(2,1)}, bf16[128,512]{1,0:T(8,128)(2,1)S(1)}, u32[]{:S(2)}, u32[]{:S(2)}) collective-permute-start(bf16[128,512]{1,0:T(8,128)(2,1)} %refs_0_.3), channel_id=1, source_target_pairs={{0,1},{1,0},{2,3},{3,2},{4,5},{5,4},{6,7},{7,6},{8,9},{9,8},{10,11... | collective-permute-start | bytes 393224 | tf_op jit(solution)/shard_map/ppermute | solution.py:399
  8.9 2.6 %collective-permute-start.5 = (bf16[128,512]{1,0:T(8,128)(2,1)}, bf16[128,512]{1,0:T(8,128)(2,1)S(1)}, u32[]{:S(2)}, u32[]{:S(2)}) collective-permute-start(bf16[128,512]{1,0:T(8,128)(2,1)} %refs_0_.3), channel_id=1, source_target_pairs={{0,2},{1,3},{2,0},{3,1},{4,6},{5,7},{6,4},{7,5},{8,10},{9,11},{10,... | collective-permute-start | bytes 393224 | tf_op jit(solution)/shard_map/ppermute | solution.py:399
  11.5 1.9 %collective-permute-done.1.refs_2_ = bf16[2,272,128]{2,1,0:T(8,128)(2,1)S(1)} collective-permute-done((bf16[2,272,128]{2,1,0:T(8,128)(2,1)S(1)}, bf16[2,272,128]{2,1,0:T(8,128)(2,1)S(1)}, u32[]{:S(2)}, u32[]{:S(2)}) %collective-permute-start.1) | collective-permute-done | bytes 139296 | tf_op jit(solution)/shard_map/ppermute | solution.py:399
  13.4 0.0 copy-start
  13.4 0.0 copy-start.2
  13.4 0.1 collective-permute-start.3
  13.5 0.5 collective-permute-start.4
  14.0 0.0 collective-permute-done.6.refs_0_.refs_1_
  14.0 3.0 %collective-permute-done.5.came_ref.refs_2_ = bf16[128,512]{1,0:T(8,128)(2,1)S(1)} collective-permute-done((bf16[128,512]{1,0:T(8,128)(2,1)}, bf16[128,512]{1,0:T(8,128)(2,1)S(1)}, u32[]{:S(2)}, u32[]{:S(2)}) %collective-permute-start.5) | collective-permute-done | bytes 131104 | tf_op jit(solution)/shard_map/ppermute | solution.py:399
  17.1 0.0 copy-start.1
  17.1 0.4 collective-permute-start.7
  17.5 0.3 early_cotangent.1.early_ref
  17.8 0.0 copy-start.5
  17.8 0.0 collective-permute-done.4.refs_5_
  17.8 0.6 %copy-done.1 = bf16[10,2,2,128,128]{4,3,2,1,0:T(8,128)(2,1)S(1)} copy-done((bf16[10,2,2,128,128]{4,3,2,1,0:T(8,128)(2,1)S(1)}, bf16[10,2,2,128,128]{4,3,2,1,0:T(8,128)(2,1)}, u32[]{:S(2)}) %copy-start.1) | copy-done | bytes 1310744
  18.4 2.8 %forward_mix.1 = (bf16[8,32,128]{2,1,0:T(8,128)(2,1)S(1)}, bf16[8,16,128]{2,1,0:T(8,128)(2,1)S(1)}) custom-call(bf16[10,2,2,128,128]{4,3,2,1,0:T(8,128)(2,1)S(1)} %copy-done.1, bf16[2,272,128]{2,1,0:T(8,128)(2,1)S(1)} %get-tuple-element.28.refs_0_, bf16[2,272,128]{2,1,0:T(8,128)(2,1)S(1)} %collective-permute-done.refs_1_, ...), custom_call_target="tpu_custom_call" | custom-call | tf_op jit(solution)/shard_map/forward_mix/pallas_call | solution.py:377
  21.2 0.9 %collective-permute-done.7.refs_3_ = bf16[128,512]{1,0:T(8,128)(2,1)S(1)} collective-permute-done((bf16[128,512]{1,0:T(8,128)(2,1)S(1)}, bf16[128,512]{1,0:T(8,128)(2,1)S(1)}, u32[]{:S(2)}, u32[]{:S(2)}) %collective-permute-start.7) | collective-permute-done | bytes 131104 | tf_op jit(solution)/shard_map/ppermute | solution.py:399
  22.1 0.4 cotangent.1
  22.5 0.1 collective-permute-start.20
  22.6 1.6 %collective-permute-start.8 = (bf16[2,64,128]{2,1,0:T(8,128)(2,1)S(1)}, bf16[2,64,128]{2,1,0:T(8,128)(2,1)S(1)}, u32[]{:S(2)}, u32[]{:S(2)}) collective-permute-start(bf16[2,64,128]{2,1,0:T(8,128)(2,1)S(1)} %get-tuple-element.35), channel_id=1, source_target_pairs={{0,8},{4,12},{8,0},{12,4},{16,24},{20,28},{24,16},{28,20},{1,9},{5... | collective-permute-start | bytes 98312 | tf_op jit(solution)/shard_map/ppermute | solution.py:399
  24.2 1.5 %collective-permute-start.9 = (bf16[2,64,128]{2,1,0:T(8,128)(2,1)S(1)}, bf16[2,64,128]{2,1,0:T(8,128)(2,1)S(1)}, u32[]{:S(2)}, u32[]{:S(2)}) collective-permute-start(bf16[2,64,128]{2,1,0:T(8,128)(2,1)S(1)} %get-tuple-element.36), channel_id=1, source_target_pairs={{0,16},{4,20},{8,24},{12,28},{16,0},{20,4},{24,8},{28,12},{1,17},{... | collective-permute-start | bytes 98312 | tf_op jit(solution)/shard_map/ppermute | solution.py:399
  25.7 0.5 collective-permute-start.10
  26.2 0.4 collective-permute-done.8.refs_1_.refs_5_
  26.6 0.1 collective-permute-start.12
  26.7 1.4 %collective-permute-done.9.refs_2_.refs_6_ = bf16[2,64,128]{2,1,0:T(8,128)(2,1)S(1)} collective-permute-done((bf16[2,64,128]{2,1,0:T(8,128)(2,1)S(1)}, bf16[2,64,128]{2,1,0:T(8,128)(2,1)S(1)}, u32[]{:S(2)}, u32[]{:S(2)}) %collective-permute-start.9) | collective-permute-done | bytes 32800 | tf_op jit(solution)/shard_map/ppermute | solution.py:399
  28.1 2.4 %collective-permute-done.10.refs_3_.refs_7_ = bf16[2,64,128]{2,1,0:T(8,128)(2,1)S(1)} collective-permute-done((bf16[2,64,128]{2,1,0:T(8,128)(2,1)S(1)}, bf16[2,64,128]{2,1,0:T(8,128)(2,1)S(1)}, u32[]{:S(2)}, u32[]{:S(2)}) %collective-permute-start.10) | collective-permute-done | bytes 32800 | tf_op jit(solution)/shard_map/ppermute | solution.py:399
  30.5 1.2 %collective-permute-done.14.refs_7_.refs_11_ = bf16[2,64,128]{2,1,0:T(8,128)(2,1)S(1)} collective-permute-done((bf16[2,64,128]{2,1,0:T(8,128)(2,1)S(1)}, bf16[2,64,128]{2,1,0:T(8,128)(2,1)S(1)}, u32[]{:S(2)}, u32[]{:S(2)}) %collective-permute-start.14) | collective-permute-done | bytes 32800 | tf_op jit(solution)/shard_map/ppermute | solution.py:399
  31.7 1.4 %project.1 = (bf16[128,512]{1,0:T(8,128)(2,1)}, bf16[128,512]{1,0:T(8,128)(2,1)}, bf16[2,128,512]{2,1,0:T(8,128)(2,1)}, bf16[2,256,256]{2,1,0:T(8,128)(2,1)}, bf16[2,256,256]{2,1,0:T(8,128)(2,1)}) custom-call(bf16[256,2048]{1,0:T(8,128)(2,1)S(1)} %copy-done, bf16[128,1024]{1,0:T(8,128)(2,1)S(1)} %collective-permute-done.20.came_ref, ...), custom_call_target="tpu_custom_call" | custom-call | tf_op jit(solution)/shard_map/project/pallas_call | solution.py:377
  33.1 0.0 copy-start.3
  33.1 0.4 collective-permute-start.21
  33.5 0.5 %collective-permute-start.23 = (bf16[2,256,256]{2,1,0:T(8,128)(2,1)}, bf16[2,256,256]{2,1,0:T(8,128)(2,1)S(1)}, u32[]{:S(2)}, u32[]{:S(2)}) collective-permute-start(bf16[2,256,256]{2,1,0:T(8,128)(2,1)} %get-tuple-element.47), channel_id=1, source_target_pairs={{0,8},{4,12},{8,0},{12,4},{16,24},{20,28},{24,16},{28,20},{1,9},{5... | collective-permute-start | bytes 786440 | tf_op jit(solution)/shard_map/ppermute | solution.py:399
  34.0 2.5 %backward_mix.1 = (bf16[16,32,128]{2,1,0:T(8,128)(2,1)S(1)}, bf16[16,32,128]{2,1,0:T(8,128)(2,1)S(1)}, bf16[16,32,128]{2,1,0:T(8,128)(2,1)S(1)}, bf16[16,32,128]{2,1,0:T(8,128)(2,1)S(1)}) custom-call(bf16[10,2,2,128,128]{4,3,2,1,0:T(8,128)(2,1)S(1)} %copy-done.1, bf16[8,16,128]{2,1,0:T(8,128)(2,1)S(1)} %get-tuple-element.32.map_ref, ...), custom_call_target="tpu_custom_call" | custom-call | tf_op jit(solution)/shard_map/backward_mix/pallas_call | solution.py:377
  36.5 1.6 %collective-permute-start.15 = (bf16[16,32,128]{2,1,0:T(8,128)(2,1)S(1)}, bf16[16,32,128]{2,1,0:T(8,128)(2,1)S(1)}, u32[]{:S(2)}, u32[]{:S(2)}) collective-permute-start(bf16[16,32,128]{2,1,0:T(8,128)(2,1)S(1)} %get-tuple-element.39), channel_id=1, source_target_pairs={{0,8},{4,12},{8,0},{12,4},{16,24},{20,28},{24,16},{28,20},{1,9},{5... | collective-permute-start | bytes 393224 | tf_op jit(solution)/shard_map/ppermute | solution.py:399
  38.1 0.5 collective-permute-start.16
  38.6 1.5 %collective-permute-start.17 = (bf16[16,32,128]{2,1,0:T(8,128)(2,1)S(1)}, bf16[16,32,128]{2,1,0:T(8,128)(2,1)S(1)}, u32[]{:S(2)}, u32[]{:S(2)}) collective-permute-start(bf16[16,32,128]{2,1,0:T(8,128)(2,1)S(1)} %get-tuple-element.41), channel_id=1, source_target_pairs={{0,24},{4,28},{8,16},{12,20},{16,8},{20,12},{24,0},{28,4},{1,25},{... | collective-permute-start | bytes 393224 | tf_op jit(solution)/shard_map/ppermute | solution.py:399
  40.1 1.7 %collective-permute-done.21.got_ref = bf16[2,128,512]{2,1,0:T(8,128)(2,1)S(1)} collective-permute-done((bf16[2,128,512]{2,1,0:T(8,128)(2,1)}, bf16[2,128,512]{2,1,0:T(8,128)(2,1)S(1)}, u32[]{:S(2)}, u32[]{:S(2)}) %collective-permute-start.21) | collective-permute-done | bytes 262176 | tf_op jit(solution)/shard_map/ppermute | solution.py:399
  41.8 1.4 %collective-permute-start.22 = (bf16[128,512]{1,0:T(8,128)(2,1)S(1)}, bf16[128,512]{1,0:T(8,128)(2,1)S(1)}, u32[]{:S(2)}, u32[]{:S(2)}) collective-permute-start(bf16[128,512]{1,0:T(8,128)(2,1)S(1)} %fold_shares.1), channel_id=1, source_target_pairs={{0,2},{1,3},{2,0},{3,1},{4,6},{5,7},{6,4},{7,5},{8,10},{9,11},{10,... | collective-permute-start | bytes 393224 | tf_op jit(solution)/shard_map/ppermute | solution.py:399
  43.3 0.6 %collective-permute-start.24 = (bf16[256,256]{1,0:T(8,128)(2,1)S(1)}, bf16[256,256]{1,0:T(8,128)(2,1)S(1)}, u32[]{:S(2)}, u32[]{:S(2)}) collective-permute-start(bf16[256,256]{1,0:T(8,128)(2,1)S(1)} %fold_parts.1), channel_id=1, source_target_pairs={{0,16},{4,20},{8,24},{12,28},{16,0},{20,4},{24,8},{28,12},{1,17},{... | collective-permute-start | bytes 393224 | tf_op jit(solution)/shard_map/ppermute | solution.py:399
  43.8 1.9 %collective-permute-done.15.refs_1_ = bf16[16,32,128]{2,1,0:T(8,128)(2,1)S(1)} collective-permute-done((bf16[16,32,128]{2,1,0:T(8,128)(2,1)S(1)}, bf16[16,32,128]{2,1,0:T(8,128)(2,1)S(1)}, u32[]{:S(2)}, u32[]{:S(2)}) %collective-permute-start.15) | collective-permute-done | bytes 131104 | tf_op jit(solution)/shard_map/ppermute | solution.py:399
  45.7 0.1 collective-permute-start.18
  45.8 1.7 %collective-permute-done.17.refs_3_ = bf16[16,32,128]{2,1,0:T(8,128)(2,1)S(1)} collective-permute-done((bf16[16,32,128]{2,1,0:T(8,128)(2,1)S(1)}, bf16[16,32,128]{2,1,0:T(8,128)(2,1)S(1)}, u32[]{:S(2)}, u32[]{:S(2)}) %collective-permute-start.17) | collective-permute-done | bytes 131104 | tf_op jit(solution)/shard_map/ppermute | solution.py:399
  47.5 2.7 %collective-permute-done.22.share_ref = bf16[128,512]{1,0:T(8,128)(2,1)S(1)} collective-permute-done((bf16[128,512]{1,0:T(8,128)(2,1)S(1)}, bf16[128,512]{1,0:T(8,128)(2,1)S(1)}, u32[]{:S(2)}, u32[]{:S(2)}) %collective-permute-start.22) | collective-permute-done | bytes 131104 | tf_op jit(solution)/shard_map/ppermute | solution.py:399
  50.2 0.1 arrive.1
  50.3 1.1 %finish.1 = (bf16[8,128,256]{2,1,0:T(8,128)(2,1)}, bf16[128,512]{1,0:T(8,128)(2,1)}, f32[256,256]{1,0:T(8,128)}) custom-call(bf16[16,32,128]{2,1,0:T(8,128)(2,1)S(1)} %get-tuple-element.38.refs_0_, bf16[16,32,128]{2,1,0:T(8,128)(2,1)S(1)} %collective-permute-done.15.refs_1_, bf16[16,32,128]{2,1,0:T(8,128)(2,1)S(1)} %collective-permute-done.16.refs_2_, ...), custom_call_target="tpu_custom_call" | custom-call | tf_op jit(solution)/shard_map/finish/pallas_call | solution.py:377
  (29 shorter events, 0.2 us)
Async XLA Ops:
  2.3 9.2 %collective-permute-start = (bf16[2,272,128]{2,1,0:T(8,128)(2,1)S(1)}, bf16[2,272,128]{2,1,0:T(8,128)(2,1)S(1)}, u32[]{:S(2)}, u32[]{:S(2)}) collective-permute-start(bf16[2,272,128]{2,1,0:T(8,128)(2,1)S(1)} %get-tuple-element.29), channel_id=1, source_target_pairs={{0,8},{4,12},{8,0},{12,4},{16,24},{20,28},{24,16},{28,20},{1,9},{5... | collective-permute-start | bytes 417800 | tf_op jit(solution)/shard_map/ppermute | solution.py:399
  5.3 8.1 %collective-permute-start.1 = (bf16[2,272,128]{2,1,0:T(8,128)(2,1)S(1)}, bf16[2,272,128]{2,1,0:T(8,128)(2,1)S(1)}, u32[]{:S(2)}, u32[]{:S(2)}) collective-permute-start(bf16[2,272,128]{2,1,0:T(8,128)(2,1)S(1)} %get-tuple-element.30), channel_id=1, source_target_pairs={{0,16},{4,20},{8,24},{12,28},{16,0},{20,4},{24,8},{28,12},{1,17},{... | collective-permute-start | bytes 417800 | tf_op jit(solution)/shard_map/ppermute | solution.py:399
  6.8 6.7 %collective-permute-start.2 = (bf16[2,272,128]{2,1,0:T(8,128)(2,1)S(1)}, bf16[2,272,128]{2,1,0:T(8,128)(2,1)S(1)}, u32[]{:S(2)}, u32[]{:S(2)}) collective-permute-start(bf16[2,272,128]{2,1,0:T(8,128)(2,1)S(1)} %get-tuple-element.31), channel_id=1, source_target_pairs={{0,24},{4,28},{8,16},{12,20},{16,8},{20,12},{24,0},{28,4},{1,25},{... | collective-permute-start | bytes 417800 | tf_op jit(solution)/shard_map/ppermute | solution.py:399
  6.8 7.2 %collective-permute-start.6 = (bf16[128,512]{1,0:T(8,128)(2,1)}, bf16[128,512]{1,0:T(8,128)(2,1)S(1)}, u32[]{:S(2)}, u32[]{:S(2)}) collective-permute-start(bf16[128,512]{1,0:T(8,128)(2,1)} %refs_0_.3), channel_id=1, source_target_pairs={{0,1},{1,0},{2,3},{3,2},{4,5},{5,4},{6,7},{7,6},{8,9},{9,8},{10,11... | collective-permute-start | bytes 393224 | tf_op jit(solution)/shard_map/ppermute | solution.py:399
  8.9 8.2 %collective-permute-start.5 = (bf16[128,512]{1,0:T(8,128)(2,1)}, bf16[128,512]{1,0:T(8,128)(2,1)S(1)}, u32[]{:S(2)}, u32[]{:S(2)}) collective-permute-start(bf16[128,512]{1,0:T(8,128)(2,1)} %refs_0_.3), channel_id=1, source_target_pairs={{0,2},{1,3},{2,0},{3,1},{4,6},{5,7},{6,4},{7,5},{8,10},{9,11},{10,... | collective-permute-start | bytes 393224 | tf_op jit(solution)/shard_map/ppermute | solution.py:399
  13.4 4.1 %copy-start = (bf16[256,2048]{1,0:T(8,128)(2,1)S(1)}, bf16[256,2048]{1,0:T(8,128)(2,1)}, u32[]{:S(2)}) copy-start(bf16[256,2048]{1,0:T(8,128)(2,1)} %w_ref.5) | copy-start | bytes 3145732
  13.4 4.1 %copy-start.2 = (bf16[128,512]{1,0:T(8,128)(2,1)S(1)}, bf16[128,512]{1,0:T(8,128)(2,1)}, u32[]{:S(2)}) copy-start(bf16[128,512]{1,0:T(8,128)(2,1)} %refs_0_.3) | copy-start | bytes 393220
  13.4 4.4 %collective-permute-start.3 = (bf16[3,1,272,128]{3,2,1,0:T(8,128)(2,1)S(1)}, bf16[3,1,272,128]{3,2,1,0:T(8,128)(2,1)S(1)}, u32[]{:S(2)}, u32[]{:S(2)}) collective-permute-start(bf16[3,1,272,128]{3,2,1,0:T(8,128)(2,1)S(1)} %gather.2), channel_id=1, source_target_pairs={{0,4},{4,0},{8,12},{12,8},{16,20},{20,16},{24,28},{28,24},{1,5},{5... | collective-permute-start | bytes 626696 | tf_op jit(solution)/shard_map/ppermute | solution.py:399
  13.5 4.3 %collective-permute-start.4 = (bf16[2,272,128]{2,1,0:T(8,128)(2,1)S(1)}, bf16[2,272,128]{2,1,0:T(8,128)(2,1)S(1)}, u32[]{:S(2)}, u32[]{:S(2)}) collective-permute-start(bf16[2,272,128]{2,1,0:T(8,128)(2,1)S(1)} %collective-permute-done.2.refs_3_), channel_id=1, source_target_pairs={{0,4},{4,0},{8,12},{12,8},{16,20},{20,16},{24,28},{28,24},{1,5},{5... | collective-permute-start | bytes 417800 | tf_op jit(solution)/shard_map/ppermute | solution.py:399
  17.1 1.3 %copy-start.1 = (bf16[10,2,2,128,128]{4,3,2,1,0:T(8,128)(2,1)S(1)}, bf16[10,2,2,128,128]{4,3,2,1,0:T(8,128)(2,1)}, u32[]{:S(2)}) copy-start(bf16[10,2,2,128,128]{4,3,2,1,0:T(8,128)(2,1)} %mix_ref.3) | copy-start | bytes 3932164
  17.1 5.0 %collective-permute-start.7 = (bf16[128,512]{1,0:T(8,128)(2,1)S(1)}, bf16[128,512]{1,0:T(8,128)(2,1)S(1)}, u32[]{:S(2)}, u32[]{:S(2)}) collective-permute-start(bf16[128,512]{1,0:T(8,128)(2,1)S(1)} %relay.1), channel_id=1, source_target_pairs={{0,1},{1,0},{2,3},{3,2},{4,5},{5,4},{6,7},{7,6},{8,9},{9,8},{10,11... | collective-permute-start | bytes 393224 | tf_op jit(solution)/shard_map/ppermute | solution.py:399
  17.8 4.3 %copy-start.5 = (s32[1024]{0:T(1024)S(1)}, s32[1024]{0:T(1024)}, u32[]{:S(2)}) copy-start(s32[1024]{0:T(1024)} %param.8) | copy-start | bytes 12292
  22.5 9.2 %collective-permute-start.20 = (bf16[128,1024]{1,0:T(8,128)(2,1)S(1)}, bf16[128,1024]{1,0:T(8,128)(2,1)S(1)}, u32[]{:S(2)}, u32[]{:S(2)}) collective-permute-start(bf16[128,1024]{1,0:T(8,128)(2,1)S(1)} %get-tuple-element.42), channel_id=1, source_target_pairs={{0,4},{4,0},{8,12},{12,8},{16,20},{20,16},{24,28},{28,24},{1,5},{5... | collective-permute-start | bytes 786440 | tf_op jit(solution)/shard_map/ppermute | solution.py:399
  22.6 4.0 %collective-permute-start.8 = (bf16[2,64,128]{2,1,0:T(8,128)(2,1)S(1)}, bf16[2,64,128]{2,1,0:T(8,128)(2,1)S(1)}, u32[]{:S(2)}, u32[]{:S(2)}) collective-permute-start(bf16[2,64,128]{2,1,0:T(8,128)(2,1)S(1)} %get-tuple-element.35), channel_id=1, source_target_pairs={{0,8},{4,12},{8,0},{12,4},{16,24},{20,28},{24,16},{28,20},{1,9},{5... | collective-permute-start | bytes 98312 | tf_op jit(solution)/shard_map/ppermute | solution.py:399
  24.2 3.9 %collective-permute-start.9 = (bf16[2,64,128]{2,1,0:T(8,128)(2,1)S(1)}, bf16[2,64,128]{2,1,0:T(8,128)(2,1)S(1)}, u32[]{:S(2)}, u32[]{:S(2)}) collective-permute-start(bf16[2,64,128]{2,1,0:T(8,128)(2,1)S(1)} %get-tuple-element.36), channel_id=1, source_target_pairs={{0,16},{4,20},{8,24},{12,28},{16,0},{20,4},{24,8},{28,12},{1,17},{... | collective-permute-start | bytes 98312 | tf_op jit(solution)/shard_map/ppermute | solution.py:399
  25.7 4.8 %collective-permute-start.10 = (bf16[2,64,128]{2,1,0:T(8,128)(2,1)S(1)}, bf16[2,64,128]{2,1,0:T(8,128)(2,1)S(1)}, u32[]{:S(2)}, u32[]{:S(2)}) collective-permute-start(bf16[2,64,128]{2,1,0:T(8,128)(2,1)S(1)} %get-tuple-element.37), channel_id=1, source_target_pairs={{0,24},{4,28},{8,16},{12,20},{16,8},{20,12},{24,0},{28,4},{1,25},{... | collective-permute-start | bytes 98312 | tf_op jit(solution)/shard_map/ppermute | solution.py:399
  26.2 4.3 %collective-permute-start.11 = (bf16[2,64,128]{2,1,0:T(8,128)(2,1)S(1)}, bf16[2,64,128]{2,1,0:T(8,128)(2,1)S(1)}, u32[]{:S(2)}, u32[]{:S(2)}) collective-permute-start(bf16[2,64,128]{2,1,0:T(8,128)(2,1)S(1)} %get-tuple-element.34.refs_0_.refs_4_), channel_id=1, source_target_pairs={{0,4},{4,0},{8,12},{12,8},{16,20},{20,16},{24,28},{28,24},{1,5},{5... | collective-permute-start | bytes 98312 | tf_op jit(solution)/shard_map/ppermute | solution.py:399
  26.6 3.9 %collective-permute-start.12 = (bf16[2,64,128]{2,1,0:T(8,128)(2,1)S(1)}, bf16[2,64,128]{2,1,0:T(8,128)(2,1)S(1)}, u32[]{:S(2)}, u32[]{:S(2)}) collective-permute-start(bf16[2,64,128]{2,1,0:T(8,128)(2,1)S(1)} %collective-permute-done.8.refs_1_.refs_5_), channel_id=1, source_target_pairs={{0,4},{4,0},{8,12},{12,8},{16,20},{20,16},{24,28},{28,24},{1,5},{5... | collective-permute-start | bytes 98312 | tf_op jit(solution)/shard_map/ppermute | solution.py:399
  28.1 2.4 %collective-permute-start.13 = (bf16[2,64,128]{2,1,0:T(8,128)(2,1)S(1)}, bf16[2,64,128]{2,1,0:T(8,128)(2,1)S(1)}, u32[]{:S(2)}, u32[]{:S(2)}) collective-permute-start(bf16[2,64,128]{2,1,0:T(8,128)(2,1)S(1)} %collective-permute-done.9.refs_2_.refs_6_), channel_id=1, source_target_pairs={{0,4},{4,0},{8,12},{12,8},{16,20},{20,16},{24,28},{28,24},{1,5},{5... | collective-permute-start | bytes 98312 | tf_op jit(solution)/shard_map/ppermute | solution.py:399
  30.5 1.2 %collective-permute-start.14 = (bf16[2,64,128]{2,1,0:T(8,128)(2,1)S(1)}, bf16[2,64,128]{2,1,0:T(8,128)(2,1)S(1)}, u32[]{:S(2)}, u32[]{:S(2)}) collective-permute-start(bf16[2,64,128]{2,1,0:T(8,128)(2,1)S(1)} %collective-permute-done.10.refs_3_.refs_7_), channel_id=1, source_target_pairs={{0,4},{4,0},{8,12},{12,8},{16,20},{20,16},{24,28},{28,24},{1,5},{5... | collective-permute-start | bytes 98312 | tf_op jit(solution)/shard_map/ppermute | solution.py:399
  33.1 8.7 %copy-start.4 = (bf16[128,512]{1,0:T(8,128)(2,1)S(1)}, bf16[128,512]{1,0:T(8,128)(2,1)}, u32[]{:S(2)}) copy-start(bf16[128,512]{1,0:T(8,128)(2,1)} %get-tuple-element.45.kept_ref) | copy-start | bytes 393220
  33.1 10.1 %copy-start.3 = (bf16[2,256,256]{2,1,0:T(8,128)(2,1)S(1)}, bf16[2,256,256]{2,1,0:T(8,128)(2,1)}, u32[]{:S(2)}) copy-start(bf16[2,256,256]{2,1,0:T(8,128)(2,1)} %get-tuple-element.46.held_ref.refs_7_) | copy-start | bytes 786436
  33.1 8.7 %collective-permute-start.21 = (bf16[2,128,512]{2,1,0:T(8,128)(2,1)}, bf16[2,128,512]{2,1,0:T(8,128)(2,1)S(1)}, u32[]{:S(2)}, u32[]{:S(2)}) collective-permute-start(bf16[2,128,512]{2,1,0:T(8,128)(2,1)} %get-tuple-element.44), channel_id=1, source_target_pairs={{0,1},{1,0},{2,3},{3,2},{4,5},{5,4},{6,7},{7,6},{8,9},{9,8},{10,11... | collective-permute-start | bytes 786440 | tf_op jit(solution)/shard_map/ppermute | solution.py:399
  33.5 9.7 %collective-permute-start.23 = (bf16[2,256,256]{2,1,0:T(8,128)(2,1)}, bf16[2,256,256]{2,1,0:T(8,128)(2,1)S(1)}, u32[]{:S(2)}, u32[]{:S(2)}) collective-permute-start(bf16[2,256,256]{2,1,0:T(8,128)(2,1)} %get-tuple-element.47), channel_id=1, source_target_pairs={{0,8},{4,12},{8,0},{12,4},{16,24},{20,28},{24,16},{28,20},{1,9},{5... | collective-permute-start | bytes 786440 | tf_op jit(solution)/shard_map/ppermute | solution.py:399
  34.0 16.2 %copy-start.6 = (bf16[128,512]{1,0:T(8,128)(2,1)S(1)}, bf16[128,512]{1,0:T(8,128)(2,1)}, u32[]{:S(2)}) copy-start(bf16[128,512]{1,0:T(8,128)(2,1)} %get-tuple-element.43.kept_ref) | copy-start | bytes 393220
  36.5 9.2 %collective-permute-start.15 = (bf16[16,32,128]{2,1,0:T(8,128)(2,1)S(1)}, bf16[16,32,128]{2,1,0:T(8,128)(2,1)S(1)}, u32[]{:S(2)}, u32[]{:S(2)}) collective-permute-start(bf16[16,32,128]{2,1,0:T(8,128)(2,1)S(1)} %get-tuple-element.39), channel_id=1, source_target_pairs={{0,8},{4,12},{8,0},{12,4},{16,24},{20,28},{24,16},{28,20},{1,9},{5... | collective-permute-start | bytes 393224 | tf_op jit(solution)/shard_map/ppermute | solution.py:399
  38.1 7.6 %collective-permute-start.16 = (bf16[16,32,128]{2,1,0:T(8,128)(2,1)S(1)}, bf16[16,32,128]{2,1,0:T(8,128)(2,1)S(1)}, u32[]{:S(2)}, u32[]{:S(2)}) collective-permute-start(bf16[16,32,128]{2,1,0:T(8,128)(2,1)S(1)} %get-tuple-element.40), channel_id=1, source_target_pairs={{0,16},{4,20},{8,24},{12,28},{16,0},{20,4},{24,8},{28,12},{1,17},{... | collective-permute-start | bytes 393224 | tf_op jit(solution)/shard_map/ppermute | solution.py:399
  38.6 8.9 %collective-permute-start.17 = (bf16[16,32,128]{2,1,0:T(8,128)(2,1)S(1)}, bf16[16,32,128]{2,1,0:T(8,128)(2,1)S(1)}, u32[]{:S(2)}, u32[]{:S(2)}) collective-permute-start(bf16[16,32,128]{2,1,0:T(8,128)(2,1)S(1)} %get-tuple-element.41), channel_id=1, source_target_pairs={{0,24},{4,28},{8,16},{12,20},{16,8},{20,12},{24,0},{28,4},{1,25},{... | collective-permute-start | bytes 393224 | tf_op jit(solution)/shard_map/ppermute | solution.py:399
  41.8 8.4 %collective-permute-start.22 = (bf16[128,512]{1,0:T(8,128)(2,1)S(1)}, bf16[128,512]{1,0:T(8,128)(2,1)S(1)}, u32[]{:S(2)}, u32[]{:S(2)}) collective-permute-start(bf16[128,512]{1,0:T(8,128)(2,1)S(1)} %fold_shares.1), channel_id=1, source_target_pairs={{0,2},{1,3},{2,0},{3,1},{4,6},{5,7},{6,4},{7,5},{8,10},{9,11},{10,... | collective-permute-start | bytes 393224 | tf_op jit(solution)/shard_map/ppermute | solution.py:399
  43.3 6.9 %collective-permute-start.24 = (bf16[256,256]{1,0:T(8,128)(2,1)S(1)}, bf16[256,256]{1,0:T(8,128)(2,1)S(1)}, u32[]{:S(2)}, u32[]{:S(2)}) collective-permute-start(bf16[256,256]{1,0:T(8,128)(2,1)S(1)} %fold_parts.1), channel_id=1, source_target_pairs={{0,16},{4,20},{8,24},{12,28},{16,0},{20,4},{24,8},{28,12},{1,17},{... | collective-permute-start | bytes 393224 | tf_op jit(solution)/shard_map/ppermute | solution.py:399
  45.7 4.6 %collective-permute-start.18 = (bf16[3,8,32,128]{3,2,1,0:T(8,128)(2,1)S(1)}, bf16[3,8,32,128]{3,2,1,0:T(8,128)(2,1)S(1)}, u32[]{:S(2)}, u32[]{:S(2)}) collective-permute-start(bf16[3,8,32,128]{3,2,1,0:T(8,128)(2,1)S(1)} %gather.3), channel_id=1, source_target_pairs={{0,4},{4,0},{8,12},{12,8},{16,20},{20,16},{24,28},{28,24},{1,5},{5... | collective-permute-start | bytes 589832 | tf_op jit(solution)/shard_map/ppermute | solution.py:399
  47.5 2.8 %collective-permute-start.19 = (bf16[16,32,128]{2,1,0:T(8,128)(2,1)S(1)}, bf16[16,32,128]{2,1,0:T(8,128)(2,1)S(1)}, u32[]{:S(2)}, u32[]{:S(2)}) collective-permute-start(bf16[16,32,128]{2,1,0:T(8,128)(2,1)S(1)} %collective-permute-done.17.refs_3_), channel_id=1, source_target_pairs={{0,4},{4,0},{8,12},{12,8},{16,20},{20,16},{24,28},{28,24},{1,5},{5... | collective-permute-start | bytes 393224 | tf_op jit(solution)/shard_map/ppermute | solution.py:399

commit v5 on v4

--- a/solution.py
+++ b/solution.py
@@ -15,7 +15,7 @@
 NN = (((1,), (0,)), ((), ()))
 TAIL = 16
 RELAY = 5_000_000_000
-SUMS = 1_500_000_000
+SUMS = 1_000_000_000
 
 
 def contract(matrix, operand, backward):
@@ -289,42 +289,48 @@
         send_ref[:, o * outs : (o + 1) * outs] = cots[o][:, pl.ds(other, outs)]
 
 
-def project_kernel(w_ref, came_ref, *refs):
-    cots, pieces, (kept_ref, last_ref, sent_ref, held_ref, gone_ref) = refs[:4], refs[4:12], refs[12:17]
-    share_ref, part_ref, pool_ref, sems = refs[17:]
-    shares = [kept_ref, sent_ref.at[0], last_ref, sent_ref.at[1]]
+def project_kernel(w_ref, *refs):
+    pieces, (kept_ref, passed_ref, sent_ref, share_ref, pool_ref, sems) = refs[:8], refs[8:]
+    feats = pieces[0].shape[1] // 2
+    outs_tp = share_ref.shape[2]
+    place = lax.axis_index("tp")
+    targets = [kept_ref, sent_ref.at[0], passed_ref, sent_ref.at[1]]
+    for g, piece, at in sources(pieces):
+        pool_ref[g] = piece[at, feats:, :]
+    pooled = jnp.concatenate([pool_ref[g] for g in range(len(pieces))], axis=0).T
+    copies = []
+    for o in (3, 1, 2, 0):
+        at = pl.multiple_of((place ^ o) * outs_tp, outs_tp)
+        share_ref[o] = lax.dot_general(
+            pooled, w_ref[:, pl.ds(at, outs_tp)], NN, preferred_element_type=F32
+        ).astype(BF16)
+        copies.append(pltpu.make_async_copy(share_ref.at[o], targets[o], sems.at[o]))
+        copies[-1].start()
+    for copy in copies:
+        copy.wait()
+
+
+def gradient_kernel(came_ref, *refs):
+    cots, pieces, (held_ref, gone_ref, part_ref, pool_ref, sems) = refs[:4], refs[4:12], refs[-5:]
     feats, pool_rows = pieces[0].shape[1] // 2, pieces[0].shape[2]
-    outs_tp = cots[0].shape[1]
     outs = came_ref.shape[1] // 4
     place, me = lax.axis_index("tp"), lax.axis_index("tok")
-    copies = []
-
-    def send(source, target):
-        copies.append(pltpu.make_async_copy(source, target, sems.at[len(copies)]))
-        copies[-1].start()
-
     mine = pl.multiple_of((me % 2) * outs, outs)
     for g, piece, at in sources(pieces):
         pool_ref[g, :, :pool_rows] = piece[at, feats:, :]
         pool_ref[g, :, pool_rows:] = piece[1 - at, feats:, :]
     turned = jnp.concatenate([pool_ref[g] for g in range(len(pieces))], axis=0)
-    pooled = turned[:, :pool_rows].T
-    for o in (3, 1, 2, 0):
-        at = pl.multiple_of((place ^ o) * outs_tp, outs_tp)
-        share_ref[o] = lax.dot_general(
-            pooled, w_ref[:, pl.ds(at, outs_tp)], NN, preferred_element_type=F32
-        ).astype(BF16)
-        send(share_ref.at[o], shares[o])
     for o in range(4):
         own = cots[o][:, pl.ds(mine, outs)]
-        cot = jnp.concatenate(
-            [own, came_ref[:, o * outs : (o + 1) * outs]], axis=0
-        )
+        cot = jnp.concatenate([own, came_ref[:, o * outs : (o + 1) * outs]], axis=0)
         part_ref[place ^ o] = lax.dot_general(
             turned, cot, NN, preferred_element_type=F32
         ).astype(BF16)
+    copies = []
     for o in (1, 3, 0, 2):
-        send(part_ref.at[(me // 2) ^ o], (gone_ref if o % 2 else held_ref).at[o // 2])
+        target = (gone_ref if o % 2 else held_ref).at[o // 2]
+        copies.append(pltpu.make_async_copy(part_ref.at[(me // 2) ^ o], target, sems.at[o]))
+        copies[-1].start()
     for copy in copies:
         copy.wait()
 
@@ -442,13 +448,6 @@
         in_space=pltpu.HBM,
     )
     packed = exchange(packed, True)
-    early = call(
-        early_kernel,
-        (proj_weight, out_cot, across),
-        struct(pool_rows, feats_tp, dtype=F32),
-        [],
-        "early_cotangent",
-    )
     pooled, map_rows = call(
         functools.partial(forward_kernel, section_bits, blocks),
         (mix_weights, *packed),
@@ -456,6 +455,14 @@
         fields,
         "forward_mix",
     )
+    pooled, later = lax.optimization_barrier((pooled, across))
+    early = call(
+        early_kernel,
+        (proj_weight, out_cot, later),
+        struct(pool_rows, feats_tp, dtype=F32),
+        [],
+        "early_cotangent",
+    )
     *both, half = call(
         cotangent_kernel,
         (proj_weight, maps, pooled, early, *cots),
@@ -466,19 +473,29 @@
     half = swap(half, "tok", 1)
     both = exchange(both)
 
-    kept, passed, sent, held, gone = call(
+    kept, passed, sent = call(
         project_kernel,
-        (proj_weight, half, *cots, *both),
-        [in_hbm(pool_rows, outs_tp)] * 2
-        + [in_hbm(2, pool_rows, outs_tp)]
-        + [in_hbm(2, feats_tp, outs)] * 2,
+        (proj_weight, *both),
+        [in_hbm(pool_rows, outs_tp)] * 2 + [in_hbm(2, pool_rows, outs_tp)],
         [
             pltpu.VMEM((4, pool_rows, outs_tp), BF16),
+            pltpu.VMEM((owners, feats, pool_rows), BF16),
+            pltpu.SemaphoreType.DMA((4,)),
+        ],
+        "project",
+        out_space=pltpu.HBM,
+    )
+    half, passed = lax.optimization_barrier((half, passed))
+    held, gone = call(
+        gradient_kernel,
+        (half, *cots, *both),
+        [in_hbm(2, feats_tp, outs)] * 2,
+        [
             pltpu.VMEM((4, feats_tp, outs), BF16),
             pltpu.VMEM((owners, feats, 2 * pool_rows), BF16),
-            pltpu.SemaphoreType.DMA((8,)),
+            pltpu.SemaphoreType.DMA((4,)),
         ],
-        "project",
+        "projector_gradient",
         out_space=pltpu.HBM,
     )
     sent, gone = swap(sent, "tp", 1), swap(gone, "tok", 2)

time: 51.6 us -> 51.4 us (level)
  waiting for transfers between devices: 19.3 us -> 15.6 us
  starting transfers between devices: 20.4 us -> 23.6 us
  Pallas kernels: 10.2 us -> 11.1 us
  local copies, waits for them, and re-layouts: 0.6 us -> 0.04 us
    ppermute x25, waiting for transfers between devices: 19.3 us -> 15.6 us  [swap(): return lax.ppermute(piece, axis, [(i, i ^ offset) for i in range(size)])]
    ppermute x25, starting transfers between devices: 20.4 us -> 23.6 us  [swap(): return lax.ppermute(piece, axis, [(i, i ^ offset) for i in range(size)])]
    pallas_call x13 -> x14, Pallas kernels: 10.2 us -> 11.1 us  [call(): pl.pallas_call(kernel, out_shape=out_shape, in_specs=[into] * len(operand...]
    unnamed x14, local copies, waits for them, and re-layouts: 0.6 us -> 0.04 us
  transfers between devices with their start and end apart: 25 -> 25, of which waited for: 11 -> 13; matrix products, arithmetic and copies ran while one was open for 0% -> 0% of each run, Pallas kernels for 11% -> 16%
where the time goes in v5:
time: 51.4 us; the launch traced here: 51.2 us
  starting transfers between devices  23.6 us (46%)
  waiting for transfers between devices  15.6 us (30%)
  Pallas kernels  11.1 us (22%)
  between operations  0.85 us (2%)
    ppermute x25, starting transfers between devices, swap(): return lax.ppermute(piece, axis, [(i, i ^ offset) for i in range(size)])  23.6 us
    ppermute x25, waiting for transfers between devices, swap(): return lax.ppermute(piece, axis, [(i, i ^ offset) for i in range(size)])  15.6 us
    pallas_call x14, Pallas kernels, call(): pl.pallas_call(kernel, out_shape=out_shape, in_specs=[into] * len(operand...  11.1 us
  transfers between devices with their start and end apart: 25, of which 13 were waited for; matrix products, arithmetic and copies ran while one was open for 0% of the time, Pallas kernels for 16%

profile of v5, /device:TPU:0, one launch (start us, length us, event | category | flops | bytes accessed | tf_op | source)
XLA Modules:
  0.0 51.2 jit_solution(15132126861996537843)
XLA Ops:
  0.6 1.6 %pack.1 = (bf16[2,272,128]{2,1,0:T(8,128)(2,1)S(1)}, bf16[2,272,128]{2,1,0:T(8,128)(2,1)S(1)}, bf16[2,272,128]{2,1,0:T(8,128)(2,1)S(1)}, bf16[2,272,128]{2,1,0:T(8,128)(2,1)S(1)}) custom-call(bf16[8,128,256]{2,1,0:T(8,128)(2,1)} %bitcast.5, s32[8,128]{1,0:T(8,128)} %bitcast.3), custom_call_target="tpu_custom_call" | custom-call | tf_op jit(solution)/shard_map/pack/pallas_call | solution.py:383
  2.3 3.0 %collective-permute-start = (bf16[2,272,128]{2,1,0:T(8,128)(2,1)S(1)}, bf16[2,272,128]{2,1,0:T(8,128)(2,1)S(1)}, u32[]{:S(2)}, u32[]{:S(2)}) collective-permute-start(bf16[2,272,128]{2,1,0:T(8,128)(2,1)S(1)} %get-tuple-element.33), channel_id=1, source_target_pairs={{0,8},{4,12},{8,0},{12,4},{16,24},{20,28},{24,16},{28,20},{1,9},{5... | collective-permute-start | bytes 417800 | tf_op jit(solution)/shard_map/ppermute | solution.py:405
  5.3 1.5 %collective-permute-start.1 = (bf16[2,272,128]{2,1,0:T(8,128)(2,1)S(1)}, bf16[2,272,128]{2,1,0:T(8,128)(2,1)S(1)}, u32[]{:S(2)}, u32[]{:S(2)}) collective-permute-start(bf16[2,272,128]{2,1,0:T(8,128)(2,1)S(1)} %get-tuple-element.34), channel_id=1, source_target_pairs={{0,16},{4,20},{8,24},{12,28},{16,0},{20,4},{24,8},{28,12},{1,17},{... | collective-permute-start | bytes 417800 | tf_op jit(solution)/shard_map/ppermute | solution.py:405
  6.8 0.0 collective-permute-start.2
  6.8 3.0 %collective-permute-start.5 = (bf16[128,512]{1,0:T(8,128)(2,1)}, bf16[128,512]{1,0:T(8,128)(2,1)S(1)}, u32[]{:S(2)}, u32[]{:S(2)}) collective-permute-start(bf16[128,512]{1,0:T(8,128)(2,1)} %refs_0_.3), channel_id=1, source_target_pairs={{0,2},{1,3},{2,0},{3,1},{4,6},{5,7},{6,4},{7,5},{8,10},{9,11},{10,... | collective-permute-start | bytes 393224 | tf_op jit(solution)/shard_map/ppermute | solution.py:405
  9.9 1.6 %collective-permute-start.6 = (bf16[128,512]{1,0:T(8,128)(2,1)}, bf16[128,512]{1,0:T(8,128)(2,1)S(1)}, u32[]{:S(2)}, u32[]{:S(2)}) collective-permute-start(bf16[128,512]{1,0:T(8,128)(2,1)} %refs_0_.3), channel_id=1, source_target_pairs={{0,1},{1,0},{2,3},{3,2},{4,5},{5,4},{6,7},{7,6},{8,9},{9,8},{10,11... | collective-permute-start | bytes 393224 | tf_op jit(solution)/shard_map/ppermute | solution.py:405
  11.5 1.9 %collective-permute-done.1.refs_2_ = bf16[2,272,128]{2,1,0:T(8,128)(2,1)S(1)} collective-permute-done((bf16[2,272,128]{2,1,0:T(8,128)(2,1)S(1)}, bf16[2,272,128]{2,1,0:T(8,128)(2,1)S(1)}, u32[]{:S(2)}, u32[]{:S(2)}) %collective-permute-start.1) | collective-permute-done | bytes 139296 | tf_op jit(solution)/shard_map/ppermute | solution.py:405
  13.4 0.0 copy-start.1
  13.4 0.1 collective-permute-start.3
  13.5 0.5 collective-permute-start.4
  14.0 1.6 %collective-permute-done.5.came_ref.refs_2_ = bf16[128,512]{1,0:T(8,128)(2,1)S(1)} collective-permute-done((bf16[128,512]{1,0:T(8,128)(2,1)}, bf16[128,512]{1,0:T(8,128)(2,1)S(1)}, u32[]{:S(2)}, u32[]{:S(2)}) %collective-permute-start.5) | collective-permute-done | bytes 131104 | tf_op jit(solution)/shard_map/ppermute | solution.py:405
  15.7 0.2 collective-permute-done.6.refs_0_.refs_1_
  15.9 0.0 copy-start
  15.9 0.0 copy-start.2
  15.9 0.0 copy-start.5
  15.9 1.5 %collective-permute-start.7 = (bf16[128,512]{1,0:T(8,128)(2,1)S(1)}, bf16[128,512]{1,0:T(8,128)(2,1)S(1)}, u32[]{:S(2)}, u32[]{:S(2)}) collective-permute-start(bf16[128,512]{1,0:T(8,128)(2,1)S(1)} %relay.1), channel_id=1, source_target_pairs={{0,1},{1,0},{2,3},{3,2},{4,5},{5,4},{6,7},{7,6},{8,9},{9,8},{10,11... | collective-permute-start | bytes 393224 | tf_op jit(solution)/shard_map/ppermute | solution.py:405
  17.4 2.8 %forward_mix.1 = (bf16[8,32,128]{2,1,0:T(8,128)(2,1)S(1)}, bf16[8,16,128]{2,1,0:T(8,128)(2,1)S(1)}) custom-call(bf16[10,2,2,128,128]{4,3,2,1,0:T(8,128)(2,1)S(1)} %copy-done.1, bf16[2,272,128]{2,1,0:T(8,128)(2,1)S(1)} %get-tuple-element.32.refs_0_, bf16[2,272,128]{2,1,0:T(8,128)(2,1)S(1)} %collective-permute-done.refs_1_, ...), custom_call_target="tpu_custom_call" | custom-call | tf_op jit(solution)/shard_map/forward_mix/pallas_call | solution.py:383
  20.3 0.3 early_cotangent.1.early_ref
  20.6 0.3 collective-permute-done.7.refs_3_
  20.9 0.4 cotangent.1
  21.3 0.1 collective-permute-start.21
  21.4 1.6 %collective-permute-start.8 = (bf16[2,64,128]{2,1,0:T(8,128)(2,1)S(1)}, bf16[2,64,128]{2,1,0:T(8,128)(2,1)S(1)}, u32[]{:S(2)}, u32[]{:S(2)}) collective-permute-start(bf16[2,64,128]{2,1,0:T(8,128)(2,1)S(1)} %get-tuple-element.41), channel_id=1, source_target_pairs={{0,8},{4,12},{8,0},{12,4},{16,24},{20,28},{24,16},{28,20},{1,9},{5... | collective-permute-start | bytes 98312 | tf_op jit(solution)/shard_map/ppermute | solution.py:405
  23.0 1.5 %collective-permute-start.9 = (bf16[2,64,128]{2,1,0:T(8,128)(2,1)S(1)}, bf16[2,64,128]{2,1,0:T(8,128)(2,1)S(1)}, u32[]{:S(2)}, u32[]{:S(2)}) collective-permute-start(bf16[2,64,128]{2,1,0:T(8,128)(2,1)S(1)} %get-tuple-element.42), channel_id=1, source_target_pairs={{0,16},{4,20},{8,24},{12,28},{16,0},{20,4},{24,8},{28,12},{1,17},{... | collective-permute-start | bytes 98312 | tf_op jit(solution)/shard_map/ppermute | solution.py:405
  24.6 0.4 collective-permute-start.10
  25.0 0.4 collective-permute-done.8.refs_1_.refs_5_
  25.4 0.1 collective-permute-start.12
  25.5 1.5 %collective-permute-done.9.refs_2_.refs_6_ = bf16[2,64,128]{2,1,0:T(8,128)(2,1)S(1)} collective-permute-done((bf16[2,64,128]{2,1,0:T(8,128)(2,1)S(1)}, bf16[2,64,128]{2,1,0:T(8,128)(2,1)S(1)}, u32[]{:S(2)}, u32[]{:S(2)}) %collective-permute-start.9) | collective-permute-done | bytes 32800 | tf_op jit(solution)/shard_map/ppermute | solution.py:405
  26.9 2.4 %collective-permute-done.10.refs_3_.refs_7_ = bf16[2,64,128]{2,1,0:T(8,128)(2,1)S(1)} collective-permute-done((bf16[2,64,128]{2,1,0:T(8,128)(2,1)S(1)}, bf16[2,64,128]{2,1,0:T(8,128)(2,1)S(1)}, u32[]{:S(2)}, u32[]{:S(2)}) %collective-permute-start.10) | collective-permute-done | bytes 32800 | tf_op jit(solution)/shard_map/ppermute | solution.py:405
  29.4 1.2 %collective-permute-done.14.refs_7_.refs_11_ = bf16[2,64,128]{2,1,0:T(8,128)(2,1)S(1)} collective-permute-done((bf16[2,64,128]{2,1,0:T(8,128)(2,1)S(1)}, bf16[2,64,128]{2,1,0:T(8,128)(2,1)S(1)}, u32[]{:S(2)}, u32[]{:S(2)}) %collective-permute-start.14) | collective-permute-done | bytes 32800 | tf_op jit(solution)/shard_map/ppermute | solution.py:405
  30.6 1.1 %project.1 = (bf16[128,512]{1,0:T(8,128)(2,1)}, bf16[128,512]{1,0:T(8,128)(2,1)}, bf16[2,128,512]{2,1,0:T(8,128)(2,1)}) custom-call(bf16[256,2048]{1,0:T(8,128)(2,1)S(1)} %copy-done, bf16[2,64,128]{2,1,0:T(8,128)(2,1)S(1)} %get-tuple-element.40.refs_0_.refs_4_, bf16[2,64,128]{2,1,0:T(8,128)(2,1)S(1)} %collective-permute-done.8.refs_1_.refs_5_, ...), custom_call_target="tpu_custom_call" | custom-call | tf_op jit(solution)/shard_map/project/pallas_call | solution.py:383
  31.6 1.5 %collective-permute-start.20 = (bf16[2,128,512]{2,1,0:T(8,128)(2,1)}, bf16[2,128,512]{2,1,0:T(8,128)(2,1)S(1)}, u32[]{:S(2)}, u32[]{:S(2)}) collective-permute-start(bf16[2,128,512]{2,1,0:T(8,128)(2,1)} %get-tuple-element.49), channel_id=1, source_target_pairs={{0,1},{1,0},{2,3},{3,2},{4,5},{5,4},{6,7},{7,6},{8,9},{9,8},{10,11... | collective-permute-start | bytes 786440 | tf_op jit(solution)/shard_map/ppermute | solution.py:405
  33.1 1.1 %projector_gradient.1 = (bf16[2,256,256]{2,1,0:T(8,128)(2,1)}, bf16[2,256,256]{2,1,0:T(8,128)(2,1)}) custom-call(bf16[128,1024]{1,0:T(8,128)(2,1)S(1)} %collective-permute-done.21.came_ref, bf16[128,512]{1,0:T(8,128)(2,1)S(1)} %copy-done.2, bf16[128,512]{1,0:T(8,128)(2,1)S(1)} %collective-permute-done.6.refs_0_.refs_1_, ...), custom_call_target="tpu_custom_call" | custom-call | tf_op jit(solution)/shard_map/projector_gradient/pallas_call | solution.py:383
  34.2 0.0 copy-start.3
  34.3 0.6 %collective-permute-start.23 = (bf16[2,256,256]{2,1,0:T(8,128)(2,1)}, bf16[2,256,256]{2,1,0:T(8,128)(2,1)S(1)}, u32[]{:S(2)}, u32[]{:S(2)}) collective-permute-start(bf16[2,256,256]{2,1,0:T(8,128)(2,1)} %get-tuple-element.55), channel_id=1, source_target_pairs={{0,8},{4,12},{8,0},{12,4},{16,24},{20,28},{24,16},{28,20},{1,9},{5... | collective-permute-start | bytes 786440 | tf_op jit(solution)/shard_map/ppermute | solution.py:405
  34.9 2.5 %backward_mix.1 = (bf16[16,32,128]{2,1,0:T(8,128)(2,1)S(1)}, bf16[16,32,128]{2,1,0:T(8,128)(2,1)S(1)}, bf16[16,32,128]{2,1,0:T(8,128)(2,1)S(1)}, bf16[16,32,128]{2,1,0:T(8,128)(2,1)S(1)}) custom-call(bf16[10,2,2,128,128]{4,3,2,1,0:T(8,128)(2,1)S(1)} %copy-done.1, bf16[8,16,128]{2,1,0:T(8,128)(2,1)S(1)} %get-tuple-element.36.map_ref, ...), custom_call_target="tpu_custom_call" | custom-call | tf_op jit(solution)/shard_map/backward_mix/pallas_call | solution.py:383
  37.3 1.6 %collective-permute-start.15 = (bf16[16,32,128]{2,1,0:T(8,128)(2,1)S(1)}, bf16[16,32,128]{2,1,0:T(8,128)(2,1)S(1)}, u32[]{:S(2)}, u32[]{:S(2)}) collective-permute-start(bf16[16,32,128]{2,1,0:T(8,128)(2,1)S(1)} %get-tuple-element.45), channel_id=1, source_target_pairs={{0,8},{4,12},{8,0},{12,4},{16,24},{20,28},{24,16},{28,20},{1,9},{5... | collective-permute-start | bytes 393224 | tf_op jit(solution)/shard_map/ppermute | solution.py:405
  38.9 0.5 collective-permute-start.16
  39.4 1.5 %collective-permute-start.17 = (bf16[16,32,128]{2,1,0:T(8,128)(2,1)S(1)}, bf16[16,32,128]{2,1,0:T(8,128)(2,1)S(1)}, u32[]{:S(2)}, u32[]{:S(2)}) collective-permute-start(bf16[16,32,128]{2,1,0:T(8,128)(2,1)S(1)} %get-tuple-element.47), channel_id=1, source_target_pairs={{0,24},{4,28},{8,16},{12,20},{16,8},{20,12},{24,0},{28,4},{1,25},{... | collective-permute-start | bytes 393224 | tf_op jit(solution)/shard_map/ppermute | solution.py:405
  40.9 2.4 %collective-permute-start.22 = (bf16[128,512]{1,0:T(8,128)(2,1)S(1)}, bf16[128,512]{1,0:T(8,128)(2,1)S(1)}, u32[]{:S(2)}, u32[]{:S(2)}) collective-permute-start(bf16[128,512]{1,0:T(8,128)(2,1)S(1)} %fold_shares.1), channel_id=1, source_target_pairs={{0,2},{1,3},{2,0},{3,1},{4,6},{5,7},{6,4},{7,5},{8,10},{9,11},{10,... | collective-permute-start | bytes 393224 | tf_op jit(solution)/shard_map/ppermute | solution.py:405
  43.4 0.4 collective-permute-done.23.came_ref.refs_8_
  43.8 0.6 %collective-permute-start.24 = (bf16[256,256]{1,0:T(8,128)(2,1)S(1)}, bf16[256,256]{1,0:T(8,128)(2,1)S(1)}, u32[]{:S(2)}, u32[]{:S(2)}) collective-permute-start(bf16[256,256]{1,0:T(8,128)(2,1)S(1)} %fold_parts.1), channel_id=1, source_target_pairs={{0,16},{4,20},{8,24},{12,28},{16,0},{20,4},{24,8},{28,12},{1,17},{... | collective-permute-start | bytes 393224 | tf_op jit(solution)/shard_map/ppermute | solution.py:405
  44.3 2.2 %collective-permute-done.15.refs_1_ = bf16[16,32,128]{2,1,0:T(8,128)(2,1)S(1)} collective-permute-done((bf16[16,32,128]{2,1,0:T(8,128)(2,1)S(1)}, bf16[16,32,128]{2,1,0:T(8,128)(2,1)S(1)}, u32[]{:S(2)}, u32[]{:S(2)}) %collective-permute-start.15) | collective-permute-done | bytes 131104 | tf_op jit(solution)/shard_map/ppermute | solution.py:405
  46.6 0.1 collective-permute-start.18
  46.6 1.7 %collective-permute-done.17.refs_3_ = bf16[16,32,128]{2,1,0:T(8,128)(2,1)S(1)} collective-permute-done((bf16[16,32,128]{2,1,0:T(8,128)(2,1)S(1)}, bf16[16,32,128]{2,1,0:T(8,128)(2,1)S(1)}, u32[]{:S(2)}, u32[]{:S(2)}) %collective-permute-start.17) | collective-permute-done | bytes 131104 | tf_op jit(solution)/shard_map/ppermute | solution.py:405
  48.3 0.6 %collective-permute-done.22.share_ref = bf16[128,512]{1,0:T(8,128)(2,1)S(1)} collective-permute-done((bf16[128,512]{1,0:T(8,128)(2,1)S(1)}, bf16[128,512]{1,0:T(8,128)(2,1)S(1)}, u32[]{:S(2)}, u32[]{:S(2)}) %collective-permute-start.22) | collective-permute-done | bytes 131104 | tf_op jit(solution)/shard_map/ppermute | solution.py:405
  48.9 1.2 %collective-permute-done.24.part_ref = bf16[256,256]{1,0:T(8,128)(2,1)S(1)} collective-permute-done((bf16[256,256]{1,0:T(8,128)(2,1)S(1)}, bf16[256,256]{1,0:T(8,128)(2,1)S(1)}, u32[]{:S(2)}, u32[]{:S(2)}) %collective-permute-start.24) | collective-permute-done | bytes 131104 | tf_op jit(solution)/shard_map/ppermute | solution.py:405
  50.0 0.1 arrive.1
  50.1 1.1 %finish.1 = (bf16[8,128,256]{2,1,0:T(8,128)(2,1)}, bf16[128,512]{1,0:T(8,128)(2,1)}, f32[256,256]{1,0:T(8,128)}) custom-call(bf16[16,32,128]{2,1,0:T(8,128)(2,1)S(1)} %get-tuple-element.44.refs_0_, bf16[16,32,128]{2,1,0:T(8,128)(2,1)S(1)} %collective-permute-done.15.refs_1_, bf16[16,32,128]{2,1,0:T(8,128)(2,1)S(1)} %collective-permute-done.16.refs_2_, ...), custom_call_target="tpu_custom_call" | custom-call | tf_op jit(solution)/shard_map/finish/pallas_call | solution.py:383
  (30 shorter events, 0.2 us)
Async XLA Ops:
  2.3 9.2 %collective-permute-start = (bf16[2,272,128]{2,1,0:T(8,128)(2,1)S(1)}, bf16[2,272,128]{2,1,0:T(8,128)(2,1)S(1)}, u32[]{:S(2)}, u32[]{:S(2)}) collective-permute-start(bf16[2,272,128]{2,1,0:T(8,128)(2,1)S(1)} %get-tuple-element.33), channel_id=1, source_target_pairs={{0,8},{4,12},{8,0},{12,4},{16,24},{20,28},{24,16},{28,20},{1,9},{5... | collective-permute-start | bytes 417800 | tf_op jit(solution)/shard_map/ppermute | solution.py:405
  5.3 8.1 %collective-permute-start.1 = (bf16[2,272,128]{2,1,0:T(8,128)(2,1)S(1)}, bf16[2,272,128]{2,1,0:T(8,128)(2,1)S(1)}, u32[]{:S(2)}, u32[]{:S(2)}) collective-permute-start(bf16[2,272,128]{2,1,0:T(8,128)(2,1)S(1)} %get-tuple-element.34), channel_id=1, source_target_pairs={{0,16},{4,20},{8,24},{12,28},{16,0},{20,4},{24,8},{28,12},{1,17},{... | collective-permute-start | bytes 417800 | tf_op jit(solution)/shard_map/ppermute | solution.py:405
  6.8 6.7 %collective-permute-start.2 = (bf16[2,272,128]{2,1,0:T(8,128)(2,1)S(1)}, bf16[2,272,128]{2,1,0:T(8,128)(2,1)S(1)}, u32[]{:S(2)}, u32[]{:S(2)}) collective-permute-start(bf16[2,272,128]{2,1,0:T(8,128)(2,1)S(1)} %get-tuple-element.35), channel_id=1, source_target_pairs={{0,24},{4,28},{8,16},{12,20},{16,8},{20,12},{24,0},{28,4},{1,25},{... | collective-permute-start | bytes 417800 | tf_op jit(solution)/shard_map/ppermute | solution.py:405
  6.8 8.8 %collective-permute-start.5 = (bf16[128,512]{1,0:T(8,128)(2,1)}, bf16[128,512]{1,0:T(8,128)(2,1)S(1)}, u32[]{:S(2)}, u32[]{:S(2)}) collective-permute-start(bf16[128,512]{1,0:T(8,128)(2,1)} %refs_0_.3), channel_id=1, source_target_pairs={{0,2},{1,3},{2,0},{3,1},{4,6},{5,7},{6,4},{7,5},{8,10},{9,11},{10,... | collective-permute-start | bytes 393224 | tf_op jit(solution)/shard_map/ppermute | solution.py:405
  9.9 6.0 %collective-permute-start.6 = (bf16[128,512]{1,0:T(8,128)(2,1)}, bf16[128,512]{1,0:T(8,128)(2,1)S(1)}, u32[]{:S(2)}, u32[]{:S(2)}) collective-permute-start(bf16[128,512]{1,0:T(8,128)(2,1)} %refs_0_.3), channel_id=1, source_target_pairs={{0,1},{1,0},{2,3},{3,2},{4,5},{5,4},{6,7},{7,6},{8,9},{9,8},{10,11... | collective-permute-start | bytes 393224 | tf_op jit(solution)/shard_map/ppermute | solution.py:405
  13.4 4.0 %copy-start.1 = (bf16[10,2,2,128,128]{4,3,2,1,0:T(8,128)(2,1)S(1)}, bf16[10,2,2,128,128]{4,3,2,1,0:T(8,128)(2,1)}, u32[]{:S(2)}) copy-start(bf16[10,2,2,128,128]{4,3,2,1,0:T(8,128)(2,1)} %mix_ref.3) | copy-start | bytes 3932164
  13.4 4.0 %collective-permute-start.3 = (bf16[3,1,272,128]{3,2,1,0:T(8,128)(2,1)S(1)}, bf16[3,1,272,128]{3,2,1,0:T(8,128)(2,1)S(1)}, u32[]{:S(2)}, u32[]{:S(2)}) collective-permute-start(bf16[3,1,272,128]{3,2,1,0:T(8,128)(2,1)S(1)} %gather.2), channel_id=1, source_target_pairs={{0,4},{4,0},{8,12},{12,8},{16,20},{20,16},{24,28},{28,24},{1,5},{5... | collective-permute-start | bytes 626696 | tf_op jit(solution)/shard_map/ppermute | solution.py:405
  13.5 3.9 %collective-permute-start.4 = (bf16[2,272,128]{2,1,0:T(8,128)(2,1)S(1)}, bf16[2,272,128]{2,1,0:T(8,128)(2,1)S(1)}, u32[]{:S(2)}, u32[]{:S(2)}) collective-permute-start(bf16[2,272,128]{2,1,0:T(8,128)(2,1)S(1)} %collective-permute-done.2.refs_3_), channel_id=1, source_target_pairs={{0,4},{4,0},{8,12},{12,8},{16,20},{20,16},{24,28},{28,24},{1,5},{5... | collective-permute-start | bytes 417800 | tf_op jit(solution)/shard_map/ppermute | solution.py:405
  15.9 4.4 %copy-start = (bf16[256,2048]{1,0:T(8,128)(2,1)S(1)}, bf16[256,2048]{1,0:T(8,128)(2,1)}, u32[]{:S(2)}) copy-start(bf16[256,2048]{1,0:T(8,128)(2,1)} %w_ref.5) | copy-start | bytes 3145732
  15.9 4.4 %copy-start.2 = (bf16[128,512]{1,0:T(8,128)(2,1)S(1)}, bf16[128,512]{1,0:T(8,128)(2,1)}, u32[]{:S(2)}) copy-start(bf16[128,512]{1,0:T(8,128)(2,1)} %refs_0_.3) | copy-start | bytes 393220
  15.9 5.0 %copy-start.5 = (s32[1024]{0:T(1024)S(1)}, s32[1024]{0:T(1024)}, u32[]{:S(2)}) copy-start(s32[1024]{0:T(1024)} %param.8) | copy-start | bytes 12292
  15.9 5.0 %collective-permute-start.7 = (bf16[128,512]{1,0:T(8,128)(2,1)S(1)}, bf16[128,512]{1,0:T(8,128)(2,1)S(1)}, u32[]{:S(2)}, u32[]{:S(2)}) collective-permute-start(bf16[128,512]{1,0:T(8,128)(2,1)S(1)} %relay.1), channel_id=1, source_target_pairs={{0,1},{1,0},{2,3},{3,2},{4,5},{5,4},{6,7},{7,6},{8,9},{9,8},{10,11... | collective-permute-start | bytes 393224 | tf_op jit(solution)/shard_map/ppermute | solution.py:405
  21.3 11.7 %collective-permute-start.21 = (bf16[128,1024]{1,0:T(8,128)(2,1)S(1)}, bf16[128,1024]{1,0:T(8,128)(2,1)S(1)}, u32[]{:S(2)}, u32[]{:S(2)}) collective-permute-start(bf16[128,1024]{1,0:T(8,128)(2,1)S(1)} %get-tuple-element.50), channel_id=1, source_target_pairs={{0,4},{4,0},{8,12},{12,8},{16,20},{20,16},{24,28},{28,24},{1,5},{5... | collective-permute-start | bytes 786440 | tf_op jit(solution)/shard_map/ppermute | solution.py:405
  21.4 4.0 %collective-permute-start.8 = (bf16[2,64,128]{2,1,0:T(8,128)(2,1)S(1)}, bf16[2,64,128]{2,1,0:T(8,128)(2,1)S(1)}, u32[]{:S(2)}, u32[]{:S(2)}) collective-permute-start(bf16[2,64,128]{2,1,0:T(8,128)(2,1)S(1)} %get-tuple-element.41), channel_id=1, source_target_pairs={{0,8},{4,12},{8,0},{12,4},{16,24},{20,28},{24,16},{28,20},{1,9},{5... | collective-permute-start | bytes 98312 | tf_op jit(solution)/shard_map/ppermute | solution.py:405
  23.0 3.9 %collective-permute-start.9 = (bf16[2,64,128]{2,1,0:T(8,128)(2,1)S(1)}, bf16[2,64,128]{2,1,0:T(8,128)(2,1)S(1)}, u32[]{:S(2)}, u32[]{:S(2)}) collective-permute-start(bf16[2,64,128]{2,1,0:T(8,128)(2,1)S(1)} %get-tuple-element.42), channel_id=1, source_target_pairs={{0,16},{4,20},{8,24},{12,28},{16,0},{20,4},{24,8},{28,12},{1,17},{... | collective-permute-start | bytes 98312 | tf_op jit(solution)/shard_map/ppermute | solution.py:405
  24.6 4.8 %collective-permute-start.10 = (bf16[2,64,128]{2,1,0:T(8,128)(2,1)S(1)}, bf16[2,64,128]{2,1,0:T(8,128)(2,1)S(1)}, u32[]{:S(2)}, u32[]{:S(2)}) collective-permute-start(bf16[2,64,128]{2,1,0:T(8,128)(2,1)S(1)} %get-tuple-element.43), channel_id=1, source_target_pairs={{0,24},{4,28},{8,16},{12,20},{16,8},{20,12},{24,0},{28,4},{1,25},{... | collective-permute-start | bytes 98312 | tf_op jit(solution)/shard_map/ppermute | solution.py:405
  25.0 4.4 %collective-permute-start.11 = (bf16[2,64,128]{2,1,0:T(8,128)(2,1)S(1)}, bf16[2,64,128]{2,1,0:T(8,128)(2,1)S(1)}, u32[]{:S(2)}, u32[]{:S(2)}) collective-permute-start(bf16[2,64,128]{2,1,0:T(8,128)(2,1)S(1)} %get-tuple-element.40.refs_0_.refs_4_), channel_id=1, source_target_pairs={{0,4},{4,0},{8,12},{12,8},{16,20},{20,16},{24,28},{28,24},{1,5},{5... | collective-permute-start | bytes 98312 | tf_op jit(solution)/shard_map/ppermute | solution.py:405
  25.4 4.0 %collective-permute-start.12 = (bf16[2,64,128]{2,1,0:T(8,128)(2,1)S(1)}, bf16[2,64,128]{2,1,0:T(8,128)(2,1)S(1)}, u32[]{:S(2)}, u32[]{:S(2)}) collective-permute-start(bf16[2,64,128]{2,1,0:T(8,128)(2,1)S(1)} %collective-permute-done.8.refs_1_.refs_5_), channel_id=1, source_target_pairs={{0,4},{4,0},{8,12},{12,8},{16,20},{20,16},{24,28},{28,24},{1,5},{5... | collective-permute-start | bytes 98312 | tf_op jit(solution)/shard_map/ppermute | solution.py:405
  26.9 2.4 %collective-permute-start.13 = (bf16[2,64,128]{2,1,0:T(8,128)(2,1)S(1)}, bf16[2,64,128]{2,1,0:T(8,128)(2,1)S(1)}, u32[]{:S(2)}, u32[]{:S(2)}) collective-permute-start(bf16[2,64,128]{2,1,0:T(8,128)(2,1)S(1)} %collective-permute-done.9.refs_2_.refs_6_), channel_id=1, source_target_pairs={{0,4},{4,0},{8,12},{12,8},{16,20},{20,16},{24,28},{28,24},{1,5},{5... | collective-permute-start | bytes 98312 | tf_op jit(solution)/shard_map/ppermute | solution.py:405
  29.4 1.2 %collective-permute-start.14 = (bf16[2,64,128]{2,1,0:T(8,128)(2,1)S(1)}, bf16[2,64,128]{2,1,0:T(8,128)(2,1)S(1)}, u32[]{:S(2)}, u32[]{:S(2)}) collective-permute-start(bf16[2,64,128]{2,1,0:T(8,128)(2,1)S(1)} %collective-permute-done.10.refs_3_.refs_7_), channel_id=1, source_target_pairs={{0,4},{4,0},{8,12},{12,8},{16,20},{20,16},{24,28},{28,24},{1,5},{5... | collective-permute-start | bytes 98312 | tf_op jit(solution)/shard_map/ppermute | solution.py:405
  31.6 9.2 %collective-permute-start.20 = (bf16[2,128,512]{2,1,0:T(8,128)(2,1)}, bf16[2,128,512]{2,1,0:T(8,128)(2,1)S(1)}, u32[]{:S(2)}, u32[]{:S(2)}) collective-permute-start(bf16[2,128,512]{2,1,0:T(8,128)(2,1)} %get-tuple-element.49), channel_id=1, source_target_pairs={{0,1},{1,0},{2,3},{3,2},{4,5},{5,4},{6,7},{7,6},{8,9},{9,8},{10,11... | collective-permute-start | bytes 786440 | tf_op jit(solution)/shard_map/ppermute | solution.py:405
  33.1 7.8 %copy-start.4 = (bf16[128,512]{1,0:T(8,128)(2,1)S(1)}, bf16[128,512]{1,0:T(8,128)(2,1)}, u32[]{:S(2)}) copy-start(bf16[128,512]{1,0:T(8,128)(2,1)} %get-tuple-element.52.kept_ref) | copy-start | bytes 393220
  34.2 9.5 %copy-start.3 = (bf16[2,256,256]{2,1,0:T(8,128)(2,1)S(1)}, bf16[2,256,256]{2,1,0:T(8,128)(2,1)}, u32[]{:S(2)}) copy-start(bf16[2,256,256]{2,1,0:T(8,128)(2,1)} %get-tuple-element.54.held_ref.refs_7_) | copy-start | bytes 786436
  34.3 9.5 %collective-permute-start.23 = (bf16[2,256,256]{2,1,0:T(8,128)(2,1)}, bf16[2,256,256]{2,1,0:T(8,128)(2,1)S(1)}, u32[]{:S(2)}, u32[]{:S(2)}) collective-permute-start(bf16[2,256,256]{2,1,0:T(8,128)(2,1)} %get-tuple-element.55), channel_id=1, source_target_pairs={{0,8},{4,12},{8,0},{12,4},{16,24},{20,28},{24,16},{28,20},{1,9},{5... | collective-permute-start | bytes 786440 | tf_op jit(solution)/shard_map/ppermute | solution.py:405
  34.9 15.2 %copy-start.6 = (bf16[128,512]{1,0:T(8,128)(2,1)S(1)}, bf16[128,512]{1,0:T(8,128)(2,1)}, u32[]{:S(2)}) copy-start(bf16[128,512]{1,0:T(8,128)(2,1)} %get-tuple-element.48.kept_ref) | copy-start | bytes 393220
  37.3 9.2 %collective-permute-start.15 = (bf16[16,32,128]{2,1,0:T(8,128)(2,1)S(1)}, bf16[16,32,128]{2,1,0:T(8,128)(2,1)S(1)}, u32[]{:S(2)}, u32[]{:S(2)}) collective-permute-start(bf16[16,32,128]{2,1,0:T(8,128)(2,1)S(1)} %get-tuple-element.45), channel_id=1, source_target_pairs={{0,8},{4,12},{8,0},{12,4},{16,24},{20,28},{24,16},{28,20},{1,9},{5... | collective-permute-start | bytes 393224 | tf_op jit(solution)/shard_map/ppermute | solution.py:405
  38.9 7.7 %collective-permute-start.16 = (bf16[16,32,128]{2,1,0:T(8,128)(2,1)S(1)}, bf16[16,32,128]{2,1,0:T(8,128)(2,1)S(1)}, u32[]{:S(2)}, u32[]{:S(2)}) collective-permute-start(bf16[16,32,128]{2,1,0:T(8,128)(2,1)S(1)} %get-tuple-element.46), channel_id=1, source_target_pairs={{0,16},{4,20},{8,24},{12,28},{16,0},{20,4},{24,8},{28,12},{1,17},{... | collective-permute-start | bytes 393224 | tf_op jit(solution)/shard_map/ppermute | solution.py:405
  39.4 8.9 %collective-permute-start.17 = (bf16[16,32,128]{2,1,0:T(8,128)(2,1)S(1)}, bf16[16,32,128]{2,1,0:T(8,128)(2,1)S(1)}, u32[]{:S(2)}, u32[]{:S(2)}) collective-permute-start(bf16[16,32,128]{2,1,0:T(8,128)(2,1)S(1)} %get-tuple-element.47), channel_id=1, source_target_pairs={{0,24},{4,28},{8,16},{12,20},{16,8},{20,12},{24,0},{28,4},{1,25},{... | collective-permute-start | bytes 393224 | tf_op jit(solution)/shard_map/ppermute | solution.py:405
  40.9 7.9 %collective-permute-start.22 = (bf16[128,512]{1,0:T(8,128)(2,1)S(1)}, bf16[128,512]{1,0:T(8,128)(2,1)S(1)}, u32[]{:S(2)}, u32[]{:S(2)}) collective-permute-start(bf16[128,512]{1,0:T(8,128)(2,1)S(1)} %fold_shares.1), channel_id=1, source_target_pairs={{0,2},{1,3},{2,0},{3,1},{4,6},{5,7},{6,4},{7,5},{8,10},{9,11},{10,... | collective-permute-start | bytes 393224 | tf_op jit(solution)/shard_map/ppermute | solution.py:405
  43.8 6.3 %collective-permute-start.24 = (bf16[256,256]{1,0:T(8,128)(2,1)S(1)}, bf16[256,256]{1,0:T(8,128)(2,1)S(1)}, u32[]{:S(2)}, u32[]{:S(2)}) collective-permute-start(bf16[256,256]{1,0:T(8,128)(2,1)S(1)} %fold_parts.1), channel_id=1, source_target_pairs={{0,16},{4,20},{8,24},{12,28},{16,0},{20,4},{24,8},{28,12},{1,17},{... | collective-permute-start | bytes 393224 | tf_op jit(solution)/shard_map/ppermute | solution.py:405
  46.6 3.5 %collective-permute-start.18 = (bf16[3,8,32,128]{3,2,1,0:T(8,128)(2,1)S(1)}, bf16[3,8,32,128]{3,2,1,0:T(8,128)(2,1)S(1)}, u32[]{:S(2)}, u32[]{:S(2)}) collective-permute-start(bf16[3,8,32,128]{3,2,1,0:T(8,128)(2,1)S(1)} %gather.3), channel_id=1, source_target_pairs={{0,4},{4,0},{8,12},{12,8},{16,20},{20,16},{24,28},{28,24},{1,5},{5... | collective-permute-start | bytes 589832 | tf_op jit(solution)/shard_map/ppermute | solution.py:405
  48.3 1.8 %collective-permute-start.19 = (bf16[16,32,128]{2,1,0:T(8,128)(2,1)S(1)}, bf16[16,32,128]{2,1,0:T(8,128)(2,1)S(1)}, u32[]{:S(2)}, u32[]{:S(2)}) collective-permute-start(bf16[16,32,128]{2,1,0:T(8,128)(2,1)S(1)} %collective-permute-done.17.refs_3_), channel_id=1, source_target_pairs={{0,4},{4,0},{8,12},{12,8},{16,20},{20,16},{24,28},{28,24},{1,5},{5... | collective-permute-start | bytes 393224 | tf_op jit(solution)/shard_map/ppermute | solution.py:405

commit v6 on v5

--- a/solution.py
+++ b/solution.py
@@ -290,28 +290,23 @@
 
 
 def project_kernel(w_ref, *refs):
-    pieces, (kept_ref, passed_ref, sent_ref, share_ref, pool_ref, sems) = refs[:8], refs[8:]
+    pieces, (kept_ref, passed_ref, sent_ref, pool_ref) = refs[:8], refs[8:]
     feats = pieces[0].shape[1] // 2
-    outs_tp = share_ref.shape[2]
+    outs_tp = kept_ref.shape[1]
     place = lax.axis_index("tp")
     targets = [kept_ref, sent_ref.at[0], passed_ref, sent_ref.at[1]]
     for g, piece, at in sources(pieces):
         pool_ref[g] = piece[at, feats:, :]
     pooled = jnp.concatenate([pool_ref[g] for g in range(len(pieces))], axis=0).T
-    copies = []
     for o in (3, 1, 2, 0):
         at = pl.multiple_of((place ^ o) * outs_tp, outs_tp)
-        share_ref[o] = lax.dot_general(
+        targets[o][...] = lax.dot_general(
             pooled, w_ref[:, pl.ds(at, outs_tp)], NN, preferred_element_type=F32
         ).astype(BF16)
-        copies.append(pltpu.make_async_copy(share_ref.at[o], targets[o], sems.at[o]))
-        copies[-1].start()
-    for copy in copies:
-        copy.wait()
 
 
 def gradient_kernel(came_ref, *refs):
-    cots, pieces, (held_ref, gone_ref, part_ref, pool_ref, sems) = refs[:4], refs[4:12], refs[-5:]
+    cots, pieces, (held_ref, gone_ref, part_ref, pool_ref) = refs[:4], refs[4:12], refs[12:]
     feats, pool_rows = pieces[0].shape[1] // 2, pieces[0].shape[2]
     outs = came_ref.shape[1] // 4
     place, me = lax.axis_index("tp"), lax.axis_index("tok")
@@ -326,13 +321,8 @@
         part_ref[place ^ o] = lax.dot_general(
             turned, cot, NN, preferred_element_type=F32
         ).astype(BF16)
-    copies = []
-    for o in (1, 3, 0, 2):
-        target = (gone_ref if o % 2 else held_ref).at[o // 2]
-        copies.append(pltpu.make_async_copy(part_ref.at[(me // 2) ^ o], target, sems.at[o]))
-        copies[-1].start()
-    for copy in copies:
-        copy.wait()
+    for o in range(4):
+        (gone_ref if o % 2 else held_ref)[o // 2] = part_ref[(me // 2) ^ o]
 
 
 def fold_shares_kernel(kept_ref, got_ref, share_ref):
@@ -476,27 +466,20 @@
     kept, passed, sent = call(
         project_kernel,
         (proj_weight, *both),
-        [in_hbm(pool_rows, outs_tp)] * 2 + [in_hbm(2, pool_rows, outs_tp)],
-        [
-            pltpu.VMEM((4, pool_rows, outs_tp), BF16),
-            pltpu.VMEM((owners, feats, pool_rows), BF16),
-            pltpu.SemaphoreType.DMA((4,)),
-        ],
+        [struct(pool_rows, outs_tp)] * 2 + [struct(2, pool_rows, outs_tp)],
+        [pltpu.VMEM((owners, feats, pool_rows), BF16)],
         "project",
-        out_space=pltpu.HBM,
     )
     half, passed = lax.optimization_barrier((half, passed))
     held, gone = call(
         gradient_kernel,
         (half, *cots, *both),
-        [in_hbm(2, feats_tp, outs)] * 2,
+        [struct(2, feats_tp, outs)] * 2,
         [
             pltpu.VMEM((4, feats_tp, outs), BF16),
             pltpu.VMEM((owners, feats, 2 * pool_rows), BF16),
-            pltpu.SemaphoreType.DMA((4,)),
         ],
         "projector_gradient",
-        out_space=pltpu.HBM,
     )
     sent, gone = swap(sent, "tp", 1), swap(gone, "tok", 2)
     share = call(

time: 51.4 us -> 49.9 us (0.971)
  Pallas kernels: 11.1 us -> 9.6 us
    pallas_call x14, Pallas kernels: 11.1 us -> 9.6 us  [call(): pl.pallas_call(kernel, out_shape=out_shape, in_specs=[into] * len(operand...]
  transfers between devices with their start and end apart: 25 -> 25, of which waited for: 13 -> 13; matrix products, arithmetic and copies ran while one was open for 0% -> 0% of each run, Pallas kernels for 16% -> 13%
where the time goes in v6:
time: 49.9 us; the launch traced here: 49.7 us
  starting transfers between devices  23.6 us (47%)
  waiting for transfers between devices  15.6 us (31%)
  Pallas kernels  9.6 us (19%)
  between operations  0.84 us (2%)
    ppermute x25, starting transfers between devices, swap(): return lax.ppermute(piece, axis, [(i, i ^ offset) for i in range(size)])  23.6 us
    ppermute x25, waiting for transfers between devices, swap(): return lax.ppermute(piece, axis, [(i, i ^ offset) for i in range(size)])  15.6 us
    pallas_call x14, Pallas kernels, call(): pl.pallas_call(kernel, out_shape=out_shape, in_specs=[into] * len(operand...  9.6 us
  transfers between devices with their start and end apart: 25, of which 13 were waited for; matrix products, arithmetic and copies ran while one was open for 0% of the time, Pallas kernels for 13%

profile of v6, /device:TPU:0, one launch (start us, length us, event | category | flops | bytes accessed | tf_op | source)
XLA Modules:
  0.0 49.7 jit_solution(7696361630566359040)
XLA Ops:
  0.6 1.6 %pack.1 = (bf16[2,272,128]{2,1,0:T(8,128)(2,1)S(1)}, bf16[2,272,128]{2,1,0:T(8,128)(2,1)S(1)}, bf16[2,272,128]{2,1,0:T(8,128)(2,1)S(1)}, bf16[2,272,128]{2,1,0:T(8,128)(2,1)S(1)}) custom-call(bf16[8,128,256]{2,1,0:T(8,128)(2,1)} %bitcast.5, s32[8,128]{1,0:T(8,128)} %bitcast.3), custom_call_target="tpu_custom_call" | custom-call | tf_op jit(solution)/shard_map/pack/pallas_call | solution.py:373
  2.3 3.0 %collective-permute-start = (bf16[2,272,128]{2,1,0:T(8,128)(2,1)S(1)}, bf16[2,272,128]{2,1,0:T(8,128)(2,1)S(1)}, u32[]{:S(2)}, u32[]{:S(2)}) collective-permute-start(bf16[2,272,128]{2,1,0:T(8,128)(2,1)S(1)} %get-tuple-element.33), channel_id=1, source_target_pairs={{0,8},{4,12},{8,0},{12,4},{16,24},{20,28},{24,16},{28,20},{1,9},{5... | collective-permute-start | bytes 417800 | tf_op jit(solution)/shard_map/ppermute | solution.py:395
  5.3 1.5 %collective-permute-start.1 = (bf16[2,272,128]{2,1,0:T(8,128)(2,1)S(1)}, bf16[2,272,128]{2,1,0:T(8,128)(2,1)S(1)}, u32[]{:S(2)}, u32[]{:S(2)}) collective-permute-start(bf16[2,272,128]{2,1,0:T(8,128)(2,1)S(1)} %get-tuple-element.34), channel_id=1, source_target_pairs={{0,16},{4,20},{8,24},{12,28},{16,0},{20,4},{24,8},{28,12},{1,17},{... | collective-permute-start | bytes 417800 | tf_op jit(solution)/shard_map/ppermute | solution.py:395
  6.8 0.0 collective-permute-start.2
  6.8 3.0 %collective-permute-start.5 = (bf16[128,512]{1,0:T(8,128)(2,1)}, bf16[128,512]{1,0:T(8,128)(2,1)S(1)}, u32[]{:S(2)}, u32[]{:S(2)}) collective-permute-start(bf16[128,512]{1,0:T(8,128)(2,1)} %refs_0_.3), channel_id=1, source_target_pairs={{0,2},{1,3},{2,0},{3,1},{4,6},{5,7},{6,4},{7,5},{8,10},{9,11},{10,... | collective-permute-start | bytes 393224 | tf_op jit(solution)/shard_map/ppermute | solution.py:395
  9.9 1.6 %collective-permute-start.6 = (bf16[128,512]{1,0:T(8,128)(2,1)}, bf16[128,512]{1,0:T(8,128)(2,1)S(1)}, u32[]{:S(2)}, u32[]{:S(2)}) collective-permute-start(bf16[128,512]{1,0:T(8,128)(2,1)} %refs_0_.3), channel_id=1, source_target_pairs={{0,1},{1,0},{2,3},{3,2},{4,5},{5,4},{6,7},{7,6},{8,9},{9,8},{10,11... | collective-permute-start | bytes 393224 | tf_op jit(solution)/shard_map/ppermute | solution.py:395
  11.5 1.9 %collective-permute-done.1.refs_2_ = bf16[2,272,128]{2,1,0:T(8,128)(2,1)S(1)} collective-permute-done((bf16[2,272,128]{2,1,0:T(8,128)(2,1)S(1)}, bf16[2,272,128]{2,1,0:T(8,128)(2,1)S(1)}, u32[]{:S(2)}, u32[]{:S(2)}) %collective-permute-start.1) | collective-permute-done | bytes 139296 | tf_op jit(solution)/shard_map/ppermute | solution.py:395
  13.4 0.0 copy-start.1
  13.4 0.1 collective-permute-start.3
  13.5 0.5 collective-permute-start.4
  14.0 1.6 %collective-permute-done.5.came_ref.refs_2_ = bf16[128,512]{1,0:T(8,128)(2,1)S(1)} collective-permute-done((bf16[128,512]{1,0:T(8,128)(2,1)}, bf16[128,512]{1,0:T(8,128)(2,1)S(1)}, u32[]{:S(2)}, u32[]{:S(2)}) %collective-permute-start.5) | collective-permute-done | bytes 131104 | tf_op jit(solution)/shard_map/ppermute | solution.py:395
  15.7 0.2 collective-permute-done.6.refs_0_.refs_1_
  15.9 0.0 copy-start
  15.9 0.0 copy-start.2
  15.9 0.0 copy-start.3
  15.9 1.5 %collective-permute-start.7 = (bf16[128,512]{1,0:T(8,128)(2,1)S(1)}, bf16[128,512]{1,0:T(8,128)(2,1)S(1)}, u32[]{:S(2)}, u32[]{:S(2)}) collective-permute-start(bf16[128,512]{1,0:T(8,128)(2,1)S(1)} %relay.1), channel_id=1, source_target_pairs={{0,1},{1,0},{2,3},{3,2},{4,5},{5,4},{6,7},{7,6},{8,9},{9,8},{10,11... | collective-permute-start | bytes 393224 | tf_op jit(solution)/shard_map/ppermute | solution.py:395
  17.4 2.8 %forward_mix.1 = (bf16[8,32,128]{2,1,0:T(8,128)(2,1)S(1)}, bf16[8,16,128]{2,1,0:T(8,128)(2,1)S(1)}) custom-call(bf16[10,2,2,128,128]{4,3,2,1,0:T(8,128)(2,1)S(1)} %copy-done.1, bf16[2,272,128]{2,1,0:T(8,128)(2,1)S(1)} %get-tuple-element.32.refs_0_, bf16[2,272,128]{2,1,0:T(8,128)(2,1)S(1)} %collective-permute-done.refs_1_, ...), custom_call_target="tpu_custom_call" | custom-call | tf_op jit(solution)/shard_map/forward_mix/pallas_call | solution.py:373
  20.3 0.3 early_cotangent.1.early_ref
  20.6 0.3 collective-permute-done.7.refs_3_
  20.9 0.4 cotangent.1
  21.3 0.1 collective-permute-start.21
  21.4 1.6 %collective-permute-start.8 = (bf16[2,64,128]{2,1,0:T(8,128)(2,1)S(1)}, bf16[2,64,128]{2,1,0:T(8,128)(2,1)S(1)}, u32[]{:S(2)}, u32[]{:S(2)}) collective-permute-start(bf16[2,64,128]{2,1,0:T(8,128)(2,1)S(1)} %get-tuple-element.41), channel_id=1, source_target_pairs={{0,8},{4,12},{8,0},{12,4},{16,24},{20,28},{24,16},{28,20},{1,9},{5... | collective-permute-start | bytes 98312 | tf_op jit(solution)/shard_map/ppermute | solution.py:395
  23.0 1.5 %collective-permute-start.9 = (bf16[2,64,128]{2,1,0:T(8,128)(2,1)S(1)}, bf16[2,64,128]{2,1,0:T(8,128)(2,1)S(1)}, u32[]{:S(2)}, u32[]{:S(2)}) collective-permute-start(bf16[2,64,128]{2,1,0:T(8,128)(2,1)S(1)} %get-tuple-element.42), channel_id=1, source_target_pairs={{0,16},{4,20},{8,24},{12,28},{16,0},{20,4},{24,8},{28,12},{1,17},{... | collective-permute-start | bytes 98312 | tf_op jit(solution)/shard_map/ppermute | solution.py:395
  24.6 0.4 collective-permute-start.10
  25.0 0.4 collective-permute-done.8.refs_1_.refs_5_
  25.4 0.1 collective-permute-start.12
  25.5 1.5 %collective-permute-done.9.refs_2_.refs_6_ = bf16[2,64,128]{2,1,0:T(8,128)(2,1)S(1)} collective-permute-done((bf16[2,64,128]{2,1,0:T(8,128)(2,1)S(1)}, bf16[2,64,128]{2,1,0:T(8,128)(2,1)S(1)}, u32[]{:S(2)}, u32[]{:S(2)}) %collective-permute-start.9) | collective-permute-done | bytes 32800 | tf_op jit(solution)/shard_map/ppermute | solution.py:395
  26.9 2.4 %collective-permute-done.10.refs_3_.refs_7_ = bf16[2,64,128]{2,1,0:T(8,128)(2,1)S(1)} collective-permute-done((bf16[2,64,128]{2,1,0:T(8,128)(2,1)S(1)}, bf16[2,64,128]{2,1,0:T(8,128)(2,1)S(1)}, u32[]{:S(2)}, u32[]{:S(2)}) %collective-permute-start.10) | collective-permute-done | bytes 32800 | tf_op jit(solution)/shard_map/ppermute | solution.py:395
  29.4 1.2 %collective-permute-done.14.refs_7_.refs_11_ = bf16[2,64,128]{2,1,0:T(8,128)(2,1)S(1)} collective-permute-done((bf16[2,64,128]{2,1,0:T(8,128)(2,1)S(1)}, bf16[2,64,128]{2,1,0:T(8,128)(2,1)S(1)}, u32[]{:S(2)}, u32[]{:S(2)}) %collective-permute-start.14) | collective-permute-done | bytes 32800 | tf_op jit(solution)/shard_map/ppermute | solution.py:395
  30.6 0.3 project.1
  30.9 1.5 %collective-permute-start.20 = (bf16[2,128,512]{2,1,0:T(8,128)(2,1)S(1)}, bf16[2,128,512]{2,1,0:T(8,128)(2,1)S(1)}, u32[]{:S(2)}, u32[]{:S(2)}) collective-permute-start(bf16[2,128,512]{2,1,0:T(8,128)(2,1)S(1)} %get-tuple-element.49), channel_id=1, source_target_pairs={{0,1},{1,0},{2,3},{3,2},{4,5},{5,4},{6,7},{7,6},{8,9},{9,8},{10,11... | collective-permute-start | bytes 786440 | tf_op jit(solution)/shard_map/ppermute | solution.py:395
  32.4 0.4 projector_gradient.1
  32.7 0.6 %collective-permute-start.23 = (bf16[2,256,256]{2,1,0:T(8,128)(2,1)S(1)}, bf16[2,256,256]{2,1,0:T(8,128)(2,1)S(1)}, u32[]{:S(2)}, u32[]{:S(2)}) collective-permute-start(bf16[2,256,256]{2,1,0:T(8,128)(2,1)S(1)} %get-tuple-element.55), channel_id=1, source_target_pairs={{0,8},{4,12},{8,0},{12,4},{16,24},{20,28},{24,16},{28,20},{1,9},{5... | collective-permute-start | bytes 786440 | tf_op jit(solution)/shard_map/ppermute | solution.py:395
  33.3 2.5 %backward_mix.1 = (bf16[16,32,128]{2,1,0:T(8,128)(2,1)S(1)}, bf16[16,32,128]{2,1,0:T(8,128)(2,1)S(1)}, bf16[16,32,128]{2,1,0:T(8,128)(2,1)S(1)}, bf16[16,32,128]{2,1,0:T(8,128)(2,1)S(1)}) custom-call(bf16[10,2,2,128,128]{4,3,2,1,0:T(8,128)(2,1)S(1)} %copy-done.1, bf16[8,16,128]{2,1,0:T(8,128)(2,1)S(1)} %get-tuple-element.36.map_ref, ...), custom_call_target="tpu_custom_call" | custom-call | tf_op jit(solution)/shard_map/backward_mix/pallas_call | solution.py:373
  35.8 1.6 %collective-permute-start.15 = (bf16[16,32,128]{2,1,0:T(8,128)(2,1)S(1)}, bf16[16,32,128]{2,1,0:T(8,128)(2,1)S(1)}, u32[]{:S(2)}, u32[]{:S(2)}) collective-permute-start(bf16[16,32,128]{2,1,0:T(8,128)(2,1)S(1)} %get-tuple-element.45), channel_id=1, source_target_pairs={{0,8},{4,12},{8,0},{12,4},{16,24},{20,28},{24,16},{28,20},{1,9},{5... | collective-permute-start | bytes 393224 | tf_op jit(solution)/shard_map/ppermute | solution.py:395
  37.4 0.5 %collective-permute-start.16 = (bf16[16,32,128]{2,1,0:T(8,128)(2,1)S(1)}, bf16[16,32,128]{2,1,0:T(8,128)(2,1)S(1)}, u32[]{:S(2)}, u32[]{:S(2)}) collective-permute-start(bf16[16,32,128]{2,1,0:T(8,128)(2,1)S(1)} %get-tuple-element.46), channel_id=1, source_target_pairs={{0,16},{4,20},{8,24},{12,28},{16,0},{20,4},{24,8},{28,12},{1,17},{... | collective-permute-start | bytes 393224 | tf_op jit(solution)/shard_map/ppermute | solution.py:395
  37.9 1.5 %collective-permute-start.17 = (bf16[16,32,128]{2,1,0:T(8,128)(2,1)S(1)}, bf16[16,32,128]{2,1,0:T(8,128)(2,1)S(1)}, u32[]{:S(2)}, u32[]{:S(2)}) collective-permute-start(bf16[16,32,128]{2,1,0:T(8,128)(2,1)S(1)} %get-tuple-element.47), channel_id=1, source_target_pairs={{0,24},{4,28},{8,16},{12,20},{16,8},{20,12},{24,0},{28,4},{1,25},{... | collective-permute-start | bytes 393224 | tf_op jit(solution)/shard_map/ppermute | solution.py:395
  39.4 0.0 collective-permute-done.20.got_ref
  39.4 2.4 %collective-permute-start.22 = (bf16[128,512]{1,0:T(8,128)(2,1)S(1)}, bf16[128,512]{1,0:T(8,128)(2,1)S(1)}, u32[]{:S(2)}, u32[]{:S(2)}) collective-permute-start(bf16[128,512]{1,0:T(8,128)(2,1)S(1)} %fold_shares.1), channel_id=1, source_target_pairs={{0,2},{1,3},{2,0},{3,1},{4,6},{5,7},{6,4},{7,5},{8,10},{9,11},{10,... | collective-permute-start | bytes 393224 | tf_op jit(solution)/shard_map/ppermute | solution.py:395
  41.8 0.2 collective-permute-done.23.came_ref.refs_8_
  42.0 0.6 %collective-permute-start.24 = (bf16[256,256]{1,0:T(8,128)(2,1)S(1)}, bf16[256,256]{1,0:T(8,128)(2,1)S(1)}, u32[]{:S(2)}, u32[]{:S(2)}) collective-permute-start(bf16[256,256]{1,0:T(8,128)(2,1)S(1)} %fold_parts.1), channel_id=1, source_target_pairs={{0,16},{4,20},{8,24},{12,28},{16,0},{20,4},{24,8},{28,12},{1,17},{... | collective-permute-start | bytes 393224 | tf_op jit(solution)/shard_map/ppermute | solution.py:395
  42.6 2.2 %collective-permute-done.15.refs_1_ = bf16[16,32,128]{2,1,0:T(8,128)(2,1)S(1)} collective-permute-done((bf16[16,32,128]{2,1,0:T(8,128)(2,1)S(1)}, bf16[16,32,128]{2,1,0:T(8,128)(2,1)S(1)}, u32[]{:S(2)}, u32[]{:S(2)}) %collective-permute-start.15) | collective-permute-done | bytes 131104 | tf_op jit(solution)/shard_map/ppermute | solution.py:395
  44.8 0.1 collective-permute-start.18
  44.9 1.6 %collective-permute-done.17.refs_3_ = bf16[16,32,128]{2,1,0:T(8,128)(2,1)S(1)} collective-permute-done((bf16[16,32,128]{2,1,0:T(8,128)(2,1)S(1)}, bf16[16,32,128]{2,1,0:T(8,128)(2,1)S(1)}, u32[]{:S(2)}, u32[]{:S(2)}) %collective-permute-start.17) | collective-permute-done | bytes 131104 | tf_op jit(solution)/shard_map/ppermute | solution.py:395
  46.6 1.4 %collective-permute-done.22.share_ref = bf16[128,512]{1,0:T(8,128)(2,1)S(1)} collective-permute-done((bf16[128,512]{1,0:T(8,128)(2,1)S(1)}, bf16[128,512]{1,0:T(8,128)(2,1)S(1)}, u32[]{:S(2)}, u32[]{:S(2)}) %collective-permute-start.22) | collective-permute-done | bytes 131104 | tf_op jit(solution)/shard_map/ppermute | solution.py:395
  47.9 0.6 %collective-permute-done.24.part_ref = bf16[256,256]{1,0:T(8,128)(2,1)S(1)} collective-permute-done((bf16[256,256]{1,0:T(8,128)(2,1)S(1)}, bf16[256,256]{1,0:T(8,128)(2,1)S(1)}, u32[]{:S(2)}, u32[]{:S(2)}) %collective-permute-start.24) | collective-permute-done | bytes 131104 | tf_op jit(solution)/shard_map/ppermute | solution.py:395
  48.5 0.1 arrive.1
  48.6 1.1 %finish.1 = (bf16[8,128,256]{2,1,0:T(8,128)(2,1)}, bf16[128,512]{1,0:T(8,128)(2,1)}, f32[256,256]{1,0:T(8,128)}) custom-call(bf16[16,32,128]{2,1,0:T(8,128)(2,1)S(1)} %get-tuple-element.44.refs_0_, bf16[16,32,128]{2,1,0:T(8,128)(2,1)S(1)} %collective-permute-done.15.refs_1_, bf16[16,32,128]{2,1,0:T(8,128)(2,1)S(1)} %collective-permute-done.16.refs_2_, ...), custom_call_target="tpu_custom_call" | custom-call | tf_op jit(solution)/shard_map/finish/pallas_call | solution.py:373
  (24 shorter events, 0.2 us)
Async XLA Ops:
  2.3 9.2 %collective-permute-start = (bf16[2,272,128]{2,1,0:T(8,128)(2,1)S(1)}, bf16[2,272,128]{2,1,0:T(8,128)(2,1)S(1)}, u32[]{:S(2)}, u32[]{:S(2)}) collective-permute-start(bf16[2,272,128]{2,1,0:T(8,128)(2,1)S(1)} %get-tuple-element.33), channel_id=1, source_target_pairs={{0,8},{4,12},{8,0},{12,4},{16,24},{20,28},{24,16},{28,20},{1,9},{5... | collective-permute-start | bytes 417800 | tf_op jit(solution)/shard_map/ppermute | solution.py:395
  5.3 8.1 %collective-permute-start.1 = (bf16[2,272,128]{2,1,0:T(8,128)(2,1)S(1)}, bf16[2,272,128]{2,1,0:T(8,128)(2,1)S(1)}, u32[]{:S(2)}, u32[]{:S(2)}) collective-permute-start(bf16[2,272,128]{2,1,0:T(8,128)(2,1)S(1)} %get-tuple-element.34), channel_id=1, source_target_pairs={{0,16},{4,20},{8,24},{12,28},{16,0},{20,4},{24,8},{28,12},{1,17},{... | collective-permute-start | bytes 417800 | tf_op jit(solution)/shard_map/ppermute | solution.py:395
  6.8 6.7 %collective-permute-start.2 = (bf16[2,272,128]{2,1,0:T(8,128)(2,1)S(1)}, bf16[2,272,128]{2,1,0:T(8,128)(2,1)S(1)}, u32[]{:S(2)}, u32[]{:S(2)}) collective-permute-start(bf16[2,272,128]{2,1,0:T(8,128)(2,1)S(1)} %get-tuple-element.35), channel_id=1, source_target_pairs={{0,24},{4,28},{8,16},{12,20},{16,8},{20,12},{24,0},{28,4},{1,25},{... | collective-permute-start | bytes 417800 | tf_op jit(solution)/shard_map/ppermute | solution.py:395
  6.8 8.8 %collective-permute-start.5 = (bf16[128,512]{1,0:T(8,128)(2,1)}, bf16[128,512]{1,0:T(8,128)(2,1)S(1)}, u32[]{:S(2)}, u32[]{:S(2)}) collective-permute-start(bf16[128,512]{1,0:T(8,128)(2,1)} %refs_0_.3), channel_id=1, source_target_pairs={{0,2},{1,3},{2,0},{3,1},{4,6},{5,7},{6,4},{7,5},{8,10},{9,11},{10,... | collective-permute-start | bytes 393224 | tf_op jit(solution)/shard_map/ppermute | solution.py:395
  9.9 6.0 %collective-permute-start.6 = (bf16[128,512]{1,0:T(8,128)(2,1)}, bf16[128,512]{1,0:T(8,128)(2,1)S(1)}, u32[]{:S(2)}, u32[]{:S(2)}) collective-permute-start(bf16[128,512]{1,0:T(8,128)(2,1)} %refs_0_.3), channel_id=1, source_target_pairs={{0,1},{1,0},{2,3},{3,2},{4,5},{5,4},{6,7},{7,6},{8,9},{9,8},{10,11... | collective-permute-start | bytes 393224 | tf_op jit(solution)/shard_map/ppermute | solution.py:395
  13.4 4.0 %copy-start.1 = (bf16[10,2,2,128,128]{4,3,2,1,0:T(8,128)(2,1)S(1)}, bf16[10,2,2,128,128]{4,3,2,1,0:T(8,128)(2,1)}, u32[]{:S(2)}) copy-start(bf16[10,2,2,128,128]{4,3,2,1,0:T(8,128)(2,1)} %mix_ref.3) | copy-start | bytes 3932164
  13.4 4.0 %collective-permute-start.3 = (bf16[3,1,272,128]{3,2,1,0:T(8,128)(2,1)S(1)}, bf16[3,1,272,128]{3,2,1,0:T(8,128)(2,1)S(1)}, u32[]{:S(2)}, u32[]{:S(2)}) collective-permute-start(bf16[3,1,272,128]{3,2,1,0:T(8,128)(2,1)S(1)} %gather.2), channel_id=1, source_target_pairs={{0,4},{4,0},{8,12},{12,8},{16,20},{20,16},{24,28},{28,24},{1,5},{5... | collective-permute-start | bytes 626696 | tf_op jit(solution)/shard_map/ppermute | solution.py:395
  13.5 3.9 %collective-permute-start.4 = (bf16[2,272,128]{2,1,0:T(8,128)(2,1)S(1)}, bf16[2,272,128]{2,1,0:T(8,128)(2,1)S(1)}, u32[]{:S(2)}, u32[]{:S(2)}) collective-permute-start(bf16[2,272,128]{2,1,0:T(8,128)(2,1)S(1)} %collective-permute-done.2.refs_3_), channel_id=1, source_target_pairs={{0,4},{4,0},{8,12},{12,8},{16,20},{20,16},{24,28},{28,24},{1,5},{5... | collective-permute-start | bytes 417800 | tf_op jit(solution)/shard_map/ppermute | solution.py:395
  15.9 4.4 %copy-start = (bf16[256,2048]{1,0:T(8,128)(2,1)S(1)}, bf16[256,2048]{1,0:T(8,128)(2,1)}, u32[]{:S(2)}) copy-start(bf16[256,2048]{1,0:T(8,128)(2,1)} %w_ref.5) | copy-start | bytes 3145732
  15.9 4.4 %copy-start.2 = (bf16[128,512]{1,0:T(8,128)(2,1)S(1)}, bf16[128,512]{1,0:T(8,128)(2,1)}, u32[]{:S(2)}) copy-start(bf16[128,512]{1,0:T(8,128)(2,1)} %refs_0_.3) | copy-start | bytes 393220
  15.9 5.0 %copy-start.3 = (s32[1024]{0:T(1024)S(1)}, s32[1024]{0:T(1024)}, u32[]{:S(2)}) copy-start(s32[1024]{0:T(1024)} %param.8) | copy-start | bytes 12292
  15.9 5.0 %collective-permute-start.7 = (bf16[128,512]{1,0:T(8,128)(2,1)S(1)}, bf16[128,512]{1,0:T(8,128)(2,1)S(1)}, u32[]{:S(2)}, u32[]{:S(2)}) collective-permute-start(bf16[128,512]{1,0:T(8,128)(2,1)S(1)} %relay.1), channel_id=1, source_target_pairs={{0,1},{1,0},{2,3},{3,2},{4,5},{5,4},{6,7},{7,6},{8,9},{9,8},{10,11... | collective-permute-start | bytes 393224 | tf_op jit(solution)/shard_map/ppermute | solution.py:395
  21.3 11.0 %collective-permute-start.21 = (bf16[128,1024]{1,0:T(8,128)(2,1)S(1)}, bf16[128,1024]{1,0:T(8,128)(2,1)S(1)}, u32[]{:S(2)}, u32[]{:S(2)}) collective-permute-start(bf16[128,1024]{1,0:T(8,128)(2,1)S(1)} %get-tuple-element.50), channel_id=1, source_target_pairs={{0,4},{4,0},{8,12},{12,8},{16,20},{20,16},{24,28},{28,24},{1,5},{5... | collective-permute-start | bytes 786440 | tf_op jit(solution)/shard_map/ppermute | solution.py:395
  21.4 4.0 %collective-permute-start.8 = (bf16[2,64,128]{2,1,0:T(8,128)(2,1)S(1)}, bf16[2,64,128]{2,1,0:T(8,128)(2,1)S(1)}, u32[]{:S(2)}, u32[]{:S(2)}) collective-permute-start(bf16[2,64,128]{2,1,0:T(8,128)(2,1)S(1)} %get-tuple-element.41), channel_id=1, source_target_pairs={{0,8},{4,12},{8,0},{12,4},{16,24},{20,28},{24,16},{28,20},{1,9},{5... | collective-permute-start | bytes 98312 | tf_op jit(solution)/shard_map/ppermute | solution.py:395
  23.0 3.9 %collective-permute-start.9 = (bf16[2,64,128]{2,1,0:T(8,128)(2,1)S(1)}, bf16[2,64,128]{2,1,0:T(8,128)(2,1)S(1)}, u32[]{:S(2)}, u32[]{:S(2)}) collective-permute-start(bf16[2,64,128]{2,1,0:T(8,128)(2,1)S(1)} %get-tuple-element.42), channel_id=1, source_target_pairs={{0,16},{4,20},{8,24},{12,28},{16,0},{20,4},{24,8},{28,12},{1,17},{... | collective-permute-start | bytes 98312 | tf_op jit(solution)/shard_map/ppermute | solution.py:395
  24.6 4.8 %collective-permute-start.10 = (bf16[2,64,128]{2,1,0:T(8,128)(2,1)S(1)}, bf16[2,64,128]{2,1,0:T(8,128)(2,1)S(1)}, u32[]{:S(2)}, u32[]{:S(2)}) collective-permute-start(bf16[2,64,128]{2,1,0:T(8,128)(2,1)S(1)} %get-tuple-element.43), channel_id=1, source_target_pairs={{0,24},{4,28},{8,16},{12,20},{16,8},{20,12},{24,0},{28,4},{1,25},{... | collective-permute-start | bytes 98312 | tf_op jit(solution)/shard_map/ppermute | solution.py:395
  25.0 4.4 %collective-permute-start.11 = (bf16[2,64,128]{2,1,0:T(8,128)(2,1)S(1)}, bf16[2,64,128]{2,1,0:T(8,128)(2,1)S(1)}, u32[]{:S(2)}, u32[]{:S(2)}) collective-permute-start(bf16[2,64,128]{2,1,0:T(8,128)(2,1)S(1)} %get-tuple-element.40.refs_0_.refs_4_), channel_id=1, source_target_pairs={{0,4},{4,0},{8,12},{12,8},{16,20},{20,16},{24,28},{28,24},{1,5},{5... | collective-permute-start | bytes 98312 | tf_op jit(solution)/shard_map/ppermute | solution.py:395
  25.4 4.0 %collective-permute-start.12 = (bf16[2,64,128]{2,1,0:T(8,128)(2,1)S(1)}, bf16[2,64,128]{2,1,0:T(8,128)(2,1)S(1)}, u32[]{:S(2)}, u32[]{:S(2)}) collective-permute-start(bf16[2,64,128]{2,1,0:T(8,128)(2,1)S(1)} %collective-permute-done.8.refs_1_.refs_5_), channel_id=1, source_target_pairs={{0,4},{4,0},{8,12},{12,8},{16,20},{20,16},{24,28},{28,24},{1,5},{5... | collective-permute-start | bytes 98312 | tf_op jit(solution)/shard_map/ppermute | solution.py:395
  26.9 2.4 %collective-permute-start.13 = (bf16[2,64,128]{2,1,0:T(8,128)(2,1)S(1)}, bf16[2,64,128]{2,1,0:T(8,128)(2,1)S(1)}, u32[]{:S(2)}, u32[]{:S(2)}) collective-permute-start(bf16[2,64,128]{2,1,0:T(8,128)(2,1)S(1)} %collective-permute-done.9.refs_2_.refs_6_), channel_id=1, source_target_pairs={{0,4},{4,0},{8,12},{12,8},{16,20},{20,16},{24,28},{28,24},{1,5},{5... | collective-permute-start | bytes 98312 | tf_op jit(solution)/shard_map/ppermute | solution.py:395
  29.4 1.2 %collective-permute-start.14 = (bf16[2,64,128]{2,1,0:T(8,128)(2,1)S(1)}, bf16[2,64,128]{2,1,0:T(8,128)(2,1)S(1)}, u32[]{:S(2)}, u32[]{:S(2)}) collective-permute-start(bf16[2,64,128]{2,1,0:T(8,128)(2,1)S(1)} %collective-permute-done.10.refs_3_.refs_7_), channel_id=1, source_target_pairs={{0,4},{4,0},{8,12},{12,8},{16,20},{20,16},{24,28},{28,24},{1,5},{5... | collective-permute-start | bytes 98312 | tf_op jit(solution)/shard_map/ppermute | solution.py:395
  30.9 8.4 %collective-permute-start.20 = (bf16[2,128,512]{2,1,0:T(8,128)(2,1)S(1)}, bf16[2,128,512]{2,1,0:T(8,128)(2,1)S(1)}, u32[]{:S(2)}, u32[]{:S(2)}) collective-permute-start(bf16[2,128,512]{2,1,0:T(8,128)(2,1)S(1)} %get-tuple-element.49), channel_id=1, source_target_pairs={{0,1},{1,0},{2,3},{3,2},{4,5},{5,4},{6,7},{7,6},{8,9},{9,8},{10,11... | collective-permute-start | bytes 786440 | tf_op jit(solution)/shard_map/ppermute | solution.py:395
  32.7 9.3 %collective-permute-start.23 = (bf16[2,256,256]{2,1,0:T(8,128)(2,1)S(1)}, bf16[2,256,256]{2,1,0:T(8,128)(2,1)S(1)}, u32[]{:S(2)}, u32[]{:S(2)}) collective-permute-start(bf16[2,256,256]{2,1,0:T(8,128)(2,1)S(1)} %get-tuple-element.55), channel_id=1, source_target_pairs={{0,8},{4,12},{8,0},{12,4},{16,24},{20,28},{24,16},{28,20},{1,9},{5... | collective-permute-start | bytes 786440 | tf_op jit(solution)/shard_map/ppermute | solution.py:395
  35.8 9.0 %collective-permute-start.15 = (bf16[16,32,128]{2,1,0:T(8,128)(2,1)S(1)}, bf16[16,32,128]{2,1,0:T(8,128)(2,1)S(1)}, u32[]{:S(2)}, u32[]{:S(2)}) collective-permute-start(bf16[16,32,128]{2,1,0:T(8,128)(2,1)S(1)} %get-tuple-element.45), channel_id=1, source_target_pairs={{0,8},{4,12},{8,0},{12,4},{16,24},{20,28},{24,16},{28,20},{1,9},{5... | collective-permute-start | bytes 393224 | tf_op jit(solution)/shard_map/ppermute | solution.py:395
  37.4 7.4 %collective-permute-start.16 = (bf16[16,32,128]{2,1,0:T(8,128)(2,1)S(1)}, bf16[16,32,128]{2,1,0:T(8,128)(2,1)S(1)}, u32[]{:S(2)}, u32[]{:S(2)}) collective-permute-start(bf16[16,32,128]{2,1,0:T(8,128)(2,1)S(1)} %get-tuple-element.46), channel_id=1, source_target_pairs={{0,16},{4,20},{8,24},{12,28},{16,0},{20,4},{24,8},{28,12},{1,17},{... | collective-permute-start | bytes 393224 | tf_op jit(solution)/shard_map/ppermute | solution.py:395
  37.9 8.7 %collective-permute-start.17 = (bf16[16,32,128]{2,1,0:T(8,128)(2,1)S(1)}, bf16[16,32,128]{2,1,0:T(8,128)(2,1)S(1)}, u32[]{:S(2)}, u32[]{:S(2)}) collective-permute-start(bf16[16,32,128]{2,1,0:T(8,128)(2,1)S(1)} %get-tuple-element.47), channel_id=1, source_target_pairs={{0,24},{4,28},{8,16},{12,20},{16,8},{20,12},{24,0},{28,4},{1,25},{... | collective-permute-start | bytes 393224 | tf_op jit(solution)/shard_map/ppermute | solution.py:395
  39.4 8.5 %collective-permute-start.22 = (bf16[128,512]{1,0:T(8,128)(2,1)S(1)}, bf16[128,512]{1,0:T(8,128)(2,1)S(1)}, u32[]{:S(2)}, u32[]{:S(2)}) collective-permute-start(bf16[128,512]{1,0:T(8,128)(2,1)S(1)} %fold_shares.1), channel_id=1, source_target_pairs={{0,2},{1,3},{2,0},{3,1},{4,6},{5,7},{6,4},{7,5},{8,10},{9,11},{10,... | collective-permute-start | bytes 393224 | tf_op jit(solution)/shard_map/ppermute | solution.py:395
  42.0 6.5 %collective-permute-start.24 = (bf16[256,256]{1,0:T(8,128)(2,1)S(1)}, bf16[256,256]{1,0:T(8,128)(2,1)S(1)}, u32[]{:S(2)}, u32[]{:S(2)}) collective-permute-start(bf16[256,256]{1,0:T(8,128)(2,1)S(1)} %fold_parts.1), channel_id=1, source_target_pairs={{0,16},{4,20},{8,24},{12,28},{16,0},{20,4},{24,8},{28,12},{1,17},{... | collective-permute-start | bytes 393224 | tf_op jit(solution)/shard_map/ppermute | solution.py:395
  44.8 3.8 %collective-permute-start.18 = (bf16[3,8,32,128]{3,2,1,0:T(8,128)(2,1)S(1)}, bf16[3,8,32,128]{3,2,1,0:T(8,128)(2,1)S(1)}, u32[]{:S(2)}, u32[]{:S(2)}) collective-permute-start(bf16[3,8,32,128]{3,2,1,0:T(8,128)(2,1)S(1)} %gather.3), channel_id=1, source_target_pairs={{0,4},{4,0},{8,12},{12,8},{16,20},{20,16},{24,28},{28,24},{1,5},{5... | collective-permute-start | bytes 589832 | tf_op jit(solution)/shard_map/ppermute | solution.py:395
  46.5 2.0 %collective-permute-start.19 = (bf16[16,32,128]{2,1,0:T(8,128)(2,1)S(1)}, bf16[16,32,128]{2,1,0:T(8,128)(2,1)S(1)}, u32[]{:S(2)}, u32[]{:S(2)}) collective-permute-start(bf16[16,32,128]{2,1,0:T(8,128)(2,1)S(1)} %collective-permute-done.17.refs_3_), channel_id=1, source_target_pairs={{0,4},{4,0},{8,12},{12,8},{16,20},{20,16},{24,28},{28,24},{1,5},{5... | collective-permute-start | bytes 393224 | tf_op jit(solution)/shard_map/ppermute | solution.py:395
